TPU v7x, 32 devices: a whole 2x2x4 slice. The times are simulated.
32 devices in a mesh: dp: 8 (over y, x, core), ctx: 4 (over z).
Axes of the slice: x: 2, y: 2, z: 4, core: 2. Of those that a mesh axis runs over, the one named last changes fastest.
Arguments:
- q_src: bfloat16 [4096, 4096], P(('dp', 'ctx')), may hold values from -40 to 40
- kv_src: bfloat16 [4096, 1024], P(('dp', 'ctx')), may hold values from -40 to 40
- route: int32 [4096, 1], replicated, may hold values from 0 to 7; in each aligned block of 512 rows (0 to 511, 512 to 1023, ...) at most 96 rows name the same one
- doc_ids: int32 [8, 768], P('dp'), may hold values from 0 to 5, never falling along the last dimension, each value on 1 to 256 neighbouring positions
Outputs:
- attended: bfloat16 [6144, 4096], P(('dp', 'ctx'))
Inputs may be any that keep to these rules, and one draw needn't show every extreme that they name: `route`: within each source group's 512 rows (aligned blocks of 512 rows), no sequence is named by more than 96 rows, a bound that some block reaches. `doc_ids`: never falling along a sequence; every document has 1 to 256 slots and one has exactly 256.
All inputs are finite; a program needn't handle non-finite values.
Results may differ from a plain program's by a relative error of at most 0.011.
Values may be sent and summed in bfloat16 or wider, within the bound.
No kernel may reach another device: no remote copies, remote signals or barrier semaphores. Data moves between devices by JAX's collectives and lax.ppermute only.
A program may use at most 64 MiB of HBM per device.

v0:
```python
import math

import jax
import jax.numpy as jnp
from jax import lax
from jax.sharding import PartitionSpec as P

Q_HEADS = 32
KV_HEADS = 4
HEAD_DIM = 128


def attend(queries, kv_pairs, doc_rows, live_rows, kv_local):
    pack_len = queries.shape[0]
    head_count = queries.shape[1] // HEAD_DIM
    group_size = head_count // kv_local
    block_len = math.gcd(pack_len, 512)
    doc_most = pack_len // 3
    window = min(pack_len, doc_most + block_len)
    score_scale = HEAD_DIM ** (-0.5)
    grouped = queries.reshape(pack_len, kv_local, group_size, HEAD_DIM)
    split_pairs = kv_pairs.reshape(pack_len, 2, kv_local, HEAD_DIM)

    def one_block(block_index):
        row_start = block_index * block_len
        key_start = jnp.maximum(row_start + block_len - window, 0)
        query_block = lax.dynamic_slice_in_dim(grouped, row_start, block_len, 0)
        key_block = lax.dynamic_slice_in_dim(split_pairs, key_start, window, 0)
        query_docs = lax.dynamic_slice_in_dim(doc_rows, row_start, block_len, 0)
        key_docs = lax.dynamic_slice_in_dim(doc_rows, key_start, window, 0)
        query_pos = row_start + jnp.arange(block_len, dtype=jnp.int32)
        key_pos = key_start + jnp.arange(window, dtype=jnp.int32)
        allowed = (query_docs[:, None] == key_docs[None, :]) & (
            key_pos[None, :] <= query_pos[:, None]
        )
        scores = (
            jnp.einsum(
                "qkgd,skd->kgqs", query_block, key_block[:, 0], preferred_element_type=jnp.float32
            )
            * score_scale
        )
        masked = jnp.where(allowed, scores, -1e30)
        row_max = jnp.max(masked, axis=-1, keepdims=True)
        exponent = jnp.where(allowed, jnp.exp(masked - row_max), 0.0)
        probs = exponent / jnp.sum(exponent, axis=-1, keepdims=True)
        weights = probs.astype(jnp.bfloat16)
        mixed = jnp.einsum(
            "kgqs,skd->qkgd", weights, key_block[:, 1], preferred_element_type=jnp.float32
        )
        mixed = jnp.where((query_pos < live_rows)[:, None, None, None], mixed, 0.0)
        return mixed.astype(jnp.bfloat16).reshape(block_len, head_count * HEAD_DIM)

    blocks = lax.map(one_block, jnp.arange(pack_len // block_len, dtype=jnp.int32))
    return blocks.reshape(pack_len, head_count * HEAD_DIM)


def on_device(q_src, kv_src, route, doc_ids):
    ctx_size = lax.axis_size("ctx")
    dp_size = lax.axis_size("dp")
    rows_dev = q_src.shape[0]
    heads_dev = Q_HEADS // ctx_size
    kv_rows = kv_src.reshape(rows_dev, 2, KV_HEADS, HEAD_DIM)
    wide_pairs = jnp.repeat(kv_rows, Q_HEADS // KV_HEADS, axis=2)
    wide_pairs = wide_pairs.reshape(rows_dev, 2, ctx_size, heads_dev * HEAD_DIM)
    wide_pairs = wide_pairs.transpose(0, 2, 1, 3).reshape(
        rows_dev, ctx_size * 2 * heads_dev * HEAD_DIM
    )
    queries, kv_pairs = (
        lax.all_to_all(q_src, "ctx", split_axis=1, concat_axis=0, tiled=True),
        lax.all_to_all(wide_pairs, "ctx", split_axis=1, concat_axis=0, tiled=True),
    )
    length = rows_dev * ctx_size
    capacity = 3 * length // (2 * dp_size)
    pack_len = dp_size * capacity
    pack_plan = route.reshape(dp_size, length)
    seq_ids = jnp.arange(dp_size, dtype=jnp.int32)
    counts = jnp.sum((pack_plan[:, :, None] == seq_ids[None, None, :]).astype(jnp.int32), axis=1)
    own_index = lax.axis_index("dp")
    own_plan = lax.dynamic_slice_in_dim(pack_plan, own_index, 1, 0)[0]
    onehot = (own_plan[:, None] == seq_ids[None, :]).astype(jnp.int32)
    slot_rank = jnp.sum((jnp.cumsum(onehot, axis=0) - onehot) * onehot, axis=1)
    target = own_plan * capacity + slot_rank
    send_q = jnp.zeros((pack_len, queries.shape[1]), jnp.bfloat16).at[target].set(queries)
    send_kv = jnp.zeros((pack_len, kv_pairs.shape[1]), jnp.bfloat16).at[target].set(kv_pairs)
    recv_q, recv_kv = (
        lax.all_to_all(
            send_q.reshape(dp_size, capacity, -1), "dp", split_axis=0, concat_axis=0, tiled=True
        ),
        lax.all_to_all(
            send_kv.reshape(dp_size, capacity, -1), "dp", split_axis=0, concat_axis=0, tiled=True
        ),
    )
    incoming = lax.dynamic_slice_in_dim(counts, own_index, 1, 1)[:, 0]
    starts = jnp.cumsum(incoming) - incoming
    live_rows = jnp.sum(incoming)
    packed_pos = jnp.arange(pack_len, dtype=jnp.int32)
    source_idx = jnp.sum((starts[None, :] <= packed_pos[:, None]).astype(jnp.int32), axis=1) - 1
    offset = jnp.minimum(packed_pos - jnp.take(starts, source_idx), capacity - 1)
    gather_idx = source_idx * capacity + offset
    packed_q = jnp.take(recv_q.reshape(pack_len, -1), gather_idx, axis=0)
    packed_kv = jnp.take(recv_kv.reshape(pack_len, -1), gather_idx, axis=0)
    attended = attend(packed_q, packed_kv, doc_ids[0], live_rows, heads_dev)
    return lax.all_to_all(attended, "ctx", split_axis=0, concat_axis=1, tiled=True)


def solution(mesh):
    in_specs = (P(("dp", "ctx"), None), P(("dp", "ctx"), None), P(), P("dp", None))
    out_specs = P(("dp", "ctx"), None)
    return jax.shard_map(
        on_device, mesh=mesh, in_specs=in_specs, out_specs=out_specs, check_vma=False
    )
```

profile of v0, /device:TPU:18, one launch (start us, length us, event | category | flops | bytes accessed | tf_op | source)
XLA Modules:
  0.0 236.6 jit_solution(18314709253404496055)
XLA Ops:
  0.0 2.3 copy.38
  2.3 5.2 %all-to-all-start.2 = ((bf16[128,4,1024]{0,2,1:T(8,128)(2,1)}), bf16[128,4,1024]{0,2,1:T(8,128)(2,1)S(1)}, u32[]{:S(2)}, u32[]{:S(2)}) async-start(bf16[128,4,1024]{0,2,1:T(8,128)(2,1)} %bitcast.30), calls=%async_computation.2 | async-start | bytes 2097152 | tf_op jit(solution)/shard_map/all_to_all | solution.py:69
  8.3 2.1 reshape_reshape.3
  10.3 4.5 %all_to_all.48 = bf16[128,4,2048]{2,0,1:T(8,128)(2,1)} reshape(bf16[128,4,2,1024]{3,2,0,1:T(2,128)(2,1)} %bitcast.132) | data formatting | bytes 4194304 | tf_op jit(solution)/shard_map/all_to_all | solution.py:70
  14.8 15.1 %all-to-all-done.2 = bf16[128,4,1024]{0,2,1:T(8,128)(2,1)S(1)} async-done(((bf16[128,4,1024]{0,2,1:T(8,128)(2,1)}), bf16[128,4,1024]{0,2,1:T(8,128)(2,1)S(1)}, u32[]{:S(2)}, u32[]{:S(2)}) %all-to-all-start.2) | async-done | bytes 1048608 | tf_op jit(solution)/shard_map/all_to_all | solution.py:69
  30.0 6.9 %all-to-all-start = ((bf16[128,4,2048]{2,0,1:T(8,128)(2,1)}), bf16[128,4,2048]{2,0,1:T(8,128)(2,1)S(1)}, u32[]{:S(2)}, u32[]{:S(2)}) async-start(bf16[128,4,2048]{2,0,1:T(8,128)(2,1)} %all_to_all.48), calls=%async_computation | async-start | bytes 4194304 | tf_op jit(solution)/shard_map/all_to_all | solution.py:70
  40.9 4.5 %scatter_custom_fusion.1 = bf16[768,1024]{1,0:T(8,128)(2,1)} fusion(s32[512]{0:T(512)S(1)} %bitcast.143, bf16[512,1024]{1,0:T(8,128)(2,1)} %bitcast.139, bf16[]{:T(256)} %constant.145.clone.1), kind=kCustom, calls=%fused_computation.34 | custom fusion | bytes 1573376 | tf_op jit(solution)/shard_map/scatter | solution.py:83
  45.4 35.8 %all-to-all-done = bf16[128,4,2048]{2,0,1:T(8,128)(2,1)S(1)} async-done(((bf16[128,4,2048]{2,0,1:T(8,128)(2,1)}), bf16[128,4,2048]{2,0,1:T(8,128)(2,1)S(1)}, u32[]{:S(2)}, u32[]{:S(2)}) %all-to-all-start) | async-done | bytes 2097184 | tf_op jit(solution)/shard_map/all_to_all | solution.py:70
  81.2 1.4 copy-done.2
  82.6 4.3 %all-to-all-start.3 = ((bf16[8,96,1024]{2,1,0:T(8,128)(2,1)}), bf16[8,96,1024]{2,1,0:T(8,128)(2,1)S(1)}, u32[]{:S(2)}, u32[]{:S(2)}) async-start(bf16[8,96,1024]{2,1,0:T(8,128)(2,1)} %bitcast.33), calls=%async_computation.3 | async-start | bytes 3145728 | tf_op jit(solution)/shard_map/all_to_all | solution.py:86
  86.9 6.7 %scatter_custom_fusion = bf16[768,2048]{1,0:T(8,128)(2,1)} fusion(s32[512]{0:T(512)S(1)} %bitcast.144, bf16[512,2048]{1,0:T(8,128)(2,1)} %bitcast.137, bf16[]{:T(256)} %constant.145.clone.1), kind=kCustom, calls=%fused_computation.32 | custom fusion | bytes 3146240 | tf_op jit(solution)/shard_map/scatter | solution.py:84
  93.6 12.8 %all-to-all-done.3 = bf16[8,96,1024]{2,1,0:T(8,128)(2,1)S(1)} async-done(((bf16[8,96,1024]{2,1,0:T(8,128)(2,1)}), bf16[8,96,1024]{2,1,0:T(8,128)(2,1)S(1)}, u32[]{:S(2)}, u32[]{:S(2)}) %all-to-all-start.3) | async-done | bytes 1572896 | tf_op jit(solution)/shard_map/all_to_all | solution.py:86
  107.5 5.1 %all-to-all-start.1 = ((bf16[8,96,2048]{2,1,0:T(8,128)(2,1)}), bf16[8,96,2048]{2,1,0:T(8,128)(2,1)S(1)}, u32[]{:S(2)}, u32[]{:S(2)}) async-start(bf16[8,96,2048]{2,1,0:T(8,128)(2,1)} %bitcast.129), calls=%async_computation.1 | async-start | bytes 6291456 | tf_op jit(solution)/shard_map/all_to_all | solution.py:89
  114.4 4.4 %fusion.29 = (s32[768]{0:T(1024)S(1)}, s32[768,1]{0,1:T(1,128)S(1)}) fusion(s32[]{:T(128)} %bitcast.11, s32[]{:T(128)} %bitcast.12, s32[]{:T(128)} %bitcast.13, s32[]{:T(128)} %bitcast.14, s32[]{:T(128)} %bitcast.15, s32[]{:T(128)} %bitcast.17, s32[]{:T(128)} %bitcast.16, s32[768]{0:T(1024)S(1)} %get-tuple-element.180, s32[768]{0:T(1024)S(1)} %get-tuple-element.179), kind=kLoop, calls=%fused_computation.62 | loop fusion | flops 10752 | bytes 12316 | tf_op jit(solution)/shard_map/jit(_take)/gather | solution.py:98
  119.5 6.2 %gather_fusion.1 = bf16[768,1024]{1,0:T(8,128)(2,1)} fusion(bf16[768,1024]{1,0:T(8,128)(2,1)} %bitcast.127, s32[1024]{0:T(1024)S(1)} %pad_clamp_fusion), kind=kCustom, calls=%fused_computation.1 | custom fusion | bytes 3148800 | tf_op jit(solution)/shard_map/jit(_take)/gather | solution.py:100
  125.6 1.8 copy.49
  127.5 1.5 copy_select_fusion.1
  129.0 20.0 %all-to-all-done.1 = bf16[8,96,2048]{2,1,0:T(8,128)(2,1)S(1)} async-done(((bf16[8,96,2048]{2,1,0:T(8,128)(2,1)}), bf16[8,96,2048]{2,1,0:T(8,128)(2,1)S(1)}, u32[]{:S(2)}, u32[]{:S(2)}) %all-to-all-start.1) | async-done | bytes 3145760 | tf_op jit(solution)/shard_map/all_to_all | solution.py:89
  149.0 4.3 %gather_fusion = bf16[768,2048]{1,0:T(8,128)(2,1)} fusion(bf16[768,2048]{1,0:T(8,128)(2,1)S(1)} %bitcast.126, s32[1024]{0:T(1024)S(1)} %pad_clamp_fusion), kind=kCustom, calls=%fused_computation | custom fusion | bytes 6294528 | tf_op jit(solution)/shard_map/jit(_take)/gather | solution.py:101
  153.2 2.9 %copy.48 = bf16[96,8,16,128]{3,2,1,0:T(8,128)(2,1)S(1)} copy(bf16[96,8,16,128]{3,1,2,0:T(8,128)(2,1)} %bitcast.131) | data formatting | bytes 6291456
  156.2 2.4 %copy_select_fusion = bf16[768,2,8,128]{3,0,2,1:T(8,128)(2,1)} fusion(bf16[768,2,8,128]{3,2,1,0:T(8,128)(2,1)S(1)} %bitcast.130, pred[768]{0:T(1024)(128)(4,1)S(1)} %get-tuple-element.161), kind=kLoop, calls=%fused_computation.30 | loop fusion | flops 1572864 | bytes 6292224 | tf_op jit(solution)/shard_map/jit(_take)/select_n | solution.py:101
  158.6 36.2 %while.14 = (s32[]{:T(128)}, bf16[3,256,1024]{2,1,0:T(8,128)(2,1)S(1)}, s32[3]{0:T(128)S(1)}, s32[]{:T(128)}, bf16[768,2,8,128]{3,0,2,1:T(8,128)(2,1)}, /*index=...) while((s32[]{:T(128)}, ...), condition=%wide.region_12.13_spmd, body=%wide.region_9.12_spmd.sunk | while | flops 552465664 | bytes 35184420 | solution.py:53
  160.2 2.3 fusion.40
  162.5 1.9 copy-done
  166.1 4.3 %fusion.42 = bf16[8,128,1,256]{3,1,0,2:T(8,128)(2,1)S(1)} fusion(f32[8,256]{1,0:T(8,128)S(1)} %fusion.41, f32[8,256]{1,0:T(8,128)S(1)} %get-tuple-element.227, f32[8,512,256]{2,1,0:T(8,128)} %copy-done, pred[256,512]{0,1:T(8,128)(4,1)S(1)} %compare_and_fusion.3, bf16[768,2,8,128]{3,0,2,1:T(8,128)(2,1)} %get-tuple-element.258, s32[]{:T(128)S(6)} %max.10, ...), kind=kOutput, calls=%fused_computation.14.clone.1 | convolution fusion | flops 275251200 | bytes 5914888 | tf_op jit(solution)/shard_map/while/body/eval_jaxpr/kgqs,skd->qkgd/dot_general | solution.py:47
  172.3 2.3 fusion.40
  174.6 1.9 copy-done
  178.2 4.3 %fusion.42 = bf16[8,128,1,256]{3,1,0,2:T(8,128)(2,1)S(1)} fusion(f32[8,256]{1,0:T(8,128)S(1)} %fusion.41, f32[8,256]{1,0:T(8,128)S(1)} %get-tuple-element.227, f32[8,512,256]{2,1,0:T(8,128)} %copy-done, pred[256,512]{0,1:T(8,128)(4,1)S(1)} %compare_and_fusion.3, bf16[768,2,8,128]{3,0,2,1:T(8,128)(2,1)} %get-tuple-element.258, s32[]{:T(128)S(6)} %max.10, ...), kind=kOutput, calls=%fused_computation.14.clone.1 | convolution fusion | flops 275251200 | bytes 5914888 | tf_op jit(solution)/shard_map/while/body/eval_jaxpr/kgqs,skd->qkgd/dot_general | solution.py:47
  184.4 2.3 fusion.40
  186.7 1.9 copy-done
  190.2 4.3 %fusion.42 = bf16[8,128,1,256]{3,1,0,2:T(8,128)(2,1)S(1)} fusion(f32[8,256]{1,0:T(8,128)S(1)} %fusion.41, f32[8,256]{1,0:T(8,128)S(1)} %get-tuple-element.227, f32[8,512,256]{2,1,0:T(8,128)} %copy-done, pred[256,512]{0,1:T(8,128)(4,1)S(1)} %compare_and_fusion.3, bf16[768,2,8,128]{3,0,2,1:T(8,128)(2,1)} %get-tuple-element.258, s32[]{:T(128)S(6)} %max.10, ...), kind=kOutput, calls=%fused_computation.14.clone.1 | convolution fusion | flops 275251200 | bytes 5914888 | tf_op jit(solution)/shard_map/while/body/eval_jaxpr/kgqs,skd->qkgd/dot_general | solution.py:47
  194.8 40.5 %all_to_all.67 = bf16[4,192,1024]{2,1,0:T(8,128)(2,1)S(1)} all-to-all(bf16[4,192,1024]{2,1,0:T(8,128)(2,1)S(1)} %bitcast.138), channel_id=1, replica_groups=mesh['dp'=8,'ctx'=4] {'ctx'}, dimensions={0} | all-to-all | bytes 3145728 | tf_op jit(solution)/shard_map/all_to_all | solution.py:103
  (74 shorter events, 18.2 us)
Async XLA Ops:
  0.0 7.5 %copy-start.4 = (bf16[128,1024]{1,0:T(8,128)(2,1)S(1)}, bf16[128,1024]{1,0:T(8,128)(2,1)}, u32[]{:S(2)}) copy-start(bf16[128,1024]{1,0:T(8,128)(2,1)} %param.7) | copy-start | bytes 786436
  2.3 27.7 %all-to-all-start.2 = ((bf16[128,4,1024]{0,2,1:T(8,128)(2,1)}), bf16[128,4,1024]{0,2,1:T(8,128)(2,1)S(1)}, u32[]{:S(2)}, u32[]{:S(2)}) async-start(bf16[128,4,1024]{0,2,1:T(8,128)(2,1)} %bitcast.30), calls=%async_computation.2 | async-start | bytes 2097152 | tf_op jit(solution)/shard_map/all_to_all | solution.py:69
  14.8 22.5 %copy-start.5 = (s32[4096,1]{0,1:T(1,128)S(1)}, s32[4096,1]{0,1:T(1,128)}, u32[]{:S(2)}) copy-start(s32[4096,1]{0,1:T(1,128)} %param.8) | copy-start | bytes 49156
  30.0 51.3 %all-to-all-start = ((bf16[128,4,2048]{2,0,1:T(8,128)(2,1)}), bf16[128,4,2048]{2,0,1:T(8,128)(2,1)S(1)}, u32[]{:S(2)}, u32[]{:S(2)}) async-start(bf16[128,4,2048]{2,0,1:T(8,128)(2,1)} %all_to_all.48), calls=%async_computation | async-start | bytes 4194304 | tf_op jit(solution)/shard_map/all_to_all | solution.py:70
  81.2 1.4 copy-start.2
  82.6 23.8 %all-to-all-start.3 = ((bf16[8,96,1024]{2,1,0:T(8,128)(2,1)}), bf16[8,96,1024]{2,1,0:T(8,128)(2,1)S(1)}, u32[]{:S(2)}, u32[]{:S(2)}) async-start(bf16[8,96,1024]{2,1,0:T(8,128)(2,1)} %bitcast.33), calls=%async_computation.3 | async-start | bytes 3145728 | tf_op jit(solution)/shard_map/all_to_all | solution.py:86
  106.4 1.1 copy-start.1
  106.4 7.2 %copy-start.6 = (s32[1,768]{1,0:T(1,128)S(1)}, s32[1,768]{1,0:T(1,128)}, u32[]{:S(2)}) copy-start(s32[1,768]{1,0:T(1,128)} %param.9) | copy-start | bytes 9220
  107.5 41.5 %all-to-all-start.1 = ((bf16[8,96,2048]{2,1,0:T(8,128)(2,1)}), bf16[8,96,2048]{2,1,0:T(8,128)(2,1)S(1)}, u32[]{:S(2)}, u32[]{:S(2)}) async-start(bf16[8,96,2048]{2,1,0:T(8,128)(2,1)} %bitcast.129), calls=%async_computation.1 | async-start | bytes 6291456 | tf_op jit(solution)/shard_map/all_to_all | solution.py:89
  156.1 2.5 %copy-start.3 = (bf16[3,256,1024]{2,1,0:T(8,128)(2,1)S(1)}, bf16[3,256,1024]{2,1,0:T(8,128)(2,1)}, u32[]{:S(2)}) copy-start(bf16[3,256,1024]{2,1,0:T(8,128)(2,1)} %custom-call.4) | copy-start | bytes 4718596
  162.5 1.9 copy-start
  174.6 1.9 copy-start
  186.7 1.9 copy-start
where the time goes:
time: 240 us; the launch traced here: 237 us
  waiting for transfers between devices  83.8 us (35%)
  local copies, waits for them, and re-layouts  51.2 us (21%)
  blocking collectives  40.5 us (17%)
  starting transfers between devices  21.4 us (9%)
  matrix products  19.7 us (8%)
  other arithmetic  17.7 us (7%)
    all_to_all x1, blocking collectives, on_device(): lax.all_to_all(attended, 'ctx', split_axis=0, concat_axis=1, tiled=True)  40.5 us
    all_to_all x1, waiting for transfers between devices, on_device(): lax.all_to_all(wide_pairs, 'ctx', split_axis=1, concat_axis=0, tiled=True)  35.8 us
    all_to_all x1, waiting for transfers between devices, on_device(): lax.all_to_all(send_kv.reshape(dp_size, capacity, -1), 'dp', split_axis=0...  20 us
    all_to_all x1, waiting for transfers between devices, on_device(): lax.all_to_all(q_src, 'ctx', split_axis=1, concat_axis=0, tiled=True)  15.1 us
    dot_general x3, matrix products, one_block(): jnp.einsum('kgqs,skd->qkgd', weights, key_block[:, 1], preferred_element_...  12.8 us
    all_to_all x1, waiting for transfers between devices, on_device(): lax.all_to_all(send_q.reshape(dp_size, capacity, -1), 'dp', split_axis=0,...  12.8 us
    unnamed x16, local copies, waits for them, and re-layouts  10.1 us
    dot_general x3, matrix products, one_block(): jnp.einsum('qkgd,skd->kgqs', query_block, key_block[:, 0], preferred_elem...  6.88 us
  transfers between devices with their start and end apart: 4, of which 4 were waited for; matrix products, arithmetic and copies ran while one was open for 15% of the time, Pallas kernels for 0%

commit v1 on v0

v1 whole, which is shorter than its diff:
```python
import functools
import math

import jax
import jax.numpy as jnp
from jax import lax
from jax.experimental import pallas as pl
from jax.experimental.pallas import tpu as pltpu
from jax.sharding import PartitionSpec as P

Q_HEADS = 32
KV_HEADS = 4
HEAD_DIM = 128
BLOCK = 128
VMEM_LIMIT = 40 * 1024 * 1024
ANY = pl.BlockSpec(memory_space=pl.ANY)


def params():
    return pltpu.CompilerParams(vmem_limit_bytes=VMEM_LIMIT)


def cost(flops, moved, exps=0):
    return pl.CostEstimate(flops=int(flops), bytes_accessed=int(moved), transcendentals=int(exps))


def head_chunks(heads_dev):
    first = max(1, heads_dev // 4)
    second = (heads_dev - first + 1) // 2
    sizes = [first, second, heads_dev - first - second]
    chunks, start = [], 0
    for size in sizes:
        if size:
            chunks.append((start, size))
            start += size
    return chunks


def cut_kernel(chunks, ctx_size, with_kv, q_ref, kv_ref, *refs):
    outs, sem = refs[:-1], refs[-1]
    me = lax.axis_index("ctx")
    heads_dev = Q_HEADS // ctx_size
    group = Q_HEADS // KV_HEADS
    copies = []
    for at, (offset, heads) in enumerate(chunks):
        wide = heads * HEAD_DIM
        for step in list(range(1, ctx_size)) + [0]:
            owner = me ^ step
            out = outs[at * ctx_size + step]
            column = pl.multiple_of((owner * heads_dev + offset) * HEAD_DIM, HEAD_DIM)
            copies.append((q_ref.at[:, pl.ds(column, wide)], out.at[:, pl.ds(0, wide)]))
            if with_kv and at == 0:
                head = (owner * heads_dev) // group
                for half in range(2):
                    column = pl.multiple_of((half * KV_HEADS + head) * HEAD_DIM, HEAD_DIM)
                    copies.append(
                        (
                            kv_ref.at[:, pl.ds(column, HEAD_DIM)],
                            out.at[:, pl.ds(wide + half * HEAD_DIM, HEAD_DIM)],
                        )
                    )
    started = [pltpu.make_async_copy(a, b, sem.at[i]) for i, (a, b) in enumerate(copies)]
    for copy in started:
        copy.start()
    for copy in started:
        copy.wait()


def cut(q_src, kv_src, chunks, ctx_size, with_kv):
    rows = q_src.shape[0]
    shapes, number = [], 0
    for at, (_, heads) in enumerate(chunks):
        extra = 2 * HEAD_DIM if with_kv and at == 0 else 0
        number += ctx_size * (3 if extra else 1)
        shapes += [jax.ShapeDtypeStruct((rows, heads * HEAD_DIM + extra), jnp.bfloat16)] * ctx_size
    moved = 4 * sum([math.prod(s.shape) for s in shapes])
    outs = pl.pallas_call(
        functools.partial(cut_kernel, chunks, ctx_size, with_kv),
        out_shape=shapes,
        in_specs=[ANY, ANY],
        out_specs=[ANY] * len(shapes),
        scratch_shapes=[pltpu.SemaphoreType.DMA((number,))],
        compiler_params=params(),
        cost_estimate=cost(0, moved),
    )(q_src, kv_src)
    return [outs[i : i + ctx_size] for i in range(0, len(shapes), ctx_size)]


def swap(blocks, axis, size):
    return [blocks[0]] + [
        lax.ppermute(blocks[step], axis, [(j, j ^ step) for j in range(size)])
        for step in range(1, size)
    ]


def plan_kernel(capacity, ctx_size, route_ref, target_ref, slot_ref, live_ref, tmp):
    dp_size, length = route_ref.shape
    rows = length // ctx_size
    pack_len = dp_size * capacity
    own, me = lax.axis_index("dp"), lax.axis_index("ctx")
    mine = route_ref[pl.ds(own, 1), :]
    seq = lax.broadcasted_iota(jnp.int32, (dp_size, length), 0)
    onehot = jnp.where(mine == seq, 1.0, 0.0)
    earlier = lax.broadcasted_iota(jnp.int32, (length, length), 0)
    later = lax.broadcasted_iota(jnp.int32, (length, length), 1)
    strict = jnp.where(earlier < later, 1.0, 0.0).astype(jnp.bfloat16)
    before = jnp.dot(onehot.astype(jnp.bfloat16), strict, preferred_element_type=jnp.float32)
    rank = jnp.sum(before * onehot, axis=0, keepdims=True).astype(jnp.int32)
    tmp[...] = mine * capacity + rank
    for step in range(ctx_size):
        source = me ^ step
        target_ref[:, pl.ds(step * rows, rows)] = tmp[
            :, pl.ds(pl.multiple_of(source * rows, rows), rows)
        ]
    incoming = jnp.sum(
        jnp.where(route_ref[...] == own, 1.0, 0.0), axis=1, keepdims=True
    )
    group = lax.broadcasted_iota(jnp.int32, (dp_size, pack_len), 0)
    lane = lax.broadcasted_iota(jnp.int32, (dp_size, pack_len), 1)
    first = group * capacity
    inside = (lane >= first) & (lane < first + capacity)
    start = jnp.sum(jnp.where(lane >= first + capacity, incoming, 0.0), axis=0, keepdims=True)
    amount = jnp.sum(jnp.where(inside, incoming, 0.0), axis=0, keepdims=True).astype(jnp.int32)
    offset = jnp.sum(jnp.where(inside, lane - first, 0), axis=0, keepdims=True)
    slot_ref[...] = jnp.where(offset < amount, start.astype(jnp.int32) + offset, -1)
    live = jnp.sum(incoming, axis=0, keepdims=True).astype(jnp.int32)
    live_ref[...] = jnp.broadcast_to(live, live_ref.shape)


def plan(route, dp_size, ctx_size, capacity):
    length = route.shape[0] // dp_size
    return pl.pallas_call(
        functools.partial(plan_kernel, capacity, ctx_size),
        out_shape=[
            jax.ShapeDtypeStruct((1, length), jnp.int32),
            jax.ShapeDtypeStruct((1, dp_size * capacity), jnp.int32),
            jax.ShapeDtypeStruct((1, HEAD_DIM), jnp.int32),
        ],
        scratch_shapes=[pltpu.VMEM((1, length), jnp.int32)],
        compiler_params=params(),
        cost_estimate=cost(2 * dp_size * length * length, 8 * length * dp_size),
    )(route.reshape(dp_size, length))


def pack_kernel(capacity, target_ref, *refs):
    blocks, out_ref = refs[:-1], refs[-1]
    dp_size = out_ref.shape[0]
    length = target_ref.shape[1]
    together = math.gcd(dp_size, 8)
    data = jnp.concatenate([b[...] for b in blocks], axis=0)
    target = target_ref[...]
    high = together * capacity
    row = lax.broadcasted_iota(jnp.int32, (high, length), 0)
    for part in range(dp_size // together):
        place = jnp.where(target == row + part * high, 1.0, 0.0).astype(jnp.bfloat16)
        packed = jnp.dot(place, data, preferred_element_type=jnp.float32).astype(jnp.bfloat16)
        out_ref[part * together : (part + 1) * together] = packed.reshape(
            together, capacity, data.shape[1]
        )


def pack(target, blocks, dp_size, capacity):
    wide = blocks[0].shape[1]
    length = target.shape[1]
    size = dp_size * capacity * wide
    return pl.pallas_call(
        functools.partial(pack_kernel, capacity),
        out_shape=jax.ShapeDtypeStruct((dp_size, capacity, wide), jnp.bfloat16),
        compiler_params=params(),
        cost_estimate=cost(2 * size * length, 2 * size + 2 * length * wide),
    )(target, *blocks)


def attend_kernel(heads, doc_most, ctx_size, with_kv, recv_ref, slot_ref, live_ref, doc_ref, col_ref, *refs):
    if with_kv:
        outs, (kv_ref, acc) = refs[:ctx_size], refs[ctx_size:]
    else:
        kv_ref, outs, acc = refs[0], refs[1 : 1 + ctx_size], refs[1 + ctx_size]
    me = lax.axis_index("ctx")
    pack_len = acc.shape[0]
    wide = heads * HEAD_DIM
    scale = HEAD_DIM ** (-0.5) * math.log2(math.e)
    window = min(pack_len, doc_most + BLOCK)
    row = lax.broadcasted_iota(jnp.int32, (BLOCK, pack_len), 0)
    slot = slot_ref[...]
    live = live_ref[...]
    ones = jnp.ones((window, HEAD_DIM), jnp.bfloat16)
    received = recv_ref[...]
    for block in range(pack_len // BLOCK):
        begin = block * BLOCK
        rows = pl.ds(begin, BLOCK)
        place = jnp.where(slot == row + begin, 1.0, 0.0).astype(jnp.bfloat16)
        packed = jnp.dot(place, received, preferred_element_type=jnp.float32).astype(jnp.bfloat16)
        if with_kv:
            kv_ref[rows, :] = packed[:, wide:]
        key_start = max(0, begin + BLOCK - window)
        span = begin + BLOCK - key_start
        keys = kv_ref[pl.ds(key_start, span), :HEAD_DIM]
        values = jnp.concatenate([kv_ref[pl.ds(key_start, span), HEAD_DIM:], ones[:span]], axis=1)
        query_pos = begin + lax.broadcasted_iota(jnp.int32, (BLOCK, span), 0)
        key_pos = key_start + lax.broadcasted_iota(jnp.int32, (BLOCK, span), 1)
        docs = jnp.concatenate([col_ref[rows, :]] * (span // HEAD_DIM), axis=1)
        allowed = (docs == doc_ref[:, pl.ds(key_start, span)]) & (key_pos <= query_pos)
        alive = begin + lax.broadcasted_iota(jnp.int32, (BLOCK, HEAD_DIM), 0) < live
        for head in range(heads):
            query = packed[:, head * HEAD_DIM : (head + 1) * HEAD_DIM]
            scores = lax.dot_general(
                query, keys, (((1,), (1,)), ((), ())), preferred_element_type=jnp.float32
            )
            masked = jnp.where(allowed, scores, -1e30)
            top = jnp.max(masked, axis=1, keepdims=True)
            weights = jnp.exp2((masked - top) * scale).astype(jnp.bfloat16)
            mixed = jnp.dot(weights, values, preferred_element_type=jnp.float32)
            result = mixed[:, :HEAD_DIM] / mixed[:, HEAD_DIM:]
            acc[rows, head * HEAD_DIM : (head + 1) * HEAD_DIM] = jnp.where(
                alive, result, 0.0
            ).astype(jnp.bfloat16)
    part = pack_len // ctx_size
    for step in range(ctx_size):
        first = pl.multiple_of((me ^ step) * part, part)
        outs[step][...] = acc[pl.ds(first, part), :]


def attend(recv, slot, live, doc_row, doc_col, kv, heads, ctx_size):
    pack_len = recv.shape[0]
    doc_most = pack_len // 3
    wide = heads * HEAD_DIM
    with_kv = kv is None
    shapes = [jax.ShapeDtypeStruct((pack_len // ctx_size, wide), jnp.bfloat16)] * ctx_size
    if with_kv:
        shapes = shapes + [jax.ShapeDtypeStruct((pack_len, 2 * HEAD_DIM), jnp.bfloat16)]
    work = pack_len * (doc_most + BLOCK) * heads
    outs = pl.pallas_call(
        functools.partial(attend_kernel, heads, doc_most, ctx_size, with_kv),
        out_shape=shapes,
        scratch_shapes=[pltpu.VMEM((pack_len, wide), jnp.bfloat16)],
        compiler_params=params(),
        cost_estimate=cost(
            2 * pack_len * pack_len * recv.shape[1] + 6 * work * HEAD_DIM, 8 * pack_len * wide, work
        ),
    )(recv, slot, live, doc_row, doc_col, *([] if with_kv else [kv]))
    return list(outs[:ctx_size]), (outs[ctx_size] if with_kv else kv)


def join_kernel(chunk, ctx_size, first, *refs):
    offset, heads = chunk
    heads_dev = Q_HEADS // ctx_size
    blocks = refs[:ctx_size]
    out, sem = refs[-2:]
    me = lax.axis_index("ctx")
    copies = []
    for step in range(ctx_size):
        column = pl.multiple_of(((me ^ step) * heads_dev + offset) * HEAD_DIM, HEAD_DIM)
        copies.append(
            pltpu.make_async_copy(
                blocks[step], out.at[:, pl.ds(column, heads * HEAD_DIM)], sem.at[step]
            )
        )
    for copy in copies:
        copy.start()
    for copy in copies:
        copy.wait()


def join(blocks, chunk, out, ctx_size):
    rows = blocks[0].shape[0]
    given = [] if out is None else [out]
    return pl.pallas_call(
        functools.partial(join_kernel, chunk, ctx_size, out is None),
        out_shape=jax.ShapeDtypeStruct((rows, Q_HEADS * HEAD_DIM), jnp.bfloat16),
        in_specs=[ANY] * (ctx_size + len(given)),
        out_specs=ANY,
        scratch_shapes=[pltpu.SemaphoreType.DMA((ctx_size,))],
        input_output_aliases={ctx_size: 0} if given else {},
        compiler_params=params(),
        cost_estimate=cost(0, 4 * rows * chunk[1] * HEAD_DIM * ctx_size),
    )(*blocks, *given)


def on_device(q_src, kv_src, route, doc_ids):
    ctx_size = lax.axis_size("ctx")
    dp_size = lax.axis_size("dp")
    length = q_src.shape[0] * ctx_size
    capacity = 3 * length // (2 * dp_size)
    pack_len = dp_size * capacity
    chunks = head_chunks(Q_HEADS // ctx_size)

    cuts = cut(q_src, kv_src, chunks[:1], ctx_size, True)
    if chunks[1:]:
        cuts = cuts + cut(q_src, kv_src, chunks[1:], ctx_size, False)
    gathered = [swap(blocks, "ctx", ctx_size) for blocks in cuts]
    target, slot, live = plan(route, dp_size, ctx_size, capacity)
    doc_col = jnp.broadcast_to(doc_ids.reshape(pack_len, 1), (pack_len, HEAD_DIM))

    received = []
    for blocks in gathered:
        sent = pack(target, blocks, dp_size, capacity)
        got = lax.all_to_all(sent, "dp", split_axis=0, concat_axis=0, tiled=True)
        received.append(got.reshape(pack_len, -1))

    kv, out = None, None
    for chunk, recv in zip(chunks, received):
        blocks, kv = attend(recv, slot, live, doc_ids, doc_col, kv, chunk[1], ctx_size)
        out = join(swap(blocks, "ctx", ctx_size), chunk, out, ctx_size)
    return out


def solution(mesh):
    in_specs = (P(("dp", "ctx"), None), P(("dp", "ctx"), None), P(), P("dp", None))
    out_specs = P(("dp", "ctx"), None)
    return jax.shard_map(
        on_device, mesh=mesh, in_specs=in_specs, out_specs=out_specs, check_vma=False
    )
```

time: 240 us -> 106 us (0.44); the launches traced: 237 us -> 105 us
  local copies, waits for them, and re-layouts: 51.2 us -> 3.86 us
  blocking collectives: 40.5 us -> 0 us
  waiting for transfers between devices: 83.8 us -> 50.4 us
  matrix products: 19.7 us -> 0 us
  Pallas kernels: 0 us -> 17.4 us
  other arithmetic: 17.7 us -> 1.42 us
  starting transfers between devices: 21.4 us -> 31.9 us
    all_to_all x4 -> x3, waiting for transfers between devices: 83.8 us -> 0.01 us  [on_device(): got = lax.all_to_all(sent, 'dp', split_axis=0, concat_axis=0, tiled=True)]
    ppermute x0 -> x18, waiting for transfers between devices: none -> 50.4 us  [swap(): lax.ppermute(blocks[step], axis, [(j, j ^ step) for j in range(size)])]
    all_to_all x1 -> x0, blocking collectives: 40.5 us -> none  [on_device(): lax.all_to_all(attended, 'ctx', split_axis=0, concat_axis=1, tiled=True)]
    dot_general x6 -> x0, matrix products: 19.7 us -> none  [the longest x3 12.8 us: one_block(): jnp.einsum('kgqs,skd->qkgd', weights, key_block[:, 1], preferred_element_...]
    ppermute x0 -> x18, starting transfers between devices: none -> 19.1 us  [swap(): lax.ppermute(blocks[step], axis, [(j, j ^ step) for j in range(size)])]
    pallas_call x0 -> x12, Pallas kernels: none -> 17.4 us  [the longest x3 10 us: attend(): pl.pallas_call(functools.partial(attend_kernel, heads, doc_most, ctx_size...]
    scatter x2 -> x0, local copies, waits for them, and re-layouts: 11.2 us -> none  [the longest x1 6.71 us: on_device(): jnp.zeros((pack_len, kv_pairs.shape[1]), jnp.bfloat16).at[target]]
    gather x3 -> x0, local copies, waits for them, and re-layouts: 11 us -> none  [the longest x1 6.17 us: on_device(): packed_q = jnp.take(recv_q.reshape(pack_len, -1), gather_idx, axis=0)]
  transfers between devices with their start and end apart: 4 -> 21, of which waited for: 4 -> 13; matrix products, arithmetic and copies ran while one was open for 15% -> 2% of each run, Pallas kernels for 0% -> 14%
where the time goes in v1:
time: 106 us; the launch traced here: 105 us
  waiting for transfers between devices  50.4 us (48%)
  starting transfers between devices  31.9 us (30%)
  Pallas kernels  17.4 us (16%)
  local copies, waits for them, and re-layouts  3.86 us (4%)
  other arithmetic  1.42 us (1%)
    ppermute x18, waiting for transfers between devices, swap(): lax.ppermute(blocks[step], axis, [(j, j ^ step) for j in range(size)])  50.4 us
    ppermute x18, starting transfers between devices, swap(): lax.ppermute(blocks[step], axis, [(j, j ^ step) for j in range(size)])  19.1 us
    all_to_all x3, starting transfers between devices, on_device(): got = lax.all_to_all(sent, 'dp', split_axis=0, concat_axis=0, tiled=True)  12.8 us
    pallas_call x3, Pallas kernels, attend(): pl.pallas_call(functools.partial(attend_kernel, heads, doc_most, ctx_size...  10 us
    pallas_call x3, Pallas kernels, pack(): pl.pallas_call(functools.partial(pack_kernel, capacity), out_shape=jax.Sh...  4.22 us
    unnamed x15, local copies, waits for them, and re-layouts  3.7 us
    pallas_call x3, Pallas kernels, join(): pl.pallas_call(functools.partial(join_kernel, chunk, ctx_size, out is Non...  2.45 us
  transfers between devices with their start and end apart: 21, of which 13 were waited for; matrix products, arithmetic and copies ran while one was open for 2% of the time, Pallas kernels for 14%

profile of v1, /device:TPU:18, one launch (start us, length us, event | category | flops | bytes accessed | tf_op | source)
XLA Modules:
  0.0 105.3 jit_solution(11274009434256312849)
XLA Ops:
  0.0 1.2 %copy-done = bf16[128,4096]{1,0:T(8,128)(2,1)S(1)} copy-done((bf16[128,4096]{1,0:T(8,128)(2,1)S(1)}, bf16[128,4096]{1,0:T(8,128)(2,1)}, u32[]{:S(2)}) %copy-start) | copy-done | bytes 1048600
  2.4 1.6 %collective-permute-start.9 = (bf16[128,384]{1,0:T(8,128)(2,1)S(1)}, bf16[128,384]{1,0:T(8,128)(2,1)S(1)}, u32[]{:S(2)}, u32[]{:S(2)}) collective-permute-start(bf16[128,384]{1,0:T(8,128)(2,1)S(1)} %get-tuple-element.50), channel_id=1, source_target_pairs={{0,1},{1,0},{2,3},{3,2},{4,5},{5,4},{6,7},{7,6},{8,9},{9,8},{10,11... | collective-permute-start | bytes 294920 | tf_op jit(solution)/shard_map/ppermute | solution.py:91
  4.4 1.6 %collective-permute-start.11 = (bf16[128,384]{1,0:T(8,128)(2,1)S(1)}, bf16[128,384]{1,0:T(8,128)(2,1)S(1)}, u32[]{:S(2)}, u32[]{:S(2)}) collective-permute-start(bf16[128,384]{1,0:T(8,128)(2,1)S(1)} %get-tuple-element.52), channel_id=1, source_target_pairs={{0,3},{1,2},{2,1},{3,0},{4,7},{5,6},{6,5},{7,4},{8,11},{9,10},{10,... | collective-permute-start | bytes 294920 | tf_op jit(solution)/shard_map/ppermute | solution.py:91
  6.5 1.4 %reduce.4 = s32[4096]{0:T(1024)S(1)} reduce(s32[4096,1]{0,1:T(1,128)} %param.6, s32[]{:T(128)} %broadcast.4), dimensions={1}, to_apply=%param.6.reduce_sub_computation.3 | reduce | bytes 32772 | tf_op args[2]
  8.1 3.3 %collective-permute-done.10.refs_2_ = bf16[128,384]{1,0:T(8,128)(2,1)S(1)} collective-permute-done((bf16[128,384]{1,0:T(8,128)(2,1)S(1)}, bf16[128,384]{1,0:T(8,128)(2,1)S(1)}, u32[]{:S(2)}, u32[]{:S(2)}) %collective-permute-start.10) | collective-permute-done | bytes 98336 | tf_op jit(solution)/shard_map/ppermute | solution.py:91
  11.4 3.1 %collective-permute-done.11.refs_3_ = bf16[128,384]{1,0:T(8,128)(2,1)S(1)} collective-permute-done((bf16[128,384]{1,0:T(8,128)(2,1)S(1)}, bf16[128,384]{1,0:T(8,128)(2,1)S(1)}, u32[]{:S(2)}, u32[]{:S(2)}) %collective-permute-start.11) | collective-permute-done | bytes 98336 | tf_op jit(solution)/shard_map/ppermute | solution.py:91
  14.5 1.4 %shard_map.53 = bf16[8,96,384]{2,1,0:T(8,128)(2,1)} custom-call(s32[1,512]{1,0:T(1,128)S(1)} %get-tuple-element.33.target_ref, bf16[128,384]{1,0:T(8,128)(2,1)S(1)} %get-tuple-element.49.refs_0_, bf16[128,384]{1,0:T(8,128)(2,1)S(1)} %collective-permute-done.9.refs_1_, bf16[128,384]{1,0:T(8,128)(2,1)S(1)} %collective-permute-done.10.refs_2_, ...), custom_call_target="tpu_custom_call" | custom-call | flops 301989888 | bytes 983040 | tf_op jit(solution)/shard_map/pallas_call | solution.py:166
  15.9 4.3 %all-to-all-start.2 = ((bf16[8,96,384]{2,1,0:T(8,128)(2,1)}), bf16[8,96,384]{2,1,0:T(8,128)(2,1)S(1)}, u32[]{:S(2)}, u32[]{:S(2)}) async-start(bf16[8,96,384]{2,1,0:T(8,128)(2,1)} %shard_map.53), calls=%async_computation.2 | async-start | bytes 1179648 | tf_op jit(solution)/shard_map/all_to_all | solution.py:298
  20.9 1.5 %collective-permute-start.4 = (bf16[128,512]{1,0:T(8,128)(2,1)S(1)}, bf16[128,512]{1,0:T(8,128)(2,1)S(1)}, u32[]{:S(2)}, u32[]{:S(2)}) collective-permute-start(bf16[128,512]{1,0:T(8,128)(2,1)S(1)} %get-tuple-element.42), channel_id=1, source_target_pairs={{0,2},{1,3},{2,0},{3,1},{4,6},{5,7},{6,4},{7,5},{8,10},{9,11},{10,... | collective-permute-start | bytes 393224 | tf_op jit(solution)/shard_map/ppermute | solution.py:91
  22.4 1.6 %collective-permute-start.5 = (bf16[128,512]{1,0:T(8,128)(2,1)S(1)}, bf16[128,512]{1,0:T(8,128)(2,1)S(1)}, u32[]{:S(2)}, u32[]{:S(2)}) collective-permute-start(bf16[128,512]{1,0:T(8,128)(2,1)S(1)} %get-tuple-element.43), channel_id=1, source_target_pairs={{0,3},{1,2},{2,1},{3,0},{4,7},{5,6},{6,5},{7,4},{8,11},{9,10},{10,... | collective-permute-start | bytes 393224 | tf_op jit(solution)/shard_map/ppermute | solution.py:91
  24.0 2.9 %collective-permute-done.3.refs_1_ = bf16[128,512]{1,0:T(8,128)(2,1)S(1)} collective-permute-done((bf16[128,512]{1,0:T(8,128)(2,1)S(1)}, bf16[128,512]{1,0:T(8,128)(2,1)S(1)}, u32[]{:S(2)}, u32[]{:S(2)}) %collective-permute-start.3) | collective-permute-done | bytes 131104 | tf_op jit(solution)/shard_map/ppermute | solution.py:91
  26.8 5.1 %collective-permute-done.4.refs_2_ = bf16[128,512]{1,0:T(8,128)(2,1)S(1)} collective-permute-done((bf16[128,512]{1,0:T(8,128)(2,1)S(1)}, bf16[128,512]{1,0:T(8,128)(2,1)S(1)}, u32[]{:S(2)}, u32[]{:S(2)}) %collective-permute-start.4) | collective-permute-done | bytes 131104 | tf_op jit(solution)/shard_map/ppermute | solution.py:91
  31.9 3.7 %collective-permute-done.5.refs_3_ = bf16[128,512]{1,0:T(8,128)(2,1)S(1)} collective-permute-done((bf16[128,512]{1,0:T(8,128)(2,1)S(1)}, bf16[128,512]{1,0:T(8,128)(2,1)S(1)}, u32[]{:S(2)}, u32[]{:S(2)}) %collective-permute-start.5) | collective-permute-done | bytes 131104 | tf_op jit(solution)/shard_map/ppermute | solution.py:91
  35.7 1.5 %shard_map.50 = bf16[8,96,512]{2,1,0:T(8,128)(2,1)} custom-call(s32[1,512]{1,0:T(1,128)S(1)} %get-tuple-element.33.target_ref, bf16[128,512]{1,0:T(8,128)(2,1)S(1)} %get-tuple-element.40.refs_0_, bf16[128,512]{1,0:T(8,128)(2,1)S(1)} %collective-permute-done.3.refs_1_, bf16[128,512]{1,0:T(8,128)(2,1)S(1)} %collective-permute-done.4.refs_2_, ...), custom_call_target="tpu_custom_call" | custom-call | flops 402653184 | bytes 1310720 | tf_op jit(solution)/shard_map/pallas_call | solution.py:166
  37.1 4.3 %all-to-all-start.1 = ((bf16[8,96,512]{2,1,0:T(8,128)(2,1)}), bf16[8,96,512]{2,1,0:T(8,128)(2,1)S(1)}, u32[]{:S(2)}, u32[]{:S(2)}) async-start(bf16[8,96,512]{2,1,0:T(8,128)(2,1)} %shard_map.50), calls=%async_computation.1 | async-start | bytes 1572864 | tf_op jit(solution)/shard_map/all_to_all | solution.py:298
  41.4 2.0 %collective-permute-start.1 = (bf16[128,384]{1,0:T(8,128)(2,1)S(1)}, bf16[128,384]{1,0:T(8,128)(2,1)S(1)}, u32[]{:S(2)}, u32[]{:S(2)}) collective-permute-start(bf16[128,384]{1,0:T(8,128)(2,1)S(1)} %get-tuple-element.36), channel_id=1, source_target_pairs={{0,2},{1,3},{2,0},{3,1},{4,6},{5,7},{6,4},{7,5},{8,10},{9,11},{10,... | collective-permute-start | bytes 294920 | tf_op jit(solution)/shard_map/ppermute | solution.py:91
  43.4 1.5 %collective-permute-start.2 = (bf16[128,384]{1,0:T(8,128)(2,1)S(1)}, bf16[128,384]{1,0:T(8,128)(2,1)S(1)}, u32[]{:S(2)}, u32[]{:S(2)}) collective-permute-start(bf16[128,384]{1,0:T(8,128)(2,1)S(1)} %get-tuple-element.37), channel_id=1, source_target_pairs={{0,3},{1,2},{2,1},{3,0},{4,7},{5,6},{6,5},{7,4},{8,11},{9,10},{10,... | collective-permute-start | bytes 294920 | tf_op jit(solution)/shard_map/ppermute | solution.py:91
  44.9 2.1 %collective-permute-done.refs_1_ = bf16[128,384]{1,0:T(8,128)(2,1)S(1)} collective-permute-done((bf16[128,384]{1,0:T(8,128)(2,1)S(1)}, bf16[128,384]{1,0:T(8,128)(2,1)S(1)}, u32[]{:S(2)}, u32[]{:S(2)}) %collective-permute-start) | collective-permute-done | bytes 98336 | tf_op jit(solution)/shard_map/ppermute | solution.py:91
  47.1 3.6 %collective-permute-done.1.refs_2_ = bf16[128,384]{1,0:T(8,128)(2,1)S(1)} collective-permute-done((bf16[128,384]{1,0:T(8,128)(2,1)S(1)}, bf16[128,384]{1,0:T(8,128)(2,1)S(1)}, u32[]{:S(2)}, u32[]{:S(2)}) %collective-permute-start.1) | collective-permute-done | bytes 98336 | tf_op jit(solution)/shard_map/ppermute | solution.py:91
  50.7 3.1 %collective-permute-done.2.refs_3_ = bf16[128,384]{1,0:T(8,128)(2,1)S(1)} collective-permute-done((bf16[128,384]{1,0:T(8,128)(2,1)S(1)}, bf16[128,384]{1,0:T(8,128)(2,1)S(1)}, u32[]{:S(2)}, u32[]{:S(2)}) %collective-permute-start.2) | collective-permute-done | bytes 98336 | tf_op jit(solution)/shard_map/ppermute | solution.py:91
  53.8 1.4 %shard_map.48 = bf16[8,96,384]{2,1,0:T(8,128)(2,1)} custom-call(s32[1,512]{1,0:T(1,128)S(1)} %get-tuple-element.33.target_ref, bf16[128,384]{1,0:T(8,128)(2,1)S(1)} %get-tuple-element.34.refs_0_, bf16[128,384]{1,0:T(8,128)(2,1)S(1)} %collective-permute-done.refs_1_, bf16[128,384]{1,0:T(8,128)(2,1)S(1)} %collective-permute-done.1.refs_2_, ...), custom_call_target="tpu_custom_call" | custom-call | flops 301989888 | bytes 983040 | tf_op jit(solution)/shard_map/pallas_call | solution.py:166
  55.2 4.2 %all-to-all-start = ((bf16[8,96,384]{2,1,0:T(8,128)(2,1)}), bf16[8,96,384]{2,1,0:T(8,128)(2,1)S(1)}, u32[]{:S(2)}, u32[]{:S(2)}) async-start(bf16[8,96,384]{2,1,0:T(8,128)(2,1)} %shard_map.48), calls=%async_computation | async-start | bytes 1179648 | tf_op jit(solution)/shard_map/all_to_all | solution.py:298
  59.6 3.6 %shard_map.51 = (bf16[192,256]{1,0:T(8,128)(2,1)S(1)}, bf16[192,256]{1,0:T(8,128)(2,1)S(1)}, bf16[192,256]{1,0:T(8,128)(2,1)S(1)}, bf16[192,256]{1,0:T(8,128)(2,1)S(1)}, bf16[768,256]{1,0:T(8,128)(2,1)S(1)}) custom-call(bf16[768,512]{1,0:T(8,128)(2,1)S(1)} %bitcast.4, s32[1,768]{1,0:T(1,128)S(1)} %get-tuple-element.38.slot_ref, ...), custom_call_target="tpu_custom_call" | custom-call | flops 1056964608 | bytes 1572864 | tf_op jit(solution)/shard_map/pallas_call | solution.py:233
  63.2 3.2 %shard_map.54 = (bf16[192,384]{1,0:T(8,128)(2,1)S(1)}, bf16[192,384]{1,0:T(8,128)(2,1)S(1)}, bf16[192,384]{1,0:T(8,128)(2,1)S(1)}, bf16[192,384]{1,0:T(8,128)(2,1)S(1)}) custom-call(bf16[768,384]{1,0:T(8,128)(2,1)S(1)} %bitcast.5, s32[1,768]{1,0:T(1,128)S(1)} %get-tuple-element.38.slot_ref, s32[1,128]{1,0:T(1,128)S(1)} %get-tuple-element.39.live_ref, ...), custom_call_target="tpu_custom_call" | custom-call | flops 1132462080 | bytes 2359296 | tf_op jit(solution)/shard_map/pallas_call | solution.py:233
  66.5 2.0 %collective-permute-start.15 = (bf16[192,256]{1,0:T(8,128)(2,1)S(1)}, bf16[192,256]{1,0:T(8,128)(2,1)S(1)}, u32[]{:S(2)}, u32[]{:S(2)}) collective-permute-start(bf16[192,256]{1,0:T(8,128)(2,1)S(1)} %get-tuple-element.58), channel_id=1, source_target_pairs={{0,1},{1,0},{2,3},{3,2},{4,5},{5,4},{6,7},{7,6},{8,9},{9,8},{10,11... | collective-permute-start | bytes 294920 | tf_op jit(solution)/shard_map/ppermute | solution.py:91
  68.8 1.2 %collective-permute-start.17 = (bf16[192,256]{1,0:T(8,128)(2,1)S(1)}, bf16[192,256]{1,0:T(8,128)(2,1)S(1)}, u32[]{:S(2)}, u32[]{:S(2)}) collective-permute-start(bf16[192,256]{1,0:T(8,128)(2,1)S(1)} %get-tuple-element.60), channel_id=1, source_target_pairs={{0,3},{1,2},{2,1},{3,0},{4,7},{5,6},{6,5},{7,4},{8,11},{9,10},{10,... | collective-permute-start | bytes 294920 | tf_op jit(solution)/shard_map/ppermute | solution.py:91
  70.1 2.8 %collective-permute-start.13 = (bf16[192,384]{1,0:T(8,128)(2,1)S(1)}, bf16[192,384]{1,0:T(8,128)(2,1)S(1)}, u32[]{:S(2)}, u32[]{:S(2)}) collective-permute-start(bf16[192,384]{1,0:T(8,128)(2,1)S(1)} %get-tuple-element.55), channel_id=1, source_target_pairs={{0,2},{1,3},{2,0},{3,1},{4,6},{5,7},{6,4},{7,5},{8,10},{9,11},{10,... | collective-permute-start | bytes 442376 | tf_op jit(solution)/shard_map/ppermute | solution.py:91
  73.9 3.2 %shard_map.52 = (bf16[192,384]{1,0:T(8,128)(2,1)S(1)}, bf16[192,384]{1,0:T(8,128)(2,1)S(1)}, bf16[192,384]{1,0:T(8,128)(2,1)S(1)}, bf16[192,384]{1,0:T(8,128)(2,1)S(1)}) custom-call(bf16[768,384]{1,0:T(8,128)(2,1)S(1)} %bitcast.6, s32[1,768]{1,0:T(1,128)S(1)} %get-tuple-element.38.slot_ref, s32[1,128]{1,0:T(1,128)S(1)} %get-tuple-element.39.live_ref, ...), custom_call_target="tpu_custom_call" | custom-call | flops 1132462080 | bytes 2359296 | tf_op jit(solution)/shard_map/pallas_call | solution.py:233
  77.1 1.5 %collective-permute-start.14 = (bf16[192,384]{1,0:T(8,128)(2,1)S(1)}, bf16[192,384]{1,0:T(8,128)(2,1)S(1)}, u32[]{:S(2)}, u32[]{:S(2)}) collective-permute-start(bf16[192,384]{1,0:T(8,128)(2,1)S(1)} %get-tuple-element.56), channel_id=1, source_target_pairs={{0,3},{1,2},{2,1},{3,0},{4,7},{5,6},{6,5},{7,4},{8,11},{9,10},{10,... | collective-permute-start | bytes 442376 | tf_op jit(solution)/shard_map/ppermute | solution.py:91
  79.1 7.1 %collective-permute-done.17.refs_3_ = bf16[192,256]{1,0:T(8,128)(2,1)S(1)} collective-permute-done((bf16[192,256]{1,0:T(8,128)(2,1)S(1)}, bf16[192,256]{1,0:T(8,128)(2,1)S(1)}, u32[]{:S(2)}, u32[]{:S(2)}) %collective-permute-start.17) | collective-permute-done | bytes 98336 | tf_op jit(solution)/shard_map/ppermute | solution.py:91
  88.1 10.8 %collective-permute-done.14.refs_3_ = bf16[192,384]{1,0:T(8,128)(2,1)S(1)} collective-permute-done((bf16[192,384]{1,0:T(8,128)(2,1)S(1)}, bf16[192,384]{1,0:T(8,128)(2,1)S(1)}, u32[]{:S(2)}, u32[]{:S(2)}) %collective-permute-start.14) | collective-permute-done | bytes 147488 | tf_op jit(solution)/shard_map/ppermute | solution.py:91
  100.1 4.2 %collective-permute-done.8.refs_3_ = bf16[192,384]{1,0:T(8,128)(2,1)S(1)} collective-permute-done((bf16[192,384]{1,0:T(8,128)(2,1)S(1)}, bf16[192,384]{1,0:T(8,128)(2,1)S(1)}, u32[]{:S(2)}, u32[]{:S(2)}) %collective-permute-start.8) | collective-permute-done | bytes 147488 | tf_op jit(solution)/shard_map/ppermute | solution.py:91
  (41 shorter events, 8.9 us)
Async XLA Ops:
  0.0 1.2 %copy-start = (bf16[128,4096]{1,0:T(8,128)(2,1)S(1)}, bf16[128,4096]{1,0:T(8,128)(2,1)}, u32[]{:S(2)}) copy-start(bf16[128,4096]{1,0:T(8,128)(2,1)} %q_ref.3) | copy-start | bytes 3145732
  1.2 0.9 copy-start.2
  2.2 18.0 %copy-start.1 = (bf16[128,4096]{1,0:T(8,128)(2,1)S(1)}, bf16[128,4096]{1,0:T(8,128)(2,1)}, u32[]{:S(2)}) copy-start(bf16[128,4096]{1,0:T(8,128)(2,1)} %q_ref.3) | copy-start | bytes 3145732
  2.2 18.0 %copy-start.3 = (bf16[128,1024]{1,0:T(8,128)(2,1)S(1)}, bf16[128,1024]{1,0:T(8,128)(2,1)}, u32[]{:S(2)}) copy-start(bf16[128,1024]{1,0:T(8,128)(2,1)} %kv_ref.3) | copy-start | bytes 786436
  2.4 5.7 %collective-permute-start.9 = (bf16[128,384]{1,0:T(8,128)(2,1)S(1)}, bf16[128,384]{1,0:T(8,128)(2,1)S(1)}, u32[]{:S(2)}, u32[]{:S(2)}) collective-permute-start(bf16[128,384]{1,0:T(8,128)(2,1)S(1)} %get-tuple-element.50), channel_id=1, source_target_pairs={{0,1},{1,0},{2,3},{3,2},{4,5},{5,4},{6,7},{7,6},{8,9},{9,8},{10,11... | collective-permute-start | bytes 294920 | tf_op jit(solution)/shard_map/ppermute | solution.py:91
  4.0 7.4 %collective-permute-start.10 = (bf16[128,384]{1,0:T(8,128)(2,1)S(1)}, bf16[128,384]{1,0:T(8,128)(2,1)S(1)}, u32[]{:S(2)}, u32[]{:S(2)}) collective-permute-start(bf16[128,384]{1,0:T(8,128)(2,1)S(1)} %get-tuple-element.51), channel_id=1, source_target_pairs={{0,2},{1,3},{2,0},{3,1},{4,6},{5,7},{6,4},{7,5},{8,10},{9,11},{10,... | collective-permute-start | bytes 294920 | tf_op jit(solution)/shard_map/ppermute | solution.py:91
  4.4 10.1 %collective-permute-start.11 = (bf16[128,384]{1,0:T(8,128)(2,1)S(1)}, bf16[128,384]{1,0:T(8,128)(2,1)S(1)}, u32[]{:S(2)}, u32[]{:S(2)}) collective-permute-start(bf16[128,384]{1,0:T(8,128)(2,1)S(1)} %get-tuple-element.52), channel_id=1, source_target_pairs={{0,3},{1,2},{2,1},{3,0},{4,7},{5,6},{6,5},{7,4},{8,11},{9,10},{10,... | collective-permute-start | bytes 294920 | tf_op jit(solution)/shard_map/ppermute | solution.py:91
  15.9 21.2 %all-to-all-start.2 = ((bf16[8,96,384]{2,1,0:T(8,128)(2,1)}), bf16[8,96,384]{2,1,0:T(8,128)(2,1)S(1)}, u32[]{:S(2)}, u32[]{:S(2)}) async-start(bf16[8,96,384]{2,1,0:T(8,128)(2,1)} %shard_map.53), calls=%async_computation.2 | async-start | bytes 1179648 | tf_op jit(solution)/shard_map/all_to_all | solution.py:298
  20.4 6.4 %collective-permute-start.3 = (bf16[128,512]{1,0:T(8,128)(2,1)S(1)}, bf16[128,512]{1,0:T(8,128)(2,1)S(1)}, u32[]{:S(2)}, u32[]{:S(2)}) collective-permute-start(bf16[128,512]{1,0:T(8,128)(2,1)S(1)} %get-tuple-element.41), channel_id=1, source_target_pairs={{0,1},{1,0},{2,3},{3,2},{4,5},{5,4},{6,7},{7,6},{8,9},{9,8},{10,11... | collective-permute-start | bytes 393224 | tf_op jit(solution)/shard_map/ppermute | solution.py:91
  20.9 11.0 %collective-permute-start.4 = (bf16[128,512]{1,0:T(8,128)(2,1)S(1)}, bf16[128,512]{1,0:T(8,128)(2,1)S(1)}, u32[]{:S(2)}, u32[]{:S(2)}) collective-permute-start(bf16[128,512]{1,0:T(8,128)(2,1)S(1)} %get-tuple-element.42), channel_id=1, source_target_pairs={{0,2},{1,3},{2,0},{3,1},{4,6},{5,7},{6,4},{7,5},{8,10},{9,11},{10,... | collective-permute-start | bytes 393224 | tf_op jit(solution)/shard_map/ppermute | solution.py:91
  22.4 13.2 %collective-permute-start.5 = (bf16[128,512]{1,0:T(8,128)(2,1)S(1)}, bf16[128,512]{1,0:T(8,128)(2,1)S(1)}, u32[]{:S(2)}, u32[]{:S(2)}) collective-permute-start(bf16[128,512]{1,0:T(8,128)(2,1)S(1)} %get-tuple-element.43), channel_id=1, source_target_pairs={{0,3},{1,2},{2,1},{3,0},{4,7},{5,6},{6,5},{7,4},{8,11},{9,10},{10,... | collective-permute-start | bytes 393224 | tf_op jit(solution)/shard_map/ppermute | solution.py:91
  37.1 22.3 %copy-start.4 = (s32[1,768]{1,0:T(1,128)S(1)}, s32[1,768]{1,0:T(1,128)}, u32[]{:S(2)}) copy-start(s32[1,768]{1,0:T(1,128)} %doc_ref.5) | copy-start | bytes 9220
  37.1 18.1 %all-to-all-start.1 = ((bf16[8,96,512]{2,1,0:T(8,128)(2,1)}), bf16[8,96,512]{2,1,0:T(8,128)(2,1)S(1)}, u32[]{:S(2)}, u32[]{:S(2)}) async-start(bf16[8,96,512]{2,1,0:T(8,128)(2,1)} %shard_map.50), calls=%async_computation.1 | async-start | bytes 1572864 | tf_op jit(solution)/shard_map/all_to_all | solution.py:298
  41.4 5.6 %collective-permute-start = (bf16[128,384]{1,0:T(8,128)(2,1)S(1)}, bf16[128,384]{1,0:T(8,128)(2,1)S(1)}, u32[]{:S(2)}, u32[]{:S(2)}) collective-permute-start(bf16[128,384]{1,0:T(8,128)(2,1)S(1)} %get-tuple-element.35), channel_id=1, source_target_pairs={{0,1},{1,0},{2,3},{3,2},{4,5},{5,4},{6,7},{7,6},{8,9},{9,8},{10,11... | collective-permute-start | bytes 294920 | tf_op jit(solution)/shard_map/ppermute | solution.py:91
  41.4 9.3 %collective-permute-start.1 = (bf16[128,384]{1,0:T(8,128)(2,1)S(1)}, bf16[128,384]{1,0:T(8,128)(2,1)S(1)}, u32[]{:S(2)}, u32[]{:S(2)}) collective-permute-start(bf16[128,384]{1,0:T(8,128)(2,1)S(1)} %get-tuple-element.36), channel_id=1, source_target_pairs={{0,2},{1,3},{2,0},{3,1},{4,6},{5,7},{6,4},{7,5},{8,10},{9,11},{10,... | collective-permute-start | bytes 294920 | tf_op jit(solution)/shard_map/ppermute | solution.py:91
  43.4 10.4 %collective-permute-start.2 = (bf16[128,384]{1,0:T(8,128)(2,1)S(1)}, bf16[128,384]{1,0:T(8,128)(2,1)S(1)}, u32[]{:S(2)}, u32[]{:S(2)}) collective-permute-start(bf16[128,384]{1,0:T(8,128)(2,1)S(1)} %get-tuple-element.37), channel_id=1, source_target_pairs={{0,3},{1,2},{2,1},{3,0},{4,7},{5,6},{6,5},{7,4},{8,11},{9,10},{10,... | collective-permute-start | bytes 294920 | tf_op jit(solution)/shard_map/ppermute | solution.py:91
  55.2 17.7 %all-to-all-start = ((bf16[8,96,384]{2,1,0:T(8,128)(2,1)}), bf16[8,96,384]{2,1,0:T(8,128)(2,1)S(1)}, u32[]{:S(2)}, u32[]{:S(2)}) async-start(bf16[8,96,384]{2,1,0:T(8,128)(2,1)} %shard_map.48), calls=%async_computation | async-start | bytes 1179648 | tf_op jit(solution)/shard_map/all_to_all | solution.py:298
  63.2 3.2 %copy-start.5 = (bf16[768,256]{1,0:T(8,128)(2,1)}, bf16[768,256]{1,0:T(8,128)(2,1)S(1)}, u32[]{:S(2)}) copy-start(bf16[768,256]{1,0:T(8,128)(2,1)S(1)} %get-tuple-element.44.refs_0_) | copy-start | bytes 1179652
  66.4 19.8 %collective-permute-start.12 = (bf16[192,384]{1,0:T(8,128)(2,1)S(1)}, bf16[192,384]{1,0:T(8,128)(2,1)S(1)}, u32[]{:S(2)}, u32[]{:S(2)}) collective-permute-start(bf16[192,384]{1,0:T(8,128)(2,1)S(1)} %get-tuple-element.54), channel_id=1, source_target_pairs={{0,1},{1,0},{2,3},{3,2},{4,5},{5,4},{6,7},{7,6},{8,9},{9,8},{10,11... | collective-permute-start | bytes 442376 | tf_op jit(solution)/shard_map/ppermute | solution.py:91
  66.5 10.6 %collective-permute-start.15 = (bf16[192,256]{1,0:T(8,128)(2,1)S(1)}, bf16[192,256]{1,0:T(8,128)(2,1)S(1)}, u32[]{:S(2)}, u32[]{:S(2)}) collective-permute-start(bf16[192,256]{1,0:T(8,128)(2,1)S(1)} %get-tuple-element.58), channel_id=1, source_target_pairs={{0,1},{1,0},{2,3},{3,2},{4,5},{5,4},{6,7},{7,6},{8,9},{9,8},{10,11... | collective-permute-start | bytes 294920 | tf_op jit(solution)/shard_map/ppermute | solution.py:91
  68.5 10.1 %collective-permute-start.16 = (bf16[192,256]{1,0:T(8,128)(2,1)S(1)}, bf16[192,256]{1,0:T(8,128)(2,1)S(1)}, u32[]{:S(2)}, u32[]{:S(2)}) collective-permute-start(bf16[192,256]{1,0:T(8,128)(2,1)S(1)} %get-tuple-element.59), channel_id=1, source_target_pairs={{0,2},{1,3},{2,0},{3,1},{4,6},{5,7},{6,4},{7,5},{8,10},{9,11},{10,... | collective-permute-start | bytes 294920 | tf_op jit(solution)/shard_map/ppermute | solution.py:91
  68.8 17.4 %collective-permute-start.17 = (bf16[192,256]{1,0:T(8,128)(2,1)S(1)}, bf16[192,256]{1,0:T(8,128)(2,1)S(1)}, u32[]{:S(2)}, u32[]{:S(2)}) collective-permute-start(bf16[192,256]{1,0:T(8,128)(2,1)S(1)} %get-tuple-element.60), channel_id=1, source_target_pairs={{0,3},{1,2},{2,1},{3,0},{4,7},{5,6},{6,5},{7,4},{8,11},{9,10},{10,... | collective-permute-start | bytes 294920 | tf_op jit(solution)/shard_map/ppermute | solution.py:91
  70.1 18.0 %collective-permute-start.13 = (bf16[192,384]{1,0:T(8,128)(2,1)S(1)}, bf16[192,384]{1,0:T(8,128)(2,1)S(1)}, u32[]{:S(2)}, u32[]{:S(2)}) collective-permute-start(bf16[192,384]{1,0:T(8,128)(2,1)S(1)} %get-tuple-element.55), channel_id=1, source_target_pairs={{0,2},{1,3},{2,0},{3,1},{4,6},{5,7},{6,4},{7,5},{8,10},{9,11},{10,... | collective-permute-start | bytes 442376 | tf_op jit(solution)/shard_map/ppermute | solution.py:91
  72.9 1.0 copy-start.6
  77.1 21.7 %collective-permute-start.14 = (bf16[192,384]{1,0:T(8,128)(2,1)S(1)}, bf16[192,384]{1,0:T(8,128)(2,1)S(1)}, u32[]{:S(2)}, u32[]{:S(2)}) collective-permute-start(bf16[192,384]{1,0:T(8,128)(2,1)S(1)} %get-tuple-element.56), channel_id=1, source_target_pairs={{0,3},{1,2},{2,1},{3,0},{4,7},{5,6},{6,5},{7,4},{8,11},{9,10},{10,... | collective-permute-start | bytes 442376 | tf_op jit(solution)/shard_map/ppermute | solution.py:91
  78.7 21.0 %collective-permute-start.6 = (bf16[192,384]{1,0:T(8,128)(2,1)S(1)}, bf16[192,384]{1,0:T(8,128)(2,1)S(1)}, u32[]{:S(2)}, u32[]{:S(2)}) collective-permute-start(bf16[192,384]{1,0:T(8,128)(2,1)S(1)} %get-tuple-element.46), channel_id=1, source_target_pairs={{0,1},{1,0},{2,3},{3,2},{4,5},{5,4},{6,7},{7,6},{8,9},{9,8},{10,11... | collective-permute-start | bytes 442376 | tf_op jit(solution)/shard_map/ppermute | solution.py:91
  86.2 13.9 %collective-permute-start.7 = (bf16[192,384]{1,0:T(8,128)(2,1)S(1)}, bf16[192,384]{1,0:T(8,128)(2,1)S(1)}, u32[]{:S(2)}, u32[]{:S(2)}) collective-permute-start(bf16[192,384]{1,0:T(8,128)(2,1)S(1)} %get-tuple-element.47), channel_id=1, source_target_pairs={{0,2},{1,3},{2,0},{3,1},{4,6},{5,7},{6,4},{7,5},{8,10},{9,11},{10,... | collective-permute-start | bytes 442376 | tf_op jit(solution)/shard_map/ppermute | solution.py:91
  86.2 18.1 %collective-permute-start.8 = (bf16[192,384]{1,0:T(8,128)(2,1)S(1)}, bf16[192,384]{1,0:T(8,128)(2,1)S(1)}, u32[]{:S(2)}, u32[]{:S(2)}) collective-permute-start(bf16[192,384]{1,0:T(8,128)(2,1)S(1)} %get-tuple-element.48), channel_id=1, source_target_pairs={{0,3},{1,2},{2,1},{3,0},{4,7},{5,6},{6,5},{7,4},{8,11},{9,10},{10,... | collective-permute-start | bytes 442376 | tf_op jit(solution)/shard_map/ppermute | solution.py:91

commit v2 on v1

v2 whole, which is shorter than its diff:
```python
import functools
import math

import jax
import jax.numpy as jnp
from jax import lax
from jax.experimental import pallas as pl
from jax.experimental.pallas import tpu as pltpu
from jax.sharding import PartitionSpec as P

Q_HEADS = 32
KV_HEADS = 4
HEAD_DIM = 128
BLOCK = 128
VMEM_LIMIT = 40 * 1024 * 1024
SHARES = [[4], [4]]
SWAPS = 2
D1 = False
PIN_OTHER = True
PIN_PACK = ()
D3 = (1,)
PIN_SENT = ()
PIN_OLD = ()
STACK_IN = ()
STACK_OUT = (0,)
CUT_LIMIT = 66 * 1024 * 1000
ANY = pl.BlockSpec(memory_space=pl.ANY)
HBM = pl.BlockSpec(memory_space=pltpu.HBM)
VMEM = pl.BlockSpec(memory_space=pltpu.VMEM)


def params(limit=VMEM_LIMIT):
    return pltpu.CompilerParams(vmem_limit_bytes=limit)


def cost(flops, moved, exps=0):
    return pl.CostEstimate(flops=int(flops), bytes_accessed=int(moved), transcendentals=int(exps))


def head_chunks(heads_dev):
    pieces, start = [], 0
    for piece in SHARES:
        chunks = []
        for share in piece:
            size = min(max(1, share * heads_dev // 8), heads_dev - start)
            if size:
                chunks.append((start, size))
                start += size
        if chunks:
            pieces.append(chunks)
    return pieces


def cut_kernel(piece, ctx_size, with_kv, stacked, waits, q_ref, kv_ref, *refs):
    outs, sem = refs[waits:-1], refs[-1]
    me = lax.axis_index("ctx")
    heads_dev = Q_HEADS // ctx_size
    group = Q_HEADS // KV_HEADS
    copies = []
    for step in list(range(1, ctx_size)) + [0]:
        owner = step if stacked else me ^ step
        out = outs[0].at[step] if stacked else outs[step]
        parts = [(q_ref, owner * heads_dev + piece[0][0], sum([chunk[1] for chunk in piece]))]
        if with_kv:
            head = (owner * heads_dev) // group
            first = piece[0][1]
            parts = [
                (q_ref, owner * heads_dev + piece[0][0], first),
                (kv_ref, head, 1),
                (kv_ref, KV_HEADS + head, 1),
                (q_ref, owner * heads_dev + piece[0][0] + first, parts[0][2] - first),
            ]
        place = 0
        for source, block, number in parts:
            if number:
                wide = number * HEAD_DIM
                column = pl.multiple_of(block * HEAD_DIM, HEAD_DIM)
                copies.append(
                    (source.at[:, pl.ds(column, wide)], out.at[:, pl.ds(place, wide)])
                )
                place += wide
    started = [pltpu.make_async_copy(a, b, sem.at[i]) for i, (a, b) in enumerate(copies)]
    for copy in started:
        copy.start()
    for copy in started:
        copy.wait()


def cut(q_src, kv_src, piece, ctx_size, with_kv, stacked, after, limit):
    rows = q_src.shape[0]
    wide = (sum([chunk[1] for chunk in piece]) + (2 if with_kv else 0)) * HEAD_DIM
    if stacked:
        shapes = [jax.ShapeDtypeStruct((ctx_size, rows, wide), jnp.bfloat16)]
    else:
        shapes = [jax.ShapeDtypeStruct((rows, wide), jnp.bfloat16)] * ctx_size
    number = ctx_size * ((4 if len(piece) > 1 else 3) if with_kv else 1)
    outs = pl.pallas_call(
        functools.partial(cut_kernel, piece, ctx_size, with_kv, stacked, len(after)),
        out_shape=shapes,
        in_specs=[ANY] * (2 + len(after)),
        out_specs=[VMEM] * len(shapes),
        scratch_shapes=[pltpu.SemaphoreType.DMA((number,))],
        compiler_params=params(limit),
        cost_estimate=cost(0, 4 * ctx_size * rows * wide),
    )(q_src, kv_src, *after)
    return list(outs)


def swap(blocks, axis, size, unit=1):
    return [blocks[0]] + [
        lax.ppermute(blocks[step], axis, [(j, j ^ (step * unit)) for j in range(size)])
        for step in range(1, len(blocks))
    ]


def exchange(blocks, ctx_size):
    if len(blocks) == 1:
        return [lax.all_to_all(blocks[0], "ctx", split_axis=0, concat_axis=0, tiled=True)]
    return swap(blocks, "ctx", ctx_size)


def plan_kernel(capacity, ctx_size, route_ref, target_ref, swapped_ref, slot_ref, live_ref):
    dp_size, length = route_ref.shape
    rows = length // ctx_size
    pack_len = dp_size * capacity
    own, me = lax.axis_index("dp"), lax.axis_index("ctx")
    mine = route_ref[pl.ds(own, 1), :]
    seq = lax.broadcasted_iota(jnp.int32, (dp_size, length), 0)
    onehot = jnp.where(mine == seq, 1.0, 0.0)
    earlier = lax.broadcasted_iota(jnp.int32, (length, length), 0)
    later = lax.broadcasted_iota(jnp.int32, (length, length), 1)
    strict = jnp.where(earlier < later, 1.0, 0.0).astype(jnp.bfloat16)
    before = jnp.dot(onehot.astype(jnp.bfloat16), strict, preferred_element_type=jnp.float32)
    rank = jnp.sum(before * onehot, axis=0, keepdims=True).astype(jnp.int32)
    other = mine ^ own
    place = (other & 1) * (dp_size // 2) + (other >> 1)
    target_ref[...] = place * capacity + rank
    for step in range(ctx_size):
        source = me ^ step
        swapped_ref[:, pl.ds(step * rows, rows)] = target_ref[
            :, pl.ds(pl.multiple_of(source * rows, rows), rows)
        ]
    incoming = jnp.sum(
        jnp.where(route_ref[...] == own, 1.0, 0.0), axis=1, keepdims=True
    )
    group = lax.broadcasted_iota(jnp.int32, (dp_size, pack_len), 0)
    lane = lax.broadcasted_iota(jnp.int32, (dp_size, pack_len), 1)
    block = lax.div(lane, capacity)
    source = block ^ own
    start = jnp.sum(jnp.where(group < source, incoming, 0.0), axis=0, keepdims=True)
    amount = jnp.sum(jnp.where(group == source, incoming, 0.0), axis=0, keepdims=True)
    offset = (lane - block * capacity)[:1]
    slot_ref[...] = jnp.where(
        offset < amount.astype(jnp.int32), start.astype(jnp.int32) + offset, -1
    )
    live = jnp.sum(incoming, axis=0, keepdims=True).astype(jnp.int32)
    live_ref[...] = jnp.broadcast_to(live, live_ref.shape)


def plan(route, dp_size, ctx_size, capacity):
    length = route.shape[0] // dp_size
    return pl.pallas_call(
        functools.partial(plan_kernel, capacity, ctx_size),
        out_shape=[
            jax.ShapeDtypeStruct((1, length), jnp.int32),
            jax.ShapeDtypeStruct((1, length), jnp.int32),
            jax.ShapeDtypeStruct((1, dp_size * capacity), jnp.int32),
            jax.ShapeDtypeStruct((1, HEAD_DIM), jnp.int32),
        ],
        compiler_params=params(),
        cost_estimate=cost(2 * dp_size * length * length, 8 * length * dp_size),
    )(route.reshape(dp_size, length))


def rows_of(blocks):
    parts = [b[...] for b in blocks]
    if len(parts) == 1 and parts[0].ndim == 3:
        return parts[0].reshape(-1, parts[0].shape[-1])
    return jnp.concatenate(parts, axis=0)


def place_rows(target_ref, data, begin, count):
    row = begin + lax.broadcasted_iota(jnp.int32, (count, target_ref.shape[1]), 0)
    place = jnp.where(target_ref[...] == row, 1.0, 0.0).astype(jnp.bfloat16)
    return jnp.dot(place, data, preferred_element_type=jnp.float32).astype(jnp.bfloat16)


def pack_other_kernel(number, target_ref, *refs):
    outs = refs[-SWAPS:]
    size = outs[0].shape[0]
    half = size * SWAPS
    packed = place_rows(target_ref, rows_of(refs[:number]), half, half)
    for at, out in enumerate(outs):
        out[...] = packed[at * size : (at + 1) * size]


def pack_own_kernel(number, waits, target_ref, *refs):
    got, refs = refs[:SWAPS], refs[SWAPS:]
    blocks, outs = refs[:number], refs[number + waits :]
    size = got[0].shape[0]
    half = size * SWAPS
    capacity = outs[0].shape[0] // 2
    steps = half // capacity
    packed = place_rows(target_ref, rows_of(blocks), 0, half)
    column = 0
    for first in range(0, len(outs), steps):
        wide = outs[first].shape[1]
        for step in range(steps):
            rows = slice(step * capacity, (step + 1) * capacity)
            outs[first + step][:capacity, :] = packed[rows, column : column + wide]
            begin = step * capacity % size
            part = got[step * capacity // size]
            outs[first + step][capacity:, :] = part[begin : begin + capacity, column : column + wide]
        column += wide


def deliver(target, blocks, widths, dp_size, capacity, after, later):
    wide = blocks[0].shape[-1]
    length = target.shape[1]
    half = dp_size // 2 * capacity
    estimate = cost(2 * half * length * wide, 2 * (half + length) * wide)
    other = pl.pallas_call(
        functools.partial(pack_other_kernel, len(blocks)),
        out_shape=[jax.ShapeDtypeStruct((half // SWAPS, wide), jnp.bfloat16)] * SWAPS,
        in_specs=[VMEM] * (1 + len(blocks)) + [ANY] * len(after),
        compiler_params=params(),
        cost_estimate=estimate,
    )(target, *blocks, *after)
    got = [lax.ppermute(part, "dp", [(j, j ^ 1) for j in range(dp_size)]) for part in other]
    outs = pl.pallas_call(
        functools.partial(pack_own_kernel, len(blocks), len(later)),
        out_shape=[
            jax.ShapeDtypeStruct((2 * capacity, part), jnp.bfloat16)
            for part in widths
            for _ in range(dp_size // 2)
        ],
        in_specs=[VMEM] * (1 + SWAPS + len(blocks)) + [ANY] * len(later),
        compiler_params=params(),
        cost_estimate=estimate,
    )(target, *got, *blocks, *later)
    steps = dp_size // 2
    return [
        swap(list(outs[first : first + steps]), "dp", dp_size, 2)
        for first in range(0, len(outs), steps)
    ]


def attend_kernel(
    heads, doc_most, ctx_size, number, waits, with_kv, stacked, *refs
):
    slot_ref, live_ref, doc_ref, col_ref = refs[:4]
    blocks, refs = refs[4 : 4 + number], refs[4 + number + waits :]
    if with_kv:
        outs, kv_ref, acc = refs[:-2], refs[-2], refs[-1]
    else:
        kv_ref, outs, acc = refs[0], refs[1:-1], refs[-1]
    me = lax.axis_index("ctx")
    pack_len = acc.shape[0]
    wide = heads * HEAD_DIM
    scale = HEAD_DIM ** (-0.5) * math.log2(math.e)
    window = min(pack_len, doc_most + BLOCK)
    row = lax.broadcasted_iota(jnp.int32, (BLOCK, pack_len), 0)
    slot = slot_ref[...]
    live = live_ref[...]
    ones = jnp.ones((window, HEAD_DIM), jnp.bfloat16)
    received = jnp.concatenate([b[...] for b in blocks], axis=0)
    for block in range(pack_len // BLOCK):
        begin = block * BLOCK
        rows = pl.ds(begin, BLOCK)
        place = jnp.where(slot == row + begin, 1.0, 0.0).astype(jnp.bfloat16)
        packed = jnp.dot(place, received, preferred_element_type=jnp.float32).astype(jnp.bfloat16)
        if with_kv:
            kv_ref[rows, :] = packed[:, wide:]
        key_start = max(0, begin + BLOCK - window)
        span = begin + BLOCK - key_start
        keys = kv_ref[pl.ds(key_start, span), :HEAD_DIM]
        values = jnp.concatenate([kv_ref[pl.ds(key_start, span), HEAD_DIM:], ones[:span]], axis=1)
        query_pos = begin + lax.broadcasted_iota(jnp.int32, (BLOCK, span), 0)
        key_pos = key_start + lax.broadcasted_iota(jnp.int32, (BLOCK, span), 1)
        docs = jnp.concatenate([col_ref[rows, :]] * (span // HEAD_DIM), axis=1)
        allowed = (docs == doc_ref[:, pl.ds(key_start, span)]) & (key_pos <= query_pos)
        alive = begin + lax.broadcasted_iota(jnp.int32, (BLOCK, HEAD_DIM), 0) < live
        for head in range(heads):
            query = packed[:, head * HEAD_DIM : (head + 1) * HEAD_DIM]
            scores = lax.dot_general(
                query, keys, (((1,), (1,)), ((), ())), preferred_element_type=jnp.float32
            )
            masked = jnp.where(allowed, scores, -1e30)
            top = jnp.max(masked, axis=1, keepdims=True)
            weights = jnp.exp2((masked - top) * scale).astype(jnp.bfloat16)
            mixed = jnp.dot(weights, values, preferred_element_type=jnp.float32)
            result = mixed[:, :HEAD_DIM] / mixed[:, HEAD_DIM:]
            acc[rows, head * HEAD_DIM : (head + 1) * HEAD_DIM] = jnp.where(
                alive, result, 0.0
            ).astype(jnp.bfloat16)
    part = pack_len // ctx_size
    if stacked:
        outs[0][...] = acc[...].reshape(ctx_size, part, wide)
        return
    for step in range(ctx_size):
        first = pl.multiple_of((me ^ step) * part, part)
        outs[step][...] = acc[pl.ds(first, part), :]


def attend(received, slot, live, doc_row, doc_col, kv, heads, ctx_size, stacked, after):
    pack_len = slot.shape[1]
    doc_most = pack_len // 3
    wide = heads * HEAD_DIM
    with_kv = kv is None
    part = pack_len // ctx_size
    if stacked:
        shapes = [jax.ShapeDtypeStruct((ctx_size, part, wide), jnp.bfloat16)]
    else:
        shapes = [jax.ShapeDtypeStruct((part, wide), jnp.bfloat16)] * ctx_size
    sent = len(shapes)
    if with_kv:
        shapes = shapes + [jax.ShapeDtypeStruct((pack_len, 2 * HEAD_DIM), jnp.bfloat16)]
    work = pack_len * (doc_most + BLOCK) * heads
    outs = pl.pallas_call(
        functools.partial(
            attend_kernel,
            heads,
            doc_most,
            ctx_size,
            len(received),
            len(after),
            with_kv,
            stacked,
        ),
        out_shape=shapes,
        in_specs=[VMEM] * (4 + len(received)) + [ANY] * len(after) + [VMEM] * (0 if with_kv else 1),
        scratch_shapes=[pltpu.VMEM((pack_len, wide), jnp.bfloat16)],
        compiler_params=params(),
        cost_estimate=cost(
            2 * pack_len * pack_len * received[0].shape[1] + 6 * work * HEAD_DIM,
            8 * pack_len * wide,
            work,
        ),
    )(slot, live, doc_row, doc_col, *received, *after, *([] if with_kv else [kv]))
    return list(outs[:sent]), (outs[sent] if with_kv else kv)


def join_kernel(chunk, ctx_size, number, *refs):
    offset, heads = chunk
    heads_dev = Q_HEADS // ctx_size
    blocks = refs[:number]
    out, sem = refs[-2:]
    me = lax.axis_index("ctx")
    copies = []
    for step in range(ctx_size):
        source = step if number == 1 else me ^ step
        block = blocks[0].at[step] if number == 1 else blocks[step]
        column = pl.multiple_of((source * heads_dev + offset) * HEAD_DIM, HEAD_DIM)
        copies.append(
            pltpu.make_async_copy(
                block, out.at[:, pl.ds(column, heads * HEAD_DIM)], sem.at[step]
            )
        )
    for copy in copies:
        copy.start()
    for copy in copies:
        copy.wait()


def join(blocks, chunk, out, ctx_size):
    rows = blocks[0].shape[-2]
    given = [] if out is None else [out]
    number = len(blocks)
    return pl.pallas_call(
        functools.partial(join_kernel, chunk, ctx_size, number),
        out_shape=jax.ShapeDtypeStruct((rows, Q_HEADS * HEAD_DIM), jnp.bfloat16),
        in_specs=[ANY] * (number + len(given)),
        out_specs=ANY,
        scratch_shapes=[pltpu.SemaphoreType.DMA((ctx_size,))],
        input_output_aliases={number: 0} if given else {},
        compiler_params=params(),
        cost_estimate=cost(0, 4 * rows * chunk[1] * HEAD_DIM * ctx_size),
    )(*blocks, *given)


def on_device(q_src, kv_src, route, doc_ids):
    ctx_size = lax.axis_size("ctx")
    dp_size = lax.axis_size("dp")
    length = q_src.shape[0] * ctx_size
    capacity = 3 * length // (2 * dp_size)
    pack_len = dp_size * capacity
    pieces = head_chunks(Q_HEADS // ctx_size)

    gathered, after = [], []
    for at, piece in enumerate(pieces):
        limit = VMEM_LIMIT if at else CUT_LIMIT
        blocks = cut(q_src, kv_src, piece, ctx_size, at == 0, at in STACK_IN, after, limit)
        gathered.append(exchange(blocks, ctx_size))
        after = (gathered[-1] * 2)[1:2] if D1 else blocks[:1]
    target, swapped, slot, live = plan(route, dp_size, ctx_size, capacity)
    doc_col = jnp.broadcast_to(doc_ids.reshape(pack_len, 1), (pack_len, HEAD_DIM))

    received, after = [], []
    for at, blocks in enumerate(gathered):
        widths = [chunk[1] * HEAD_DIM for chunk in pieces[at]]
        widths[0] += 0 if at else 2 * HEAD_DIM
        first = (gathered[at + 1] * 2)[1:2] if PIN_OTHER and at + 1 < len(gathered) else []
        received.append(deliver(target if at in STACK_IN else swapped, blocks, widths, dp_size, capacity, after + first, []))
        after = [received[-1][0][i] for i in PIN_PACK]

    kv, out, sends = None, None, []
    chunks = [chunk for piece in pieces for chunk in piece]
    packed = [blocks for piece in received for blocks in piece]
    for at, chunk in enumerate(chunks):
        after = [packed[i][0] for i in D3 if at == 0 and i < len(packed)]
        if at:
            after = after + kept[:1]
            after = after + [sends[at - 1][i % len(sends[at - 1])] for i in PIN_SENT]
        if at > 1:
            after = after + [sends[at - 2][i % len(sends[at - 2])] for i in PIN_OLD]
        kept, kv = attend(
            packed[at], slot, live, doc_ids, doc_col, kv, chunk[1], ctx_size, at in STACK_OUT, after
        )
        sends.append(exchange(kept, ctx_size))
    for chunk, blocks in zip(chunks, sends):
        out = join(blocks, chunk, out, ctx_size)
    return out


def solution(mesh):
    in_specs = (P(("dp", "ctx"), None), P(("dp", "ctx"), None), P(), P("dp", None))
    out_specs = P(("dp", "ctx"), None)
    return jax.shard_map(
        on_device, mesh=mesh, in_specs=in_specs, out_specs=out_specs, check_vma=False
    )
```

time: 106 us -> 90 us (0.85)
  waiting for transfers between devices: 50.4 us -> 41.4 us
  starting transfers between devices: 31.9 us -> 24.3 us
  Pallas kernels: 17.4 us -> 15.7 us
  local copies, waits for them, and re-layouts: 3.86 us -> 5.51 us
    ppermute x18 -> x19, waiting for transfers between devices: 50.4 us -> 38.3 us  [the longest x15 36 us: swap(): lax.ppermute(blocks[step], axis, [(j, j ^ step * unit) for j in range(siz...]
    all_to_all x3 -> x1, starting transfers between devices: 12.8 us -> 6.06 us  [exchange(): lax.all_to_all(blocks[0], 'ctx', split_axis=0, concat_axis=0, tiled=True)]
    all_to_all x3 -> x1, waiting for transfers between devices: 0.01 us -> 3.09 us  [exchange(): lax.all_to_all(blocks[0], 'ctx', split_axis=0, concat_axis=0, tiled=True)]
    unnamed x15 -> x23, local copies, waits for them, and re-layouts: 3.7 us -> 5.35 us
    pallas_call x8, Pallas kernels: 7.16 us -> 5.78 us  [the longest x2 2.29 us: cut(): pl.pallas_call(functools.partial(cut_kernel, piece, ctx_size, with_kv, st...]
    pallas_call x3 -> x2, Pallas kernels: 10 us -> 9.15 us  [attend(): pl.pallas_call(functools.partial(attend_kernel, heads, doc_most, ctx_size...]
    ppermute x18 -> x19, starting transfers between devices: 19.1 us -> 18.2 us  [the longest x15 17.1 us: swap(): lax.ppermute(blocks[step], axis, [(j, j ^ step * unit) for j in range(siz...]
  transfers between devices with their start and end apart: 21 -> 20, of which waited for: 13 -> 16; matrix products, arithmetic and copies ran while one was open for 2% -> 2% of each run, Pallas kernels for 14% -> 8%
where the time goes in v2:
time: 90 us; the launch traced here: 88.4 us
  waiting for transfers between devices  41.4 us (46%)
  starting transfers between devices  24.3 us (27%)
  Pallas kernels  15.7 us (17%)
  local copies, waits for them, and re-layouts  5.51 us (6%)
  other arithmetic  1.39 us (2%)
    ppermute x15, waiting for transfers between devices, swap(): lax.ppermute(blocks[step], axis, [(j, j ^ step * unit) for j in range(siz...  36 us
    ppermute x15, starting transfers between devices, swap(): lax.ppermute(blocks[step], axis, [(j, j ^ step * unit) for j in range(siz...  17.1 us
    pallas_call x2, Pallas kernels, attend(): pl.pallas_call(functools.partial(attend_kernel, heads, doc_most, ctx_size...  9.15 us
    all_to_all x1, starting transfers between devices, exchange(): lax.all_to_all(blocks[0], 'ctx', split_axis=0, concat_axis=0, tiled=True)  6.06 us
    unnamed x23, local copies, waits for them, and re-layouts  5.35 us
    all_to_all x1, waiting for transfers between devices, exchange(): lax.all_to_all(blocks[0], 'ctx', split_axis=0, concat_axis=0, tiled=True)  3.09 us
    pallas_call x2, Pallas kernels, cut(): pl.pallas_call(functools.partial(cut_kernel, piece, ctx_size, with_kv, st...  2.29 us
    ppermute x4, waiting for transfers between devices, deliver(): lax.ppermute(part, 'dp', [(j, j ^ 1) for j in range(dp_size)])  2.28 us
  transfers between devices with their start and end apart: 20, of which 16 were waited for; matrix products, arithmetic and copies ran while one was open for 2% of the time, Pallas kernels for 8%

profile of v2, /device:TPU:18, one launch (start us, length us, event | category | flops | bytes accessed | tf_op | source)
XLA Modules:
  0.0 88.4 jit_solution(2251870771933870000)
XLA Ops:
  0.0 2.2 %shard_map.47 = (bf16[128,768]{1,0:T(8,128)(2,1)}, bf16[128,768]{1,0:T(8,128)(2,1)}, bf16[128,768]{1,0:T(8,128)(2,1)}, bf16[128,768]{1,0:T(8,128)(2,1)}) custom-call(bf16[128,4096]{1,0:T(8,128)(2,1)} %q_ref.3, bf16[128,1024]{1,0:T(8,128)(2,1)} %kv_ref.3), custom_call_target="tpu_custom_call" | custom-call | bytes 1572864 | tf_op jit(solution)/shard_map/pallas_call | solution.py:97
  2.2 1.6 %collective-permute-start.8 = (bf16[128,768]{1,0:T(8,128)(2,1)}, bf16[128,768]{1,0:T(8,128)(2,1)S(1)}, u32[]{:S(2)}, u32[]{:S(2)}) collective-permute-start(bf16[128,768]{1,0:T(8,128)(2,1)} %get-tuple-element.48), channel_id=1, source_target_pairs={{0,1},{1,0},{2,3},{3,2},{4,5},{5,4},{6,7},{7,6},{8,9},{9,8},{10,11... | collective-permute-start | bytes 589832 | tf_op jit(solution)/shard_map/ppermute | solution.py:111
  4.2 1.6 %collective-permute-start.10 = (bf16[128,768]{1,0:T(8,128)(2,1)}, bf16[128,768]{1,0:T(8,128)(2,1)S(1)}, u32[]{:S(2)}, u32[]{:S(2)}) collective-permute-start(bf16[128,768]{1,0:T(8,128)(2,1)} %get-tuple-element.50), channel_id=1, source_target_pairs={{0,3},{1,2},{2,1},{3,0},{4,7},{5,6},{6,5},{7,4},{8,11},{9,10},{10,... | collective-permute-start | bytes 589832 | tf_op jit(solution)/shard_map/ppermute | solution.py:111
  5.7 1.2 %copy-done = bf16[128,4096]{1,0:T(8,128)(2,1)S(1)} copy-done((bf16[128,4096]{1,0:T(8,128)(2,1)S(1)}, bf16[128,4096]{1,0:T(8,128)(2,1)}, u32[]{:S(2)}) %copy-start) | copy-done | bytes 1048600
  7.0 0.9 %copy-done.1 = bf16[128,1024]{1,0:T(8,128)(2,1)S(1)} copy-done((bf16[128,1024]{1,0:T(8,128)(2,1)S(1)}, bf16[128,1024]{1,0:T(8,128)(2,1)}, u32[]{:S(2)}) %copy-start.1) | copy-done | bytes 262168
  7.9 0.9 %copy-done.2 = bf16[128,768]{1,0:T(8,128)(2,1)S(1)} copy-done((bf16[128,768]{1,0:T(8,128)(2,1)S(1)}, bf16[128,768]{1,0:T(8,128)(2,1)}, u32[]{:S(2)}) %copy-start.2) | copy-done | bytes 196632
  9.0 2.5 %collective-permute-start = (bf16[128,512]{1,0:T(8,128)(2,1)S(1)}, bf16[128,512]{1,0:T(8,128)(2,1)S(1)}, u32[]{:S(2)}, u32[]{:S(2)}) collective-permute-start(bf16[128,512]{1,0:T(8,128)(2,1)S(1)} %get-tuple-element.39), channel_id=1, source_target_pairs={{0,1},{1,0},{2,3},{3,2},{4,5},{5,4},{6,7},{7,6},{8,9},{9,8},{10,11... | collective-permute-start | bytes 393224 | tf_op jit(solution)/shard_map/ppermute | solution.py:111
  12.1 1.4 %reduce.4 = s32[4096]{0:T(1024)S(1)} reduce(s32[4096,1]{0,1:T(1,128)} %param.6, s32[]{:T(128)} %broadcast.4), dimensions={1}, to_apply=%param.6.reduce_sub_computation.3 | reduce | bytes 32772 | tf_op args[2]
  14.2 6.1 %collective-permute-done.refs_1_.refs_3_.refs_4_ = bf16[128,512]{1,0:T(8,128)(2,1)S(1)} collective-permute-done((bf16[128,512]{1,0:T(8,128)(2,1)S(1)}, bf16[128,512]{1,0:T(8,128)(2,1)S(1)}, u32[]{:S(2)}, u32[]{:S(2)}) %collective-permute-start) | collective-permute-done | bytes 131104 | tf_op jit(solution)/shard_map/ppermute | solution.py:111
  20.4 2.6 %collective-permute-done.10.refs_3_.refs_5_ = bf16[128,768]{1,0:T(8,128)(2,1)S(1)} collective-permute-done((bf16[128,768]{1,0:T(8,128)(2,1)}, bf16[128,768]{1,0:T(8,128)(2,1)S(1)}, u32[]{:S(2)}, u32[]{:S(2)}) %collective-permute-start.10) | collective-permute-done | bytes 196640 | tf_op jit(solution)/shard_map/ppermute | solution.py:111
  26.7 1.5 %collective-permute-start.14 = (bf16[192,768]{1,0:T(8,128)(2,1)S(1)}, bf16[192,768]{1,0:T(8,128)(2,1)S(1)}, u32[]{:S(2)}, u32[]{:S(2)}) collective-permute-start(bf16[192,768]{1,0:T(8,128)(2,1)S(1)} %get-tuple-element.55), channel_id=1, source_target_pairs={{0,16},{4,20},{8,24},{12,28},{16,0},{20,4},{24,8},{28,12},{1,17},{... | collective-permute-start | bytes 884744 | tf_op jit(solution)/shard_map/ppermute | solution.py:111
  28.2 1.4 %collective-permute-start.15 = (bf16[192,768]{1,0:T(8,128)(2,1)S(1)}, bf16[192,768]{1,0:T(8,128)(2,1)S(1)}, u32[]{:S(2)}, u32[]{:S(2)}) collective-permute-start(bf16[192,768]{1,0:T(8,128)(2,1)S(1)} %get-tuple-element.56), channel_id=1, source_target_pairs={{0,24},{4,28},{8,16},{12,20},{16,8},{20,12},{24,0},{28,4},{1,25},{... | collective-permute-start | bytes 884744 | tf_op jit(solution)/shard_map/ppermute | solution.py:111
  29.6 3.9 %collective-permute-done.1.refs_2_.refs_4_ = bf16[128,512]{1,0:T(8,128)(2,1)S(1)} collective-permute-done((bf16[128,512]{1,0:T(8,128)(2,1)S(1)}, bf16[128,512]{1,0:T(8,128)(2,1)S(1)}, u32[]{:S(2)}, u32[]{:S(2)}) %collective-permute-start.1) | collective-permute-done | bytes 131104 | tf_op jit(solution)/shard_map/ppermute | solution.py:111
  33.5 3.1 %collective-permute-done.2.refs_3_.refs_5_ = bf16[128,512]{1,0:T(8,128)(2,1)S(1)} collective-permute-done((bf16[128,512]{1,0:T(8,128)(2,1)S(1)}, bf16[128,512]{1,0:T(8,128)(2,1)S(1)}, u32[]{:S(2)}, u32[]{:S(2)}) %collective-permute-start.2) | collective-permute-done | bytes 131104 | tf_op jit(solution)/shard_map/ppermute | solution.py:111
  37.6 0.9 %collective-permute-done.3.refs_0_ = bf16[192,512]{1,0:T(8,128)(2,1)S(1)} collective-permute-done((bf16[192,512]{1,0:T(8,128)(2,1)S(1)}, bf16[192,512]{1,0:T(8,128)(2,1)S(1)}, u32[]{:S(2)}, u32[]{:S(2)}) %collective-permute-start.3) | collective-permute-done | bytes 196640 | tf_op jit(solution)/shard_map/ppermute | solution.py:229
  39.9 0.9 %collective-permute-done.14.refs_6_ = bf16[192,768]{1,0:T(8,128)(2,1)S(1)} collective-permute-done((bf16[192,768]{1,0:T(8,128)(2,1)S(1)}, bf16[192,768]{1,0:T(8,128)(2,1)S(1)}, u32[]{:S(2)}, u32[]{:S(2)}) %collective-permute-start.14) | collective-permute-done | bytes 294944 | tf_op jit(solution)/shard_map/ppermute | solution.py:111
  40.8 1.6 %collective-permute-done.15.refs_7_ = bf16[192,768]{1,0:T(8,128)(2,1)S(1)} collective-permute-done((bf16[192,768]{1,0:T(8,128)(2,1)S(1)}, bf16[192,768]{1,0:T(8,128)(2,1)S(1)}, u32[]{:S(2)}, u32[]{:S(2)}) %collective-permute-start.15) | collective-permute-done | bytes 294944 | tf_op jit(solution)/shard_map/ppermute | solution.py:111
  42.6 5.5 %shard_map.53 = (bf16[4,192,512]{2,1,0:T(8,128)(2,1)}, bf16[768,256]{1,0:T(8,128)(2,1)S(1)}) custom-call(s32[1,768]{1,0:T(1,128)S(1)} %get-tuple-element.34.refs_0_, s32[1,128]{1,0:T(1,128)S(1)} %get-tuple-element.35.refs_1_, s32[1,768]{1,0:T(1,128)S(1)} %copy-done.4, s32[768,128]{1,0:T(8,128)S(1)} %broadcast_in_dim.8.refs_3_, ...), custom_call_target="tpu_custom_call" | custom-call | flops 1811939328 | bytes 3145728 | tf_op jit(solution)/shard_map/pallas_call | solution.py:319
  48.1 6.1 %all-to-all-start = ((bf16[4,192,512]{2,1,0:T(8,128)(2,1)}), bf16[4,192,512]{2,1,0:T(8,128)(2,1)S(1)}, u32[]{:S(2)}, u32[]{:S(2)}) async-start(bf16[4,192,512]{2,1,0:T(8,128)(2,1)} %get-tuple-element.57.refs_8_), calls=%async_computation | async-start | bytes 1572864 | tf_op jit(solution)/shard_map/all_to_all | solution.py:118
  54.9 1.5 %collective-permute-start.6 = (bf16[192,512]{1,0:T(8,128)(2,1)S(1)}, bf16[192,512]{1,0:T(8,128)(2,1)S(1)}, u32[]{:S(2)}, u32[]{:S(2)}) collective-permute-start(bf16[192,512]{1,0:T(8,128)(2,1)S(1)} %copy-done.6), channel_id=1, source_target_pairs={{0,16},{4,20},{8,24},{12,28},{16,0},{20,4},{24,8},{28,12},{1,17},{... | collective-permute-start | bytes 589832 | tf_op jit(solution)/shard_map/ppermute | solution.py:111
  56.5 1.2 %collective-permute-start.7 = (bf16[192,512]{1,0:T(8,128)(2,1)S(1)}, bf16[192,512]{1,0:T(8,128)(2,1)S(1)}, u32[]{:S(2)}, u32[]{:S(2)}) collective-permute-start(bf16[192,512]{1,0:T(8,128)(2,1)S(1)} %get-tuple-element.47), channel_id=1, source_target_pairs={{0,24},{4,28},{8,16},{12,20},{16,8},{20,12},{24,0},{28,4},{1,25},{... | collective-permute-start | bytes 589832 | tf_op jit(solution)/shard_map/ppermute | solution.py:111
  57.6 3.5 %collective-permute-done.5.refs_5_ = bf16[192,512]{1,0:T(8,128)(2,1)S(1)} collective-permute-done((bf16[192,512]{1,0:T(8,128)(2,1)S(1)}, bf16[192,512]{1,0:T(8,128)(2,1)S(1)}, u32[]{:S(2)}, u32[]{:S(2)}) %collective-permute-start.5) | collective-permute-done | bytes 196640 | tf_op jit(solution)/shard_map/ppermute | solution.py:111
  61.1 2.4 %collective-permute-done.6.refs_6_ = bf16[192,512]{1,0:T(8,128)(2,1)S(1)} collective-permute-done((bf16[192,512]{1,0:T(8,128)(2,1)S(1)}, bf16[192,512]{1,0:T(8,128)(2,1)S(1)}, u32[]{:S(2)}, u32[]{:S(2)}) %collective-permute-start.6) | collective-permute-done | bytes 196640 | tf_op jit(solution)/shard_map/ppermute | solution.py:111
  63.5 1.0 %copy-done.10 = bf16[768,256]{1,0:T(8,128)(2,1)S(1)} copy-done((bf16[768,256]{1,0:T(8,128)(2,1)S(1)}, bf16[768,256]{1,0:T(8,128)(2,1)}, u32[]{:S(2)}) %copy-start.10) | copy-done | bytes 393240
  64.5 3.7 %shard_map.54 = (bf16[192,512]{1,0:T(8,128)(2,1)S(1)}, bf16[192,512]{1,0:T(8,128)(2,1)S(1)}, bf16[192,512]{1,0:T(8,128)(2,1)S(1)}, bf16[192,512]{1,0:T(8,128)(2,1)S(1)}) custom-call(s32[1,768]{1,0:T(1,128)S(1)} %get-tuple-element.34.refs_0_, s32[1,128]{1,0:T(1,128)S(1)} %get-tuple-element.35.refs_1_, s32[1,768]{1,0:T(1,128)S(1)} %copy-done.4, ...), custom_call_target="tpu_custom_call" | custom-call | flops 1509949440 | bytes 3145728 | tf_op jit(solution)/shard_map/pallas_call | solution.py:319
  68.2 1.6 %collective-permute-start.16 = (bf16[192,512]{1,0:T(8,128)(2,1)S(1)}, bf16[192,512]{1,0:T(8,128)(2,1)S(1)}, u32[]{:S(2)}, u32[]{:S(2)}) collective-permute-start(bf16[192,512]{1,0:T(8,128)(2,1)S(1)} %get-tuple-element.60), channel_id=1, source_target_pairs={{0,1},{1,0},{2,3},{3,2},{4,5},{5,4},{6,7},{7,6},{8,9},{9,8},{10,11... | collective-permute-start | bytes 589832 | tf_op jit(solution)/shard_map/ppermute | solution.py:111
  70.3 1.5 %collective-permute-start.18 = (bf16[192,512]{1,0:T(8,128)(2,1)S(1)}, bf16[192,512]{1,0:T(8,128)(2,1)S(1)}, u32[]{:S(2)}, u32[]{:S(2)}) collective-permute-start(bf16[192,512]{1,0:T(8,128)(2,1)S(1)} %get-tuple-element.62), channel_id=1, source_target_pairs={{0,3},{1,2},{2,1},{3,0},{4,7},{5,6},{6,5},{7,4},{8,11},{9,10},{10,... | collective-permute-start | bytes 589832 | tf_op jit(solution)/shard_map/ppermute | solution.py:111
  71.8 3.1 %all-to-all-done.refs_0_ = bf16[4,192,512]{2,1,0:T(8,128)(2,1)S(1)} async-done(((bf16[4,192,512]{2,1,0:T(8,128)(2,1)}), bf16[4,192,512]{2,1,0:T(8,128)(2,1)S(1)}, u32[]{:S(2)}, u32[]{:S(2)}) %all-to-all-start) | async-done | bytes 786464 | tf_op jit(solution)/shard_map/all_to_all | solution.py:118
  75.8 1.0 %collective-permute-done.16.refs_1_ = bf16[192,512]{1,0:T(8,128)(2,1)S(1)} collective-permute-done((bf16[192,512]{1,0:T(8,128)(2,1)S(1)}, bf16[192,512]{1,0:T(8,128)(2,1)S(1)}, u32[]{:S(2)}, u32[]{:S(2)}) %collective-permute-start.16) | collective-permute-done | bytes 196640 | tf_op jit(solution)/shard_map/ppermute | solution.py:111
  76.7 6.7 %collective-permute-done.17.refs_2_ = bf16[192,512]{1,0:T(8,128)(2,1)S(1)} collective-permute-done((bf16[192,512]{1,0:T(8,128)(2,1)S(1)}, bf16[192,512]{1,0:T(8,128)(2,1)S(1)}, u32[]{:S(2)}, u32[]{:S(2)}) %collective-permute-start.17) | collective-permute-done | bytes 196640 | tf_op jit(solution)/shard_map/ppermute | solution.py:111
  83.4 4.1 %collective-permute-done.18.refs_3_ = bf16[192,512]{1,0:T(8,128)(2,1)S(1)} collective-permute-done((bf16[192,512]{1,0:T(8,128)(2,1)S(1)}, bf16[192,512]{1,0:T(8,128)(2,1)S(1)}, u32[]{:S(2)}, u32[]{:S(2)}) %collective-permute-start.18) | collective-permute-done | bytes 196640 | tf_op jit(solution)/shard_map/ppermute | solution.py:111
  87.5 0.9 %shard_map.56 = bf16[192,4096]{1,0:T(8,128)(2,1)} custom-call(bf16[192,512]{1,0:T(8,128)(2,1)S(1)} %get-tuple-element.59.refs_0_, bf16[192,512]{1,0:T(8,128)(2,1)S(1)} %collective-permute-done.16.refs_1_, bf16[192,512]{1,0:T(8,128)(2,1)S(1)} %collective-permute-done.17.refs_2_, ...), custom_call_target="tpu_custom_call", output_to_operand_aliasing={{}: (4, {})} | custom-call | bytes 1572864 | tf_op jit(solution)/shard_map/pallas_call | solution.py:369
  (46 shorter events, 10.1 us)
Async XLA Ops:
  2.2 18.2 %collective-permute-start.8 = (bf16[128,768]{1,0:T(8,128)(2,1)}, bf16[128,768]{1,0:T(8,128)(2,1)S(1)}, u32[]{:S(2)}, u32[]{:S(2)}) collective-permute-start(bf16[128,768]{1,0:T(8,128)(2,1)} %get-tuple-element.48), channel_id=1, source_target_pairs={{0,1},{1,0},{2,3},{3,2},{4,5},{5,4},{6,7},{7,6},{8,9},{9,8},{10,11... | collective-permute-start | bytes 589832 | tf_op jit(solution)/shard_map/ppermute | solution.py:111
  3.8 16.6 %collective-permute-start.9 = (bf16[128,768]{1,0:T(8,128)(2,1)}, bf16[128,768]{1,0:T(8,128)(2,1)S(1)}, u32[]{:S(2)}, u32[]{:S(2)}) collective-permute-start(bf16[128,768]{1,0:T(8,128)(2,1)} %get-tuple-element.49), channel_id=1, source_target_pairs={{0,2},{1,3},{2,0},{3,1},{4,6},{5,7},{6,4},{7,5},{8,10},{9,11},{10,... | collective-permute-start | bytes 589832 | tf_op jit(solution)/shard_map/ppermute | solution.py:111
  4.2 18.8 %collective-permute-start.10 = (bf16[128,768]{1,0:T(8,128)(2,1)}, bf16[128,768]{1,0:T(8,128)(2,1)S(1)}, u32[]{:S(2)}, u32[]{:S(2)}) collective-permute-start(bf16[128,768]{1,0:T(8,128)(2,1)} %get-tuple-element.50), channel_id=1, source_target_pairs={{0,3},{1,2},{2,1},{3,0},{4,7},{5,6},{6,5},{7,4},{8,11},{9,10},{10,... | collective-permute-start | bytes 589832 | tf_op jit(solution)/shard_map/ppermute | solution.py:111
  5.7 1.2 %copy-start = (bf16[128,4096]{1,0:T(8,128)(2,1)S(1)}, bf16[128,4096]{1,0:T(8,128)(2,1)}, u32[]{:S(2)}) copy-start(bf16[128,4096]{1,0:T(8,128)(2,1)} %q_ref.3) | copy-start | bytes 3145732
  7.0 0.9 %copy-start.1 = (bf16[128,1024]{1,0:T(8,128)(2,1)S(1)}, bf16[128,1024]{1,0:T(8,128)(2,1)}, u32[]{:S(2)}) copy-start(bf16[128,1024]{1,0:T(8,128)(2,1)} %kv_ref.3) | copy-start | bytes 786436
  7.9 0.9 %copy-start.2 = (bf16[128,768]{1,0:T(8,128)(2,1)S(1)}, bf16[128,768]{1,0:T(8,128)(2,1)}, u32[]{:S(2)}) copy-start(bf16[128,768]{1,0:T(8,128)(2,1)} %get-tuple-element.37.refs_0_.refs_2_) | copy-start | bytes 589828
  8.8 14.2 %copy-start.3 = (bf16[128,768]{1,0:T(8,128)(2,1)S(1)}, bf16[128,768]{1,0:T(8,128)(2,1)}, u32[]{:S(2)}) copy-start(bf16[128,768]{1,0:T(8,128)(2,1)} %get-tuple-element.37.refs_0_.refs_2_) | copy-start | bytes 589828
  9.0 11.4 %collective-permute-start = (bf16[128,512]{1,0:T(8,128)(2,1)S(1)}, bf16[128,512]{1,0:T(8,128)(2,1)S(1)}, u32[]{:S(2)}, u32[]{:S(2)}) collective-permute-start(bf16[128,512]{1,0:T(8,128)(2,1)S(1)} %get-tuple-element.39), channel_id=1, source_target_pairs={{0,1},{1,0},{2,3},{3,2},{4,5},{5,4},{6,7},{7,6},{8,9},{9,8},{10,11... | collective-permute-start | bytes 393224 | tf_op jit(solution)/shard_map/ppermute | solution.py:111
  23.0 14.6 %copy-start.4 = (s32[1,768]{1,0:T(1,128)S(1)}, s32[1,768]{1,0:T(1,128)}, u32[]{:S(2)}) copy-start(s32[1,768]{1,0:T(1,128)} %refs_2_.3) | copy-start | bytes 9220
  23.5 1.6 %collective-permute-start.11 = (bf16[192,768]{1,0:T(8,128)(2,1)S(1)}, bf16[192,768]{1,0:T(8,128)(2,1)S(1)}, u32[]{:S(2)}, u32[]{:S(2)}) collective-permute-start(bf16[192,768]{1,0:T(8,128)(2,1)S(1)} %get-tuple-element.51), channel_id=1, source_target_pairs={{0,4},{4,0},{8,12},{12,8},{16,20},{20,16},{24,28},{28,24},{1,5},{5... | collective-permute-start | bytes 884744 | tf_op jit(solution)/shard_map/ppermute | solution.py:229
  23.6 2.0 %collective-permute-start.12 = (bf16[192,768]{1,0:T(8,128)(2,1)S(1)}, bf16[192,768]{1,0:T(8,128)(2,1)S(1)}, u32[]{:S(2)}, u32[]{:S(2)}) collective-permute-start(bf16[192,768]{1,0:T(8,128)(2,1)S(1)} %get-tuple-element.52), channel_id=1, source_target_pairs={{0,4},{4,0},{8,12},{12,8},{16,20},{20,16},{24,28},{28,24},{1,5},{5... | collective-permute-start | bytes 884744 | tf_op jit(solution)/shard_map/ppermute | solution.py:229
  24.1 9.5 %collective-permute-start.1 = (bf16[128,512]{1,0:T(8,128)(2,1)S(1)}, bf16[128,512]{1,0:T(8,128)(2,1)S(1)}, u32[]{:S(2)}, u32[]{:S(2)}) collective-permute-start(bf16[128,512]{1,0:T(8,128)(2,1)S(1)} %get-tuple-element.40), channel_id=1, source_target_pairs={{0,2},{1,3},{2,0},{3,1},{4,6},{5,7},{6,4},{7,5},{8,10},{9,11},{10,... | collective-permute-start | bytes 393224 | tf_op jit(solution)/shard_map/ppermute | solution.py:111
  24.1 12.6 %collective-permute-start.2 = (bf16[128,512]{1,0:T(8,128)(2,1)S(1)}, bf16[128,512]{1,0:T(8,128)(2,1)S(1)}, u32[]{:S(2)}, u32[]{:S(2)}) collective-permute-start(bf16[128,512]{1,0:T(8,128)(2,1)S(1)} %get-tuple-element.41), channel_id=1, source_target_pairs={{0,3},{1,2},{2,1},{3,0},{4,7},{5,6},{6,5},{7,4},{8,11},{9,10},{10,... | collective-permute-start | bytes 393224 | tf_op jit(solution)/shard_map/ppermute | solution.py:111
  26.1 13.8 %collective-permute-start.13 = (bf16[192,768]{1,0:T(8,128)(2,1)S(1)}, bf16[192,768]{1,0:T(8,128)(2,1)S(1)}, u32[]{:S(2)}, u32[]{:S(2)}) collective-permute-start(bf16[192,768]{1,0:T(8,128)(2,1)S(1)} %get-tuple-element.54), channel_id=1, source_target_pairs={{0,8},{4,12},{8,0},{12,4},{16,24},{20,28},{24,16},{28,20},{1,9},{5... | collective-permute-start | bytes 884744 | tf_op jit(solution)/shard_map/ppermute | solution.py:111
  26.7 14.2 %collective-permute-start.14 = (bf16[192,768]{1,0:T(8,128)(2,1)S(1)}, bf16[192,768]{1,0:T(8,128)(2,1)S(1)}, u32[]{:S(2)}, u32[]{:S(2)}) collective-permute-start(bf16[192,768]{1,0:T(8,128)(2,1)S(1)} %get-tuple-element.55), channel_id=1, source_target_pairs={{0,16},{4,20},{8,24},{12,28},{16,0},{20,4},{24,8},{28,12},{1,17},{... | collective-permute-start | bytes 884744 | tf_op jit(solution)/shard_map/ppermute | solution.py:111
  28.2 14.3 %collective-permute-start.15 = (bf16[192,768]{1,0:T(8,128)(2,1)S(1)}, bf16[192,768]{1,0:T(8,128)(2,1)S(1)}, u32[]{:S(2)}, u32[]{:S(2)}) collective-permute-start(bf16[192,768]{1,0:T(8,128)(2,1)S(1)} %get-tuple-element.56), channel_id=1, source_target_pairs={{0,24},{4,28},{8,16},{12,20},{16,8},{20,12},{24,0},{28,4},{1,25},{... | collective-permute-start | bytes 884744 | tf_op jit(solution)/shard_map/ppermute | solution.py:111
  37.0 1.5 %collective-permute-start.3 = (bf16[192,512]{1,0:T(8,128)(2,1)S(1)}, bf16[192,512]{1,0:T(8,128)(2,1)S(1)}, u32[]{:S(2)}, u32[]{:S(2)}) collective-permute-start(bf16[192,512]{1,0:T(8,128)(2,1)S(1)} %get-tuple-element.42), channel_id=1, source_target_pairs={{0,4},{4,0},{8,12},{12,8},{16,20},{20,16},{24,28},{28,24},{1,5},{5... | collective-permute-start | bytes 589832 | tf_op jit(solution)/shard_map/ppermute | solution.py:229
  37.1 1.7 %collective-permute-start.4 = (bf16[192,512]{1,0:T(8,128)(2,1)S(1)}, bf16[192,512]{1,0:T(8,128)(2,1)S(1)}, u32[]{:S(2)}, u32[]{:S(2)}) collective-permute-start(bf16[192,512]{1,0:T(8,128)(2,1)S(1)} %get-tuple-element.43), channel_id=1, source_target_pairs={{0,4},{4,0},{8,12},{12,8},{16,20},{20,16},{24,28},{28,24},{1,5},{5... | collective-permute-start | bytes 589832 | tf_op jit(solution)/shard_map/ppermute | solution.py:229
  39.2 0.7 copy-start.5
  39.9 8.2 %copy-start.7 = (bf16[192,512]{1,0:T(8,128)(2,1)}, bf16[192,512]{1,0:T(8,128)(2,1)S(1)}, u32[]{:S(2)}) copy-start(bf16[192,512]{1,0:T(8,128)(2,1)S(1)} %get-tuple-element.45) | copy-start | bytes 589828
  48.1 15.4 %copy-start.9 = (bf16[768,256]{1,0:T(8,128)(2,1)}, bf16[768,256]{1,0:T(8,128)(2,1)S(1)}, u32[]{:S(2)}) copy-start(bf16[768,256]{1,0:T(8,128)(2,1)S(1)} %get-tuple-element.58.refs_9_) | copy-start | bytes 1179652
  48.1 6.9 %copy-start.6 = (bf16[192,512]{1,0:T(8,128)(2,1)S(1)}, bf16[192,512]{1,0:T(8,128)(2,1)}, u32[]{:S(2)}) copy-start(bf16[192,512]{1,0:T(8,128)(2,1)} %copy-done.5) | copy-start | bytes 589828
  48.1 6.1 %copy-start.8 = (bf16[192,512]{1,0:T(8,128)(2,1)S(1)}, bf16[192,512]{1,0:T(8,128)(2,1)}, u32[]{:S(2)}) copy-start(bf16[192,512]{1,0:T(8,128)(2,1)} %copy-done.7) | copy-start | bytes 589828
  48.1 26.8 %all-to-all-start = ((bf16[4,192,512]{2,1,0:T(8,128)(2,1)}), bf16[4,192,512]{2,1,0:T(8,128)(2,1)S(1)}, u32[]{:S(2)}, u32[]{:S(2)}) async-start(bf16[4,192,512]{2,1,0:T(8,128)(2,1)} %get-tuple-element.57.refs_8_), calls=%async_computation | async-start | bytes 1572864 | tf_op jit(solution)/shard_map/all_to_all | solution.py:118
  54.1 7.0 %collective-permute-start.5 = (bf16[192,512]{1,0:T(8,128)(2,1)S(1)}, bf16[192,512]{1,0:T(8,128)(2,1)S(1)}, u32[]{:S(2)}, u32[]{:S(2)}) collective-permute-start(bf16[192,512]{1,0:T(8,128)(2,1)S(1)} %copy-done.8), channel_id=1, source_target_pairs={{0,8},{4,12},{8,0},{12,4},{16,24},{20,28},{24,16},{28,20},{1,9},{5... | collective-permute-start | bytes 589832 | tf_op jit(solution)/shard_map/ppermute | solution.py:111
  54.9 8.6 %collective-permute-start.6 = (bf16[192,512]{1,0:T(8,128)(2,1)S(1)}, bf16[192,512]{1,0:T(8,128)(2,1)S(1)}, u32[]{:S(2)}, u32[]{:S(2)}) collective-permute-start(bf16[192,512]{1,0:T(8,128)(2,1)S(1)} %copy-done.6), channel_id=1, source_target_pairs={{0,16},{4,20},{8,24},{12,28},{16,0},{20,4},{24,8},{28,12},{1,17},{... | collective-permute-start | bytes 589832 | tf_op jit(solution)/shard_map/ppermute | solution.py:111
  56.5 7.1 %collective-permute-start.7 = (bf16[192,512]{1,0:T(8,128)(2,1)S(1)}, bf16[192,512]{1,0:T(8,128)(2,1)S(1)}, u32[]{:S(2)}, u32[]{:S(2)}) collective-permute-start(bf16[192,512]{1,0:T(8,128)(2,1)S(1)} %get-tuple-element.47), channel_id=1, source_target_pairs={{0,24},{4,28},{8,16},{12,20},{16,8},{20,12},{24,0},{28,4},{1,25},{... | collective-permute-start | bytes 589832 | tf_op jit(solution)/shard_map/ppermute | solution.py:111
  63.5 1.0 %copy-start.10 = (bf16[768,256]{1,0:T(8,128)(2,1)S(1)}, bf16[768,256]{1,0:T(8,128)(2,1)}, u32[]{:S(2)}) copy-start(bf16[768,256]{1,0:T(8,128)(2,1)} %copy-done.9) | copy-start | bytes 1179652
  68.2 8.5 %collective-permute-start.16 = (bf16[192,512]{1,0:T(8,128)(2,1)S(1)}, bf16[192,512]{1,0:T(8,128)(2,1)S(1)}, u32[]{:S(2)}, u32[]{:S(2)}) collective-permute-start(bf16[192,512]{1,0:T(8,128)(2,1)S(1)} %get-tuple-element.60), channel_id=1, source_target_pairs={{0,1},{1,0},{2,3},{3,2},{4,5},{5,4},{6,7},{7,6},{8,9},{9,8},{10,11... | collective-permute-start | bytes 589832 | tf_op jit(solution)/shard_map/ppermute | solution.py:111
  69.8 13.6 %collective-permute-start.17 = (bf16[192,512]{1,0:T(8,128)(2,1)S(1)}, bf16[192,512]{1,0:T(8,128)(2,1)S(1)}, u32[]{:S(2)}, u32[]{:S(2)}) collective-permute-start(bf16[192,512]{1,0:T(8,128)(2,1)S(1)} %get-tuple-element.61), channel_id=1, source_target_pairs={{0,2},{1,3},{2,0},{3,1},{4,6},{5,7},{6,4},{7,5},{8,10},{9,11},{10,... | collective-permute-start | bytes 589832 | tf_op jit(solution)/shard_map/ppermute | solution.py:111
  70.3 17.2 %collective-permute-start.18 = (bf16[192,512]{1,0:T(8,128)(2,1)S(1)}, bf16[192,512]{1,0:T(8,128)(2,1)S(1)}, u32[]{:S(2)}, u32[]{:S(2)}) collective-permute-start(bf16[192,512]{1,0:T(8,128)(2,1)S(1)} %get-tuple-element.62), channel_id=1, source_target_pairs={{0,3},{1,2},{2,1},{3,0},{4,7},{5,6},{6,5},{7,4},{8,11},{9,10},{10,... | collective-permute-start | bytes 589832 | tf_op jit(solution)/shard_map/ppermute | solution.py:111

commit v3 on v2

--- a/solution.py
+++ b/solution.py
@@ -15,15 +15,21 @@
 VMEM_LIMIT = 40 * 1024 * 1024
 SHARES = [[4], [4]]
 SWAPS = 2
-D1 = False
-PIN_OTHER = True
-PIN_PACK = ()
+D1 = 0
+PIN_OTHER = (1,)
+PIN_PACK = (0,)
 D3 = (1,)
 PIN_SENT = ()
 PIN_OLD = ()
-STACK_IN = ()
-STACK_OUT = (0,)
-CUT_LIMIT = 66 * 1024 * 1000
+PAIRED = ()
+ORDER_Z = ()
+ORDER_D = ()
+ORDER_AT = (0, 1)
+ORDER_J = (2, 3, 1, 0)
+PIN_HAND = (0,)
+HANDS = 2
+STACK_OUT = ()
+CUT_LIMIT = VMEM_LIMIT
 ANY = pl.BlockSpec(memory_space=pl.ANY)
 HBM = pl.BlockSpec(memory_space=pltpu.HBM)
 VMEM = pl.BlockSpec(memory_space=pltpu.VMEM)
@@ -51,15 +57,16 @@
     return pieces
 
 
-def cut_kernel(piece, ctx_size, with_kv, stacked, waits, q_ref, kv_ref, *refs):
+def cut_kernel(piece, ctx_size, with_kv, paired, waits, q_ref, kv_ref, *refs):
     outs, sem = refs[waits:-1], refs[-1]
     me = lax.axis_index("ctx")
     heads_dev = Q_HEADS // ctx_size
     group = Q_HEADS // KV_HEADS
     copies = []
     for step in list(range(1, ctx_size)) + [0]:
-        owner = step if stacked else me ^ step
-        out = outs[0].at[step] if stacked else outs[step]
+        owner = me ^ step
+        rows = q_ref.shape[0]
+        out = outs[2].at[pl.ds((step - 2) * rows, rows)] if paired and step >= 2 else outs[step]
         parts = [(q_ref, owner * heads_dev + piece[0][0], sum([chunk[1] for chunk in piece]))]
         if with_kv:
             head = (owner * heads_dev) // group
@@ -86,16 +93,15 @@
         copy.wait()
 
 
-def cut(q_src, kv_src, piece, ctx_size, with_kv, stacked, after, limit):
+def cut(q_src, kv_src, piece, ctx_size, with_kv, paired, after, limit):
     rows = q_src.shape[0]
     wide = (sum([chunk[1] for chunk in piece]) + (2 if with_kv else 0)) * HEAD_DIM
-    if stacked:
-        shapes = [jax.ShapeDtypeStruct((ctx_size, rows, wide), jnp.bfloat16)]
-    else:
-        shapes = [jax.ShapeDtypeStruct((rows, wide), jnp.bfloat16)] * ctx_size
+    shapes = [jax.ShapeDtypeStruct((rows, wide), jnp.bfloat16)] * ctx_size
+    if paired:
+        shapes = shapes[:2] + [jax.ShapeDtypeStruct((2 * rows, wide), jnp.bfloat16)]
     number = ctx_size * ((4 if len(piece) > 1 else 3) if with_kv else 1)
     outs = pl.pallas_call(
-        functools.partial(cut_kernel, piece, ctx_size, with_kv, stacked, len(after)),
+        functools.partial(cut_kernel, piece, ctx_size, with_kv, paired, len(after)),
         out_shape=shapes,
         in_specs=[ANY] * (2 + len(after)),
         out_specs=[VMEM] * len(shapes),
@@ -117,6 +123,33 @@
     if len(blocks) == 1:
         return [lax.all_to_all(blocks[0], "ctx", split_axis=0, concat_axis=0, tiled=True)]
     return swap(blocks, "ctx", ctx_size)
+
+
+def in_pairs(blocks, ctx_size):
+    own, near, far = blocks
+    near = lax.ppermute(near, "ctx", [(j, j ^ 1) for j in range(ctx_size)])
+    far = lax.ppermute(far, "ctx", [(j, j ^ 2) for j in range(ctx_size)])
+    return [own, near, far]
+
+
+def hand_on_kernel(far_ref, *refs):
+    outs = refs[-HANDS:]
+    rows = outs[0].shape[0]
+    for at, out in enumerate(outs):
+        begin = far_ref.shape[0] // 2 + at * rows
+        out[...] = far_ref[begin : begin + rows, :]
+
+
+def hand_on(far, after, ctx_size):
+    rows, wide = far.shape[0] // 2, far.shape[1]
+    blocks = pl.pallas_call(
+        hand_on_kernel,
+        out_shape=[jax.ShapeDtypeStruct((rows // HANDS, wide), jnp.bfloat16)] * HANDS,
+        in_specs=[VMEM] + [ANY] * len(after),
+        compiler_params=params(),
+        cost_estimate=cost(0, 4 * rows * wide),
+    )(far, *after)
+    return [lax.ppermute(b, "ctx", [(j, j ^ 1) for j in range(ctx_size)]) for b in blocks]
 
 
 def plan_kernel(capacity, ctx_size, route_ref, target_ref, swapped_ref, slot_ref, live_ref):
@@ -172,11 +205,17 @@
     )(route.reshape(dp_size, length))
 
 
+def mixed_up(blocks, order):
+    return [blocks[at] for at in order] if len(order) == len(blocks) else list(blocks)
+
+
+def restored(refs, order):
+    return [refs[order.index(at)] for at in range(len(refs))] if len(order) == len(refs) else refs
+
+
 def rows_of(blocks):
-    parts = [b[...] for b in blocks]
-    if len(parts) == 1 and parts[0].ndim == 3:
-        return parts[0].reshape(-1, parts[0].shape[-1])
-    return jnp.concatenate(parts, axis=0)
+    rows = blocks[0].shape[0]
+    return jnp.concatenate([b[: min(rows, b.shape[0]), :] for b in blocks], axis=0)
 
 
 def place_rows(target_ref, data, begin, count):
@@ -185,23 +224,23 @@
     return jnp.dot(place, data, preferred_element_type=jnp.float32).astype(jnp.bfloat16)
 
 
-def pack_other_kernel(number, target_ref, *refs):
+def pack_other_kernel(number, order, target_ref, *refs):
     outs = refs[-SWAPS:]
     size = outs[0].shape[0]
     half = size * SWAPS
-    packed = place_rows(target_ref, rows_of(refs[:number]), half, half)
+    packed = place_rows(target_ref, rows_of(restored(refs[:number], order)), half, half)
     for at, out in enumerate(outs):
         out[...] = packed[at * size : (at + 1) * size]
 
 
-def pack_own_kernel(number, waits, target_ref, *refs):
+def pack_own_kernel(number, order, waits, target_ref, *refs):
     got, refs = refs[:SWAPS], refs[SWAPS:]
     blocks, outs = refs[:number], refs[number + waits :]
     size = got[0].shape[0]
     half = size * SWAPS
     capacity = outs[0].shape[0] // 2
     steps = half // capacity
-    packed = place_rows(target_ref, rows_of(blocks), 0, half)
+    packed = place_rows(target_ref, rows_of(restored(blocks, order)), 0, half)
     column = 0
     for first in range(0, len(outs), steps):
         wide = outs[first].shape[1]
@@ -214,21 +253,21 @@
         column += wide
 
 
-def deliver(target, blocks, widths, dp_size, capacity, after, later):
+def deliver(target, blocks, widths, dp_size, capacity, order, after, later):
     wide = blocks[0].shape[-1]
     length = target.shape[1]
     half = dp_size // 2 * capacity
     estimate = cost(2 * half * length * wide, 2 * (half + length) * wide)
     other = pl.pallas_call(
-        functools.partial(pack_other_kernel, len(blocks)),
+        functools.partial(pack_other_kernel, len(blocks), order),
         out_shape=[jax.ShapeDtypeStruct((half // SWAPS, wide), jnp.bfloat16)] * SWAPS,
         in_specs=[VMEM] * (1 + len(blocks)) + [ANY] * len(after),
         compiler_params=params(),
         cost_estimate=estimate,
-    )(target, *blocks, *after)
+    )(target, *mixed_up(blocks, order), *after)
     got = [lax.ppermute(part, "dp", [(j, j ^ 1) for j in range(dp_size)]) for part in other]
     outs = pl.pallas_call(
-        functools.partial(pack_own_kernel, len(blocks), len(later)),
+        functools.partial(pack_own_kernel, len(blocks), order, len(later)),
         out_shape=[
             jax.ShapeDtypeStruct((2 * capacity, part), jnp.bfloat16)
             for part in widths
@@ -237,7 +276,7 @@
         in_specs=[VMEM] * (1 + SWAPS + len(blocks)) + [ANY] * len(later),
         compiler_params=params(),
         cost_estimate=estimate,
-    )(target, *got, *blocks, *later)
+    )(target, *got, *mixed_up(blocks, order), *later)
     steps = dp_size // 2
     return [
         swap(list(outs[first : first + steps]), "dp", dp_size, 2)
@@ -263,7 +302,7 @@
     slot = slot_ref[...]
     live = live_ref[...]
     ones = jnp.ones((window, HEAD_DIM), jnp.bfloat16)
-    received = jnp.concatenate([b[...] for b in blocks], axis=0)
+    received = jnp.concatenate([b[...] for b in restored(blocks, ORDER_D)], axis=0)
     for block in range(pack_len // BLOCK):
         begin = block * BLOCK
         rows = pl.ds(begin, BLOCK)
@@ -279,20 +318,24 @@
         key_pos = key_start + lax.broadcasted_iota(jnp.int32, (BLOCK, span), 1)
         docs = jnp.concatenate([col_ref[rows, :]] * (span // HEAD_DIM), axis=1)
         allowed = (docs == doc_ref[:, pl.ds(key_start, span)]) & (key_pos <= query_pos)
+        bias = jnp.where(allowed, 0.0, -1e30)
         alive = begin + lax.broadcasted_iota(jnp.int32, (BLOCK, HEAD_DIM), 0) < live
-        for head in range(heads):
-            query = packed[:, head * HEAD_DIM : (head + 1) * HEAD_DIM]
-            scores = lax.dot_general(
-                query, keys, (((1,), (1,)), ((), ())), preferred_element_type=jnp.float32
-            )
-            masked = jnp.where(allowed, scores, -1e30)
-            top = jnp.max(masked, axis=1, keepdims=True)
-            weights = jnp.exp2((masked - top) * scale).astype(jnp.bfloat16)
-            mixed = jnp.dot(weights, values, preferred_element_type=jnp.float32)
-            result = mixed[:, :HEAD_DIM] / mixed[:, HEAD_DIM:]
-            acc[rows, head * HEAD_DIM : (head + 1) * HEAD_DIM] = jnp.where(
-                alive, result, 0.0
-            ).astype(jnp.bfloat16)
+        queries = jnp.concatenate(
+            [packed[:, i * HEAD_DIM : (i + 1) * HEAD_DIM] for i in range(heads)], axis=0
+        )
+        scores = lax.dot_general(
+            queries, keys, (((1,), (1,)), ((), ())), preferred_element_type=jnp.float32
+        )
+        masked = scores.reshape(heads, BLOCK, span) + bias[None]
+        top = jnp.max(masked, axis=2, keepdims=True)
+        weights = jnp.exp2((masked - top) * scale).astype(jnp.bfloat16)
+        mixed = jnp.dot(
+            weights.reshape(heads * BLOCK, span), values, preferred_element_type=jnp.float32
+        )
+        result = mixed[:, :HEAD_DIM] / mixed[:, HEAD_DIM:]
+        for i in range(heads):
+            head = jnp.where(alive, result[i * BLOCK : (i + 1) * BLOCK], 0.0)
+            acc[rows, i * HEAD_DIM : (i + 1) * HEAD_DIM] = head.astype(jnp.bfloat16)
     part = pack_len // ctx_size
     if stacked:
         outs[0][...] = acc[...].reshape(ctx_size, part, wide)
@@ -336,14 +379,14 @@
             8 * pack_len * wide,
             work,
         ),
-    )(slot, live, doc_row, doc_col, *received, *after, *([] if with_kv else [kv]))
+    )(slot, live, doc_row, doc_col, *mixed_up(received, ORDER_D), *after, *([] if with_kv else [kv]))
     return list(outs[:sent]), (outs[sent] if with_kv else kv)
 
 
 def join_kernel(chunk, ctx_size, number, *refs):
     offset, heads = chunk
     heads_dev = Q_HEADS // ctx_size
-    blocks = refs[:number]
+    blocks = restored(refs[:number], ORDER_J)
     out, sem = refs[-2:]
     me = lax.axis_index("ctx")
     copies = []
@@ -375,7 +418,7 @@
         input_output_aliases={number: 0} if given else {},
         compiler_params=params(),
         cost_estimate=cost(0, 4 * rows * chunk[1] * HEAD_DIM * ctx_size),
-    )(*blocks, *given)
+    )(*mixed_up(blocks, ORDER_J), *given)
 
 
 def on_device(q_src, kv_src, route, doc_ids):
@@ -386,22 +429,35 @@
     pack_len = dp_size * capacity
     pieces = head_chunks(Q_HEADS // ctx_size)
 
-    gathered, after = [], []
-    for at, piece in enumerate(pieces):
-        limit = VMEM_LIMIT if at else CUT_LIMIT
-        blocks = cut(q_src, kv_src, piece, ctx_size, at == 0, at in STACK_IN, after, limit)
-        gathered.append(exchange(blocks, ctx_size))
-        after = (gathered[-1] * 2)[1:2] if D1 else blocks[:1]
     target, swapped, slot, live = plan(route, dp_size, ctx_size, capacity)
     doc_col = jnp.broadcast_to(doc_ids.reshape(pack_len, 1), (pack_len, HEAD_DIM))
-
-    received, after = [], []
-    for at, blocks in enumerate(gathered):
+    gathered, received = [], []
+
+    def bring(at, after):
+        limit = VMEM_LIMIT if at else CUT_LIMIT
+        paired = at in PAIRED and ctx_size == 4
+        blocks = cut(q_src, kv_src, pieces[at], ctx_size, at == 0, paired, after, limit)
+        gathered.append(in_pairs(blocks, ctx_size) if paired else exchange(blocks, ctx_size))
+        return blocks
+
+    def route_on(at, after):
         widths = [chunk[1] * HEAD_DIM for chunk in pieces[at]]
         widths[0] += 0 if at else 2 * HEAD_DIM
-        first = (gathered[at + 1] * 2)[1:2] if PIN_OTHER and at + 1 < len(gathered) else []
-        received.append(deliver(target if at in STACK_IN else swapped, blocks, widths, dp_size, capacity, after + first, []))
-        after = [received[-1][0][i] for i in PIN_PACK]
+        received.append(deliver(swapped, gathered[at], widths, dp_size, capacity, ORDER_Z if at in ORDER_AT else (), after, []))
+
+    first = bring(0, [])
+    if len(pieces) == 1:
+        route_on(0, [])
+    elif D1 == 2:
+        route_on(0, [])
+        bring(1, received[0][0][:1])
+        route_on(1, [received[0][0][i] for i in PIN_PACK])
+    else:
+        bring(1, (gathered[0] * 2)[1:2] if D1 else first[:1])
+        route_on(0, [gathered[1][i % len(gathered[1])] for i in PIN_OTHER])
+        if len(gathered[1]) < ctx_size:
+            gathered[1] += hand_on(gathered[1][2], [received[0][0][i] for i in PIN_HAND], ctx_size)
+        route_on(1, [received[0][0][i] for i in PIN_PACK])
 
     kv, out, sends = None, None, []
     chunks = [chunk for piece in pieces for chunk in piece]

time: 90 us -> 84.5 us (0.939); the launches traced: 88.4 us -> 84.3 us
  Pallas kernels: 15.7 us -> 12 us
  local copies, waits for them, and re-layouts: 5.51 us -> 2.85 us
  waiting for transfers between devices: 41.4 us -> 42.9 us
  starting transfers between devices: 24.3 us -> 25.6 us
    ppermute x15 -> x18, starting transfers between devices: 17.1 us -> 24.5 us  [swap(): lax.ppermute(blocks[step], axis, [(j, j ^ step * unit) for j in range(siz...]
    all_to_all x1 -> x0, starting transfers between devices: 6.06 us -> none  [exchange(): lax.all_to_all(blocks[0], 'ctx', split_axis=0, concat_axis=0, tiled=True)]
    ppermute x15 -> x18, waiting for transfers between devices: 36 us -> 40.6 us  [swap(): lax.ppermute(blocks[step], axis, [(j, j ^ step * unit) for j in range(siz...]
    all_to_all x1 -> x0, waiting for transfers between devices: 3.09 us -> none  [exchange(): lax.all_to_all(blocks[0], 'ctx', split_axis=0, concat_axis=0, tiled=True)]
    unnamed x23 -> x9, local copies, waits for them, and re-layouts: 5.35 us -> 2.69 us
    pallas_call x6, Pallas kernels: 3.98 us -> 2.09 us  [the longest x2 0.85 us: deliver(): pl.pallas_call(functools.partial(pack_own_kernel, len(blocks), order, len...]
    pallas_call x2, Pallas kernels: 9.15 us -> 7.36 us  [attend(): pl.pallas_call(functools.partial(attend_kernel, heads, doc_most, ctx_size...]
  transfers between devices with their start and end apart: 20 -> 22, of which waited for: 16 -> 12; matrix products, arithmetic and copies ran while one was open for 2% -> 2% of each run, Pallas kernels for 8% -> 12%
where the time goes in v3:
time: 84.5 us; the launch traced here: 84.3 us
  waiting for transfers between devices  42.9 us (51%)
  starting transfers between devices  25.6 us (30%)
  Pallas kernels  12 us (14%)
  local copies, waits for them, and re-layouts  2.85 us (3%)
    ppermute x18, waiting for transfers between devices, swap(): lax.ppermute(blocks[step], axis, [(j, j ^ step * unit) for j in range(siz...  40.6 us
    ppermute x18, starting transfers between devices, swap(): lax.ppermute(blocks[step], axis, [(j, j ^ step * unit) for j in range(siz...  24.5 us
    pallas_call x2, Pallas kernels, attend(): pl.pallas_call(functools.partial(attend_kernel, heads, doc_most, ctx_size...  7.36 us
    unnamed x9, local copies, waits for them, and re-layouts  2.69 us
    ppermute x4, waiting for transfers between devices, deliver(): lax.ppermute(part, 'dp', [(j, j ^ 1) for j in range(dp_size)])  2.27 us
    pallas_call x2, Pallas kernels, join(): pl.pallas_call(functools.partial(join_kernel, chunk, ctx_size, number), o...  1.81 us
  transfers between devices with their start and end apart: 22, of which 12 were waited for; matrix products, arithmetic and copies ran while one was open for 2% of the time, Pallas kernels for 12%

profile of v3, /device:TPU:18, one launch (start us, length us, event | category | flops | bytes accessed | tf_op | source)
XLA Modules:
  0.0 84.3 jit_solution(680726592354040132)
XLA Ops:
  0.0 1.2 %copy-done = bf16[128,4096]{1,0:T(8,128)(2,1)S(1)} copy-done((bf16[128,4096]{1,0:T(8,128)(2,1)S(1)}, bf16[128,4096]{1,0:T(8,128)(2,1)}, u32[]{:S(2)}) %copy-start) | copy-done | bytes 1048600
  1.2 0.9 %copy-done.1 = bf16[128,1024]{1,0:T(8,128)(2,1)S(1)} copy-done((bf16[128,1024]{1,0:T(8,128)(2,1)S(1)}, bf16[128,1024]{1,0:T(8,128)(2,1)}, u32[]{:S(2)}) %copy-start.1) | copy-done | bytes 262168
  2.5 1.6 %collective-permute-start.3 = (bf16[128,768]{1,0:T(8,128)(2,1)S(1)}, bf16[128,768]{1,0:T(8,128)(2,1)S(1)}, u32[]{:S(2)}, u32[]{:S(2)}) collective-permute-start(bf16[128,768]{1,0:T(8,128)(2,1)S(1)} %get-tuple-element.45), channel_id=1, source_target_pairs={{0,1},{1,0},{2,3},{3,2},{4,5},{5,4},{6,7},{7,6},{8,9},{9,8},{10,11... | collective-permute-start | bytes 589832 | tf_op jit(solution)/shard_map/ppermute | solution.py:117
  4.5 1.6 %collective-permute-start.5 = (bf16[128,768]{1,0:T(8,128)(2,1)S(1)}, bf16[128,768]{1,0:T(8,128)(2,1)S(1)}, u32[]{:S(2)}, u32[]{:S(2)}) collective-permute-start(bf16[128,768]{1,0:T(8,128)(2,1)S(1)} %get-tuple-element.47), channel_id=1, source_target_pairs={{0,3},{1,2},{2,1},{3,0},{4,7},{5,6},{6,5},{7,4},{8,11},{9,10},{10,... | collective-permute-start | bytes 589832 | tf_op jit(solution)/shard_map/ppermute | solution.py:117
  6.2 2.5 %collective-permute-start = (bf16[128,512]{1,0:T(8,128)(2,1)S(1)}, bf16[128,512]{1,0:T(8,128)(2,1)S(1)}, u32[]{:S(2)}, u32[]{:S(2)}) collective-permute-start(bf16[128,512]{1,0:T(8,128)(2,1)S(1)} %get-tuple-element.42), channel_id=1, source_target_pairs={{0,1},{1,0},{2,3},{3,2},{4,5},{5,4},{6,7},{7,6},{8,9},{9,8},{10,11... | collective-permute-start | bytes 393224 | tf_op jit(solution)/shard_map/ppermute | solution.py:117
  9.2 0.7 reduce.4
  9.9 0.8 shard_map.46
  10.7 9.8 %collective-permute-done.refs_4_.refs_1_.refs_3_ = bf16[128,512]{1,0:T(8,128)(2,1)S(1)} collective-permute-done((bf16[128,512]{1,0:T(8,128)(2,1)S(1)}, bf16[128,512]{1,0:T(8,128)(2,1)S(1)}, u32[]{:S(2)}, u32[]{:S(2)}) %collective-permute-start) | collective-permute-done | bytes 131104 | tf_op jit(solution)/shard_map/ppermute | solution.py:117
  20.5 2.6 %collective-permute-done.5.refs_3_.refs_5_ = bf16[128,768]{1,0:T(8,128)(2,1)S(1)} collective-permute-done((bf16[128,768]{1,0:T(8,128)(2,1)S(1)}, bf16[128,768]{1,0:T(8,128)(2,1)S(1)}, u32[]{:S(2)}, u32[]{:S(2)}) %collective-permute-start.5) | collective-permute-done | bytes 196640 | tf_op jit(solution)/shard_map/ppermute | solution.py:117
  24.6 0.7 collective-permute-done.6.refs_0_
  26.1 0.6 collective-permute-start.13
  26.7 1.5 %collective-permute-start.14 = (bf16[192,768]{1,0:T(8,128)(2,1)S(1)}, bf16[192,768]{1,0:T(8,128)(2,1)S(1)}, u32[]{:S(2)}, u32[]{:S(2)}) collective-permute-start(bf16[192,768]{1,0:T(8,128)(2,1)S(1)} %get-tuple-element.58), channel_id=1, source_target_pairs={{0,16},{4,20},{8,24},{12,28},{16,0},{20,4},{24,8},{28,12},{1,17},{... | collective-permute-start | bytes 884744 | tf_op jit(solution)/shard_map/ppermute | solution.py:117
  28.2 1.4 %collective-permute-start.15 = (bf16[192,768]{1,0:T(8,128)(2,1)S(1)}, bf16[192,768]{1,0:T(8,128)(2,1)S(1)}, u32[]{:S(2)}, u32[]{:S(2)}) collective-permute-start(bf16[192,768]{1,0:T(8,128)(2,1)S(1)} %get-tuple-element.59), channel_id=1, source_target_pairs={{0,24},{4,28},{8,16},{12,20},{16,8},{20,12},{24,0},{28,4},{1,25},{... | collective-permute-start | bytes 884744 | tf_op jit(solution)/shard_map/ppermute | solution.py:117
  29.7 3.9 %collective-permute-done.1.refs_2_.refs_4_ = bf16[128,512]{1,0:T(8,128)(2,1)S(1)} collective-permute-done((bf16[128,512]{1,0:T(8,128)(2,1)S(1)}, bf16[128,512]{1,0:T(8,128)(2,1)S(1)}, u32[]{:S(2)}, u32[]{:S(2)}) %collective-permute-start.1) | collective-permute-done | bytes 131104 | tf_op jit(solution)/shard_map/ppermute | solution.py:117
  33.6 3.1 %collective-permute-done.2.refs_3_.refs_5_ = bf16[128,512]{1,0:T(8,128)(2,1)S(1)} collective-permute-done((bf16[128,512]{1,0:T(8,128)(2,1)S(1)}, bf16[128,512]{1,0:T(8,128)(2,1)S(1)}, u32[]{:S(2)}, u32[]{:S(2)}) %collective-permute-start.2) | collective-permute-done | bytes 131104 | tf_op jit(solution)/shard_map/ppermute | solution.py:117
  37.7 0.9 %collective-permute-done.8.refs_0_ = bf16[192,512]{1,0:T(8,128)(2,1)S(1)} collective-permute-done((bf16[192,512]{1,0:T(8,128)(2,1)S(1)}, bf16[192,512]{1,0:T(8,128)(2,1)S(1)}, u32[]{:S(2)}, u32[]{:S(2)}) %collective-permute-start.8) | collective-permute-done | bytes 196640 | tf_op jit(solution)/shard_map/ppermute | solution.py:268
  39.3 0.6 collective-permute-start.10
  39.9 1.5 %collective-permute-start.11 = (bf16[192,512]{1,0:T(8,128)(2,1)S(1)}, bf16[192,512]{1,0:T(8,128)(2,1)S(1)}, u32[]{:S(2)}, u32[]{:S(2)}) collective-permute-start(bf16[192,512]{1,0:T(8,128)(2,1)S(1)} %get-tuple-element.55), channel_id=1, source_target_pairs={{0,16},{4,20},{8,24},{12,28},{16,0},{20,4},{24,8},{28,12},{1,17},{... | collective-permute-start | bytes 589832 | tf_op jit(solution)/shard_map/ppermute | solution.py:117
  41.4 1.4 %collective-permute-start.12 = (bf16[192,512]{1,0:T(8,128)(2,1)S(1)}, bf16[192,512]{1,0:T(8,128)(2,1)S(1)}, u32[]{:S(2)}, u32[]{:S(2)}) collective-permute-start(bf16[192,512]{1,0:T(8,128)(2,1)S(1)} %get-tuple-element.56), channel_id=1, source_target_pairs={{0,24},{4,28},{8,16},{12,20},{16,8},{20,12},{24,0},{28,4},{1,25},{... | collective-permute-start | bytes 589832 | tf_op jit(solution)/shard_map/ppermute | solution.py:117
  43.0 3.9 %shard_map.53 = (bf16[192,512]{1,0:T(8,128)(2,1)S(1)}, bf16[192,512]{1,0:T(8,128)(2,1)S(1)}, bf16[192,512]{1,0:T(8,128)(2,1)S(1)}, bf16[192,512]{1,0:T(8,128)(2,1)S(1)}, bf16[768,256]{1,0:T(8,128)(2,1)S(1)}) custom-call(s32[1,768]{1,0:T(1,128)S(1)} %get-tuple-element.37.refs_0_, s32[1,128]{1,0:T(1,128)S(1)} %get-tuple-element.38.refs_1_, ...), custom_call_target="tpu_custom_call" | custom-call | flops 1811939328 | bytes 3145728 | tf_op jit(solution)/shard_map/pallas_call | solution.py:362
  46.9 3.1 %collective-permute-start.19 = (bf16[192,512]{1,0:T(8,128)(2,1)S(1)}, bf16[192,512]{1,0:T(8,128)(2,1)S(1)}, u32[]{:S(2)}, u32[]{:S(2)}) collective-permute-start(bf16[192,512]{1,0:T(8,128)(2,1)S(1)} %get-tuple-element.66), channel_id=1, source_target_pairs={{0,2},{1,3},{2,0},{3,1},{4,6},{5,7},{6,4},{7,5},{8,10},{9,11},{10,... | collective-permute-start | bytes 589832 | tf_op jit(solution)/shard_map/ppermute | solution.py:117
  50.0 2.0 %collective-permute-start.20 = (bf16[192,512]{1,0:T(8,128)(2,1)S(1)}, bf16[192,512]{1,0:T(8,128)(2,1)S(1)}, u32[]{:S(2)}, u32[]{:S(2)}) collective-permute-start(bf16[192,512]{1,0:T(8,128)(2,1)S(1)} %get-tuple-element.67), channel_id=1, source_target_pairs={{0,3},{1,2},{2,1},{3,0},{4,7},{5,6},{6,5},{7,4},{8,11},{9,10},{10,... | collective-permute-start | bytes 589832 | tf_op jit(solution)/shard_map/ppermute | solution.py:117
  52.0 3.5 %shard_map.54 = (bf16[192,512]{1,0:T(8,128)(2,1)S(1)}, bf16[192,512]{1,0:T(8,128)(2,1)S(1)}, bf16[192,512]{1,0:T(8,128)(2,1)S(1)}, bf16[192,512]{1,0:T(8,128)(2,1)S(1)}) custom-call(s32[1,768]{1,0:T(1,128)S(1)} %get-tuple-element.37.refs_0_, s32[1,128]{1,0:T(1,128)S(1)} %get-tuple-element.38.refs_1_, s32[1,768]{1,0:T(1,128)S(1)} %copy-done.2, ...), custom_call_target="tpu_custom_call" | custom-call | flops 1509949440 | bytes 3145728 | tf_op jit(solution)/shard_map/pallas_call | solution.py:362
  55.5 1.6 %collective-permute-start.16 = (bf16[192,512]{1,0:T(8,128)(2,1)S(1)}, bf16[192,512]{1,0:T(8,128)(2,1)S(1)}, u32[]{:S(2)}, u32[]{:S(2)}) collective-permute-start(bf16[192,512]{1,0:T(8,128)(2,1)S(1)} %get-tuple-element.62), channel_id=1, source_target_pairs={{0,2},{1,3},{2,0},{3,1},{4,6},{5,7},{6,4},{7,5},{8,10},{9,11},{10,... | collective-permute-start | bytes 589832 | tf_op jit(solution)/shard_map/ppermute | solution.py:117
  57.0 2.0 %collective-permute-start.17 = (bf16[192,512]{1,0:T(8,128)(2,1)S(1)}, bf16[192,512]{1,0:T(8,128)(2,1)S(1)}, u32[]{:S(2)}, u32[]{:S(2)}) collective-permute-start(bf16[192,512]{1,0:T(8,128)(2,1)S(1)} %get-tuple-element.63), channel_id=1, source_target_pairs={{0,3},{1,2},{2,1},{3,0},{4,7},{5,6},{6,5},{7,4},{8,11},{9,10},{10,... | collective-permute-start | bytes 589832 | tf_op jit(solution)/shard_map/ppermute | solution.py:117
  59.0 4.5 %collective-permute-done.19.refs_0_ = bf16[192,512]{1,0:T(8,128)(2,1)S(1)} collective-permute-done((bf16[192,512]{1,0:T(8,128)(2,1)S(1)}, bf16[192,512]{1,0:T(8,128)(2,1)S(1)}, u32[]{:S(2)}, u32[]{:S(2)}) %collective-permute-start.19) | collective-permute-done | bytes 196640 | tf_op jit(solution)/shard_map/ppermute | solution.py:117
  63.6 2.2 %collective-permute-start.18 = (bf16[192,512]{1,0:T(8,128)(2,1)S(1)}, bf16[192,512]{1,0:T(8,128)(2,1)S(1)}, u32[]{:S(2)}, u32[]{:S(2)}) collective-permute-start(bf16[192,512]{1,0:T(8,128)(2,1)S(1)} %get-tuple-element.64), channel_id=1, source_target_pairs={{0,1},{1,0},{2,3},{3,2},{4,5},{5,4},{6,7},{7,6},{8,9},{9,8},{10,11... | collective-permute-start | bytes 589832 | tf_op jit(solution)/shard_map/ppermute | solution.py:117
  65.8 9.5 %collective-permute-done.20.refs_1_ = bf16[192,512]{1,0:T(8,128)(2,1)S(1)} collective-permute-done((bf16[192,512]{1,0:T(8,128)(2,1)S(1)}, bf16[192,512]{1,0:T(8,128)(2,1)S(1)}, u32[]{:S(2)}, u32[]{:S(2)}) %collective-permute-start.20) | collective-permute-done | bytes 196640 | tf_op jit(solution)/shard_map/ppermute | solution.py:117
  75.3 0.9 %shard_map.55.refs_4_ = bf16[192,4096]{1,0:T(8,128)(2,1)} custom-call(bf16[192,512]{1,0:T(8,128)(2,1)S(1)} %collective-permute-done.19.refs_0_, bf16[192,512]{1,0:T(8,128)(2,1)S(1)} %collective-permute-done.20.refs_1_, bf16[192,512]{1,0:T(8,128)(2,1)S(1)} %collective-permute-done.21.refs_2_, bf16[192,512]{1,0:T(8,128)(2,1)S(1)} %get-tuple-element.60.refs_8_.refs_3_), custom_call_target="tpu_custom_call" | custom-call | bytes 1572864 | tf_op jit(solution)/shard_map/pallas_call | solution.py:412
  76.2 2.5 %collective-permute-done.16.refs_0_ = bf16[192,512]{1,0:T(8,128)(2,1)S(1)} collective-permute-done((bf16[192,512]{1,0:T(8,128)(2,1)S(1)}, bf16[192,512]{1,0:T(8,128)(2,1)S(1)}, u32[]{:S(2)}, u32[]{:S(2)}) %collective-permute-start.16) | collective-permute-done | bytes 196640 | tf_op jit(solution)/shard_map/ppermute | solution.py:117
  78.7 4.7 %collective-permute-done.17.refs_1_ = bf16[192,512]{1,0:T(8,128)(2,1)S(1)} collective-permute-done((bf16[192,512]{1,0:T(8,128)(2,1)S(1)}, bf16[192,512]{1,0:T(8,128)(2,1)S(1)}, u32[]{:S(2)}, u32[]{:S(2)}) %collective-permute-start.17) | collective-permute-done | bytes 196640 | tf_op jit(solution)/shard_map/ppermute | solution.py:117
  83.4 0.9 %shard_map.56 = bf16[192,4096]{1,0:T(8,128)(2,1)} custom-call(bf16[192,512]{1,0:T(8,128)(2,1)S(1)} %collective-permute-done.16.refs_0_, bf16[192,512]{1,0:T(8,128)(2,1)S(1)} %collective-permute-done.17.refs_1_, bf16[192,512]{1,0:T(8,128)(2,1)S(1)} %collective-permute-done.18.refs_2_, ...), custom_call_target="tpu_custom_call", output_to_operand_aliasing={{}: (4, {})} | custom-call | bytes 1572864 | tf_op jit(solution)/shard_map/pallas_call | solution.py:412
  (36 shorter events, 5.4 us)
Async XLA Ops:
  0.0 1.2 %copy-start = (bf16[128,4096]{1,0:T(8,128)(2,1)S(1)}, bf16[128,4096]{1,0:T(8,128)(2,1)}, u32[]{:S(2)}) copy-start(bf16[128,4096]{1,0:T(8,128)(2,1)} %q_ref.3) | copy-start | bytes 3145732
  1.2 0.9 %copy-start.1 = (bf16[128,1024]{1,0:T(8,128)(2,1)S(1)}, bf16[128,1024]{1,0:T(8,128)(2,1)}, u32[]{:S(2)}) copy-start(bf16[128,1024]{1,0:T(8,128)(2,1)} %kv_ref.3) | copy-start | bytes 786436
  2.2 7.0 %copy-start.3 = (s32[4096,1]{0,1:T(1,128)S(1)}, s32[4096,1]{0,1:T(1,128)}, u32[]{:S(2)}) copy-start(s32[4096,1]{0,1:T(1,128)} %param.6) | copy-start | bytes 49156
  2.5 18.0 %collective-permute-start.3 = (bf16[128,768]{1,0:T(8,128)(2,1)S(1)}, bf16[128,768]{1,0:T(8,128)(2,1)S(1)}, u32[]{:S(2)}, u32[]{:S(2)}) collective-permute-start(bf16[128,768]{1,0:T(8,128)(2,1)S(1)} %get-tuple-element.45), channel_id=1, source_target_pairs={{0,1},{1,0},{2,3},{3,2},{4,5},{5,4},{6,7},{7,6},{8,9},{9,8},{10,11... | collective-permute-start | bytes 589832 | tf_op jit(solution)/shard_map/ppermute | solution.py:117
  4.1 16.4 %collective-permute-start.4 = (bf16[128,768]{1,0:T(8,128)(2,1)S(1)}, bf16[128,768]{1,0:T(8,128)(2,1)S(1)}, u32[]{:S(2)}, u32[]{:S(2)}) collective-permute-start(bf16[128,768]{1,0:T(8,128)(2,1)S(1)} %get-tuple-element.46), channel_id=1, source_target_pairs={{0,2},{1,3},{2,0},{3,1},{4,6},{5,7},{6,4},{7,5},{8,10},{9,11},{10,... | collective-permute-start | bytes 589832 | tf_op jit(solution)/shard_map/ppermute | solution.py:117
  4.5 18.6 %collective-permute-start.5 = (bf16[128,768]{1,0:T(8,128)(2,1)S(1)}, bf16[128,768]{1,0:T(8,128)(2,1)S(1)}, u32[]{:S(2)}, u32[]{:S(2)}) collective-permute-start(bf16[128,768]{1,0:T(8,128)(2,1)S(1)} %get-tuple-element.47), channel_id=1, source_target_pairs={{0,3},{1,2},{2,1},{3,0},{4,7},{5,6},{6,5},{7,4},{8,11},{9,10},{10,... | collective-permute-start | bytes 589832 | tf_op jit(solution)/shard_map/ppermute | solution.py:117
  6.2 14.3 %collective-permute-start = (bf16[128,512]{1,0:T(8,128)(2,1)S(1)}, bf16[128,512]{1,0:T(8,128)(2,1)S(1)}, u32[]{:S(2)}, u32[]{:S(2)}) collective-permute-start(bf16[128,512]{1,0:T(8,128)(2,1)S(1)} %get-tuple-element.42), channel_id=1, source_target_pairs={{0,1},{1,0},{2,3},{3,2},{4,5},{5,4},{6,7},{7,6},{8,9},{9,8},{10,11... | collective-permute-start | bytes 393224 | tf_op jit(solution)/shard_map/ppermute | solution.py:117
  23.1 14.6 %copy-start.2 = (s32[1,768]{1,0:T(1,128)S(1)}, s32[1,768]{1,0:T(1,128)}, u32[]{:S(2)}) copy-start(s32[1,768]{1,0:T(1,128)} %refs_2_.3) | copy-start | bytes 9220
  23.6 1.6 %collective-permute-start.6 = (bf16[192,768]{1,0:T(8,128)(2,1)S(1)}, bf16[192,768]{1,0:T(8,128)(2,1)S(1)}, u32[]{:S(2)}, u32[]{:S(2)}) collective-permute-start(bf16[192,768]{1,0:T(8,128)(2,1)S(1)} %get-tuple-element.48), channel_id=1, source_target_pairs={{0,4},{4,0},{8,12},{12,8},{16,20},{20,16},{24,28},{28,24},{1,5},{5... | collective-permute-start | bytes 884744 | tf_op jit(solution)/shard_map/ppermute | solution.py:268
  23.7 2.0 %collective-permute-start.7 = (bf16[192,768]{1,0:T(8,128)(2,1)S(1)}, bf16[192,768]{1,0:T(8,128)(2,1)S(1)}, u32[]{:S(2)}, u32[]{:S(2)}) collective-permute-start(bf16[192,768]{1,0:T(8,128)(2,1)S(1)} %get-tuple-element.49), channel_id=1, source_target_pairs={{0,4},{4,0},{8,12},{12,8},{16,20},{20,16},{24,28},{28,24},{1,5},{5... | collective-permute-start | bytes 884744 | tf_op jit(solution)/shard_map/ppermute | solution.py:268
  24.2 9.5 %collective-permute-start.1 = (bf16[128,512]{1,0:T(8,128)(2,1)S(1)}, bf16[128,512]{1,0:T(8,128)(2,1)S(1)}, u32[]{:S(2)}, u32[]{:S(2)}) collective-permute-start(bf16[128,512]{1,0:T(8,128)(2,1)S(1)} %get-tuple-element.43), channel_id=1, source_target_pairs={{0,2},{1,3},{2,0},{3,1},{4,6},{5,7},{6,4},{7,5},{8,10},{9,11},{10,... | collective-permute-start | bytes 393224 | tf_op jit(solution)/shard_map/ppermute | solution.py:117
  24.2 12.6 %collective-permute-start.2 = (bf16[128,512]{1,0:T(8,128)(2,1)S(1)}, bf16[128,512]{1,0:T(8,128)(2,1)S(1)}, u32[]{:S(2)}, u32[]{:S(2)}) collective-permute-start(bf16[128,512]{1,0:T(8,128)(2,1)S(1)} %get-tuple-element.44), channel_id=1, source_target_pairs={{0,3},{1,2},{2,1},{3,0},{4,7},{5,6},{6,5},{7,4},{8,11},{9,10},{10,... | collective-permute-start | bytes 393224 | tf_op jit(solution)/shard_map/ppermute | solution.py:117
  26.1 15.3 %collective-permute-start.13 = (bf16[192,768]{1,0:T(8,128)(2,1)S(1)}, bf16[192,768]{1,0:T(8,128)(2,1)S(1)}, u32[]{:S(2)}, u32[]{:S(2)}) collective-permute-start(bf16[192,768]{1,0:T(8,128)(2,1)S(1)} %get-tuple-element.57), channel_id=1, source_target_pairs={{0,8},{4,12},{8,0},{12,4},{16,24},{20,28},{24,16},{28,20},{1,9},{5... | collective-permute-start | bytes 884744 | tf_op jit(solution)/shard_map/ppermute | solution.py:117
  26.7 16.1 %collective-permute-start.14 = (bf16[192,768]{1,0:T(8,128)(2,1)S(1)}, bf16[192,768]{1,0:T(8,128)(2,1)S(1)}, u32[]{:S(2)}, u32[]{:S(2)}) collective-permute-start(bf16[192,768]{1,0:T(8,128)(2,1)S(1)} %get-tuple-element.58), channel_id=1, source_target_pairs={{0,16},{4,20},{8,24},{12,28},{16,0},{20,4},{24,8},{28,12},{1,17},{... | collective-permute-start | bytes 884744 | tf_op jit(solution)/shard_map/ppermute | solution.py:117
  28.2 14.6 %collective-permute-start.15 = (bf16[192,768]{1,0:T(8,128)(2,1)S(1)}, bf16[192,768]{1,0:T(8,128)(2,1)S(1)}, u32[]{:S(2)}, u32[]{:S(2)}) collective-permute-start(bf16[192,768]{1,0:T(8,128)(2,1)S(1)} %get-tuple-element.59), channel_id=1, source_target_pairs={{0,24},{4,28},{8,16},{12,20},{16,8},{20,12},{24,0},{28,4},{1,25},{... | collective-permute-start | bytes 884744 | tf_op jit(solution)/shard_map/ppermute | solution.py:117
  37.1 1.5 %collective-permute-start.8 = (bf16[192,512]{1,0:T(8,128)(2,1)S(1)}, bf16[192,512]{1,0:T(8,128)(2,1)S(1)}, u32[]{:S(2)}, u32[]{:S(2)}) collective-permute-start(bf16[192,512]{1,0:T(8,128)(2,1)S(1)} %get-tuple-element.51), channel_id=1, source_target_pairs={{0,4},{4,0},{8,12},{12,8},{16,20},{20,16},{24,28},{28,24},{1,5},{5... | collective-permute-start | bytes 589832 | tf_op jit(solution)/shard_map/ppermute | solution.py:268
  37.2 1.7 %collective-permute-start.9 = (bf16[192,512]{1,0:T(8,128)(2,1)S(1)}, bf16[192,512]{1,0:T(8,128)(2,1)S(1)}, u32[]{:S(2)}, u32[]{:S(2)}) collective-permute-start(bf16[192,512]{1,0:T(8,128)(2,1)S(1)} %get-tuple-element.52), channel_id=1, source_target_pairs={{0,4},{4,0},{8,12},{12,8},{16,20},{20,16},{24,28},{28,24},{1,5},{5... | collective-permute-start | bytes 589832 | tf_op jit(solution)/shard_map/ppermute | solution.py:268
  39.3 12.7 %collective-permute-start.10 = (bf16[192,512]{1,0:T(8,128)(2,1)S(1)}, bf16[192,512]{1,0:T(8,128)(2,1)S(1)}, u32[]{:S(2)}, u32[]{:S(2)}) collective-permute-start(bf16[192,512]{1,0:T(8,128)(2,1)S(1)} %get-tuple-element.54), channel_id=1, source_target_pairs={{0,8},{4,12},{8,0},{12,4},{16,24},{20,28},{24,16},{28,20},{1,9},{5... | collective-permute-start | bytes 589832 | tf_op jit(solution)/shard_map/ppermute | solution.py:117
  39.9 12.1 %collective-permute-start.11 = (bf16[192,512]{1,0:T(8,128)(2,1)S(1)}, bf16[192,512]{1,0:T(8,128)(2,1)S(1)}, u32[]{:S(2)}, u32[]{:S(2)}) collective-permute-start(bf16[192,512]{1,0:T(8,128)(2,1)S(1)} %get-tuple-element.55), channel_id=1, source_target_pairs={{0,16},{4,20},{8,24},{12,28},{16,0},{20,4},{24,8},{28,12},{1,17},{... | collective-permute-start | bytes 589832 | tf_op jit(solution)/shard_map/ppermute | solution.py:117
  41.4 10.6 %collective-permute-start.12 = (bf16[192,512]{1,0:T(8,128)(2,1)S(1)}, bf16[192,512]{1,0:T(8,128)(2,1)S(1)}, u32[]{:S(2)}, u32[]{:S(2)}) collective-permute-start(bf16[192,512]{1,0:T(8,128)(2,1)S(1)} %get-tuple-element.56), channel_id=1, source_target_pairs={{0,24},{4,28},{8,16},{12,20},{16,8},{20,12},{24,0},{28,4},{1,25},{... | collective-permute-start | bytes 589832 | tf_op jit(solution)/shard_map/ppermute | solution.py:117
  46.9 16.6 %collective-permute-start.19 = (bf16[192,512]{1,0:T(8,128)(2,1)S(1)}, bf16[192,512]{1,0:T(8,128)(2,1)S(1)}, u32[]{:S(2)}, u32[]{:S(2)}) collective-permute-start(bf16[192,512]{1,0:T(8,128)(2,1)S(1)} %get-tuple-element.66), channel_id=1, source_target_pairs={{0,2},{1,3},{2,0},{3,1},{4,6},{5,7},{6,4},{7,5},{8,10},{9,11},{10,... | collective-permute-start | bytes 589832 | tf_op jit(solution)/shard_map/ppermute | solution.py:117
  50.0 25.3 %collective-permute-start.20 = (bf16[192,512]{1,0:T(8,128)(2,1)S(1)}, bf16[192,512]{1,0:T(8,128)(2,1)S(1)}, u32[]{:S(2)}, u32[]{:S(2)}) collective-permute-start(bf16[192,512]{1,0:T(8,128)(2,1)S(1)} %get-tuple-element.67), channel_id=1, source_target_pairs={{0,3},{1,2},{2,1},{3,0},{4,7},{5,6},{6,5},{7,4},{8,11},{9,10},{10,... | collective-permute-start | bytes 589832 | tf_op jit(solution)/shard_map/ppermute | solution.py:117
  52.0 23.3 %collective-permute-start.21 = (bf16[192,512]{1,0:T(8,128)(2,1)S(1)}, bf16[192,512]{1,0:T(8,128)(2,1)S(1)}, u32[]{:S(2)}, u32[]{:S(2)}) collective-permute-start(bf16[192,512]{1,0:T(8,128)(2,1)S(1)} %get-tuple-element.68), channel_id=1, source_target_pairs={{0,1},{1,0},{2,3},{3,2},{4,5},{5,4},{6,7},{7,6},{8,9},{9,8},{10,11... | collective-permute-start | bytes 589832 | tf_op jit(solution)/shard_map/ppermute | solution.py:117
  55.5 23.2 %collective-permute-start.16 = (bf16[192,512]{1,0:T(8,128)(2,1)S(1)}, bf16[192,512]{1,0:T(8,128)(2,1)S(1)}, u32[]{:S(2)}, u32[]{:S(2)}) collective-permute-start(bf16[192,512]{1,0:T(8,128)(2,1)S(1)} %get-tuple-element.62), channel_id=1, source_target_pairs={{0,2},{1,3},{2,0},{3,1},{4,6},{5,7},{6,4},{7,5},{8,10},{9,11},{10,... | collective-permute-start | bytes 589832 | tf_op jit(solution)/shard_map/ppermute | solution.py:117
  57.0 26.3 %collective-permute-start.17 = (bf16[192,512]{1,0:T(8,128)(2,1)S(1)}, bf16[192,512]{1,0:T(8,128)(2,1)S(1)}, u32[]{:S(2)}, u32[]{:S(2)}) collective-permute-start(bf16[192,512]{1,0:T(8,128)(2,1)S(1)} %get-tuple-element.63), channel_id=1, source_target_pairs={{0,3},{1,2},{2,1},{3,0},{4,7},{5,6},{6,5},{7,4},{8,11},{9,10},{10,... | collective-permute-start | bytes 589832 | tf_op jit(solution)/shard_map/ppermute | solution.py:117
  63.6 19.8 %collective-permute-start.18 = (bf16[192,512]{1,0:T(8,128)(2,1)S(1)}, bf16[192,512]{1,0:T(8,128)(2,1)S(1)}, u32[]{:S(2)}, u32[]{:S(2)}) collective-permute-start(bf16[192,512]{1,0:T(8,128)(2,1)S(1)} %get-tuple-element.64), channel_id=1, source_target_pairs={{0,1},{1,0},{2,3},{3,2},{4,5},{5,4},{6,7},{7,6},{8,9},{9,8},{10,11... | collective-permute-start | bytes 589832 | tf_op jit(solution)/shard_map/ppermute | solution.py:117

commit v4 on v2

v4 whole, which is shorter than its diff:
```python
import functools
import math

import jax
import jax.numpy as jnp
from jax import lax
from jax.experimental import pallas as pl
from jax.experimental.pallas import tpu as pltpu
from jax.sharding import PartitionSpec as P

Q_HEADS = 32
KV_HEADS = 4
HEAD_DIM = 128
BLOCK = 128
VMEM_LIMIT = 40 * 1024 * 1024
SWAPS = 2
JOIN_ORDER = (2, 3, 1, 0)
ANY = pl.BlockSpec(memory_space=pl.ANY)
VMEM = pl.BlockSpec(memory_space=pltpu.VMEM)


def params():
    return pltpu.CompilerParams(vmem_limit_bytes=VMEM_LIMIT)


def cost(flops, moved, exps=0):
    return pl.CostEstimate(flops=int(flops), bytes_accessed=int(moved), transcendentals=int(exps))


def head_chunks(heads_dev):
    first = max(1, heads_dev // 2)
    return [(0, first)] + ([(first, heads_dev - first)] if heads_dev > first else [])


def cut_kernel(chunk, ctx_size, with_kv, waits, q_ref, kv_ref, *refs):
    offset, heads = chunk
    outs, sem = refs[waits:-1], refs[-1]
    me = lax.axis_index("ctx")
    heads_dev = Q_HEADS // ctx_size
    group = Q_HEADS // KV_HEADS
    copies = []
    for step in list(range(1, ctx_size)) + [0]:
        owner = me ^ step
        parts = [(q_ref, owner * heads_dev + offset, heads)]
        if with_kv:
            head = (owner * heads_dev) // group
            parts += [(kv_ref, head, 1), (kv_ref, KV_HEADS + head, 1)]
        place = 0
        for source, block, number in parts:
            wide = number * HEAD_DIM
            column = pl.multiple_of(block * HEAD_DIM, HEAD_DIM)
            copies.append(
                (source.at[:, pl.ds(column, wide)], outs[step].at[:, pl.ds(place, wide)])
            )
            place += wide
    started = [pltpu.make_async_copy(a, b, sem.at[i]) for i, (a, b) in enumerate(copies)]
    for copy in started:
        copy.start()
    for copy in started:
        copy.wait()


def cut(q_src, kv_src, chunk, ctx_size, with_kv, after):
    rows = q_src.shape[0]
    wide = (chunk[1] + (2 if with_kv else 0)) * HEAD_DIM
    shapes = [jax.ShapeDtypeStruct((rows, wide), jnp.bfloat16)] * ctx_size
    outs = pl.pallas_call(
        functools.partial(cut_kernel, chunk, ctx_size, with_kv, len(after)),
        out_shape=shapes,
        in_specs=[ANY] * (2 + len(after)),
        out_specs=[VMEM] * len(shapes),
        scratch_shapes=[pltpu.SemaphoreType.DMA((ctx_size * (3 if with_kv else 1),))],
        compiler_params=params(),
        cost_estimate=cost(0, 4 * ctx_size * rows * wide),
    )(q_src, kv_src, *after)
    return list(outs)


def swap(blocks, axis, size, unit=1):
    return [blocks[0]] + [
        lax.ppermute(blocks[step], axis, [(j, j ^ (step * unit)) for j in range(size)])
        for step in range(1, len(blocks))
    ]


def plan_kernel(capacity, ctx_size, route_ref, target_ref, slot_ref, live_ref, natural):
    dp_size, length = route_ref.shape
    rows = length // ctx_size
    pack_len = dp_size * capacity
    own, me = lax.axis_index("dp"), lax.axis_index("ctx")
    mine = route_ref[pl.ds(own, 1), :]
    seq = lax.broadcasted_iota(jnp.int32, (dp_size, length), 0)
    onehot = jnp.where(mine == seq, 1.0, 0.0)
    earlier = lax.broadcasted_iota(jnp.int32, (length, length), 0)
    later = lax.broadcasted_iota(jnp.int32, (length, length), 1)
    strict = jnp.where(earlier < later, 1.0, 0.0).astype(jnp.bfloat16)
    before = jnp.dot(onehot.astype(jnp.bfloat16), strict, preferred_element_type=jnp.float32)
    rank = jnp.sum(before * onehot, axis=0, keepdims=True).astype(jnp.int32)
    other = mine ^ own
    place = (other & 1) * (dp_size // 2) + (other >> 1)
    natural[...] = place * capacity + rank
    for step in range(ctx_size):
        source = me ^ step
        target_ref[:, pl.ds(step * rows, rows)] = natural[
            :, pl.ds(pl.multiple_of(source * rows, rows), rows)
        ]
    incoming = jnp.sum(
        jnp.where(route_ref[...] == own, 1.0, 0.0), axis=1, keepdims=True
    )
    group = lax.broadcasted_iota(jnp.int32, (dp_size, pack_len), 0)
    lane = lax.broadcasted_iota(jnp.int32, (dp_size, pack_len), 1)
    block = lax.div(lane, capacity)
    source = block ^ own
    start = jnp.sum(jnp.where(group < source, incoming, 0.0), axis=0, keepdims=True)
    amount = jnp.sum(jnp.where(group == source, incoming, 0.0), axis=0, keepdims=True)
    offset = (lane - block * capacity)[:1]
    slot_ref[...] = jnp.where(
        offset < amount.astype(jnp.int32), start.astype(jnp.int32) + offset, -1
    )
    live = jnp.sum(incoming, axis=0, keepdims=True).astype(jnp.int32)
    live_ref[...] = jnp.broadcast_to(live, live_ref.shape)


def plan(route, dp_size, ctx_size, capacity):
    length = route.shape[0] // dp_size
    return pl.pallas_call(
        functools.partial(plan_kernel, capacity, ctx_size),
        out_shape=[
            jax.ShapeDtypeStruct((1, length), jnp.int32),
            jax.ShapeDtypeStruct((1, dp_size * capacity), jnp.int32),
            jax.ShapeDtypeStruct((1, HEAD_DIM), jnp.int32),
        ],
        scratch_shapes=[pltpu.VMEM((1, length), jnp.int32)],
        compiler_params=params(),
        cost_estimate=cost(2 * dp_size * length * length, 8 * length * dp_size),
    )(route.reshape(dp_size, length))


def rows_of(blocks):
    return jnp.concatenate([b[...] for b in blocks], axis=0)


def place_rows(target_ref, data, begin, count):
    row = begin + lax.broadcasted_iota(jnp.int32, (count, target_ref.shape[1]), 0)
    place = jnp.where(target_ref[...] == row, 1.0, 0.0).astype(jnp.bfloat16)
    return jnp.dot(place, data, preferred_element_type=jnp.float32).astype(jnp.bfloat16)


def pack_other_kernel(number, target_ref, *refs):
    outs = refs[-SWAPS:]
    size = outs[0].shape[0]
    half = size * SWAPS
    packed = place_rows(target_ref, rows_of(refs[:number]), half, half)
    for at, out in enumerate(outs):
        out[...] = packed[at * size : (at + 1) * size]


def pack_own_kernel(number, target_ref, *refs):
    got, refs = refs[:SWAPS], refs[SWAPS:]
    blocks, outs = refs[:number], refs[number:]
    size = got[0].shape[0]
    half = size * SWAPS
    capacity = outs[0].shape[0] // 2
    packed = place_rows(target_ref, rows_of(blocks), 0, half)
    for step, out in enumerate(outs):
        first = step * capacity
        out[:capacity, :] = packed[first : first + capacity]
        begin = first % size
        out[capacity:, :] = got[first // size][begin : begin + capacity, :]


def deliver(target, blocks, dp_size, capacity, after):
    wide = blocks[0].shape[-1]
    length = target.shape[1]
    half = dp_size // 2 * capacity
    estimate = cost(2 * half * length * wide, 2 * (half + length) * wide)
    other = pl.pallas_call(
        functools.partial(pack_other_kernel, len(blocks)),
        out_shape=[jax.ShapeDtypeStruct((half // SWAPS, wide), jnp.bfloat16)] * SWAPS,
        in_specs=[VMEM] * (1 + len(blocks)) + [ANY] * len(after),
        compiler_params=params(),
        cost_estimate=estimate,
    )(target, *blocks, *after)
    got = [lax.ppermute(part, "dp", [(j, j ^ 1) for j in range(dp_size)]) for part in other]
    outs = pl.pallas_call(
        functools.partial(pack_own_kernel, len(blocks)),
        out_shape=[jax.ShapeDtypeStruct((2 * capacity, wide), jnp.bfloat16)] * (dp_size // 2),
        compiler_params=params(),
        cost_estimate=estimate,
    )(target, *got, *blocks)
    return swap(list(outs), "dp", dp_size, 2)


def attend_kernel(
    heads, doc_most, ctx_size, number, waits, with_kv, *refs
):
    slot_ref, live_ref, doc_ref, col_ref = refs[:4]
    blocks, refs = refs[4 : 4 + number], refs[4 + number + waits :]
    if with_kv:
        outs, kv_ref, acc = refs[:-2], refs[-2], refs[-1]
    else:
        kv_ref, outs, acc = refs[0], refs[1:-1], refs[-1]
    me = lax.axis_index("ctx")
    pack_len = acc.shape[0]
    wide = heads * HEAD_DIM
    scale = HEAD_DIM ** (-0.5) * math.log2(math.e)
    window = min(pack_len, doc_most + BLOCK)
    live = live_ref[...]
    ones = jnp.ones((window, HEAD_DIM), jnp.bfloat16)
    received = rows_of(blocks)
    most = 6 * BLOCK
    row = lax.broadcasted_iota(jnp.int32, (most, pack_len), 0)
    for begin in range(0, pack_len, most):
        place = jnp.where(slot_ref[...] == row + begin, 1.0, 0.0).astype(jnp.bfloat16)
        packed = jnp.dot(place, received, preferred_element_type=jnp.float32).astype(jnp.bfloat16)
        acc[begin : begin + most, :] = packed[:, :wide]
        if with_kv:
            kv_ref[begin : begin + most, :] = packed[:, wide:]
    for block in range(pack_len // BLOCK):
        begin = block * BLOCK
        rows = pl.ds(begin, BLOCK)
        packed = acc[rows, :]
        key_start = max(0, begin + BLOCK - window)
        span = begin + BLOCK - key_start
        keys = kv_ref[pl.ds(key_start, span), :HEAD_DIM]
        values = jnp.concatenate([kv_ref[pl.ds(key_start, span), HEAD_DIM:], ones[:span]], axis=1)
        query_pos = begin + lax.broadcasted_iota(jnp.int32, (BLOCK, span), 0)
        key_pos = key_start + lax.broadcasted_iota(jnp.int32, (BLOCK, span), 1)
        docs = jnp.concatenate([col_ref[rows, :]] * (span // HEAD_DIM), axis=1)
        allowed = (docs == doc_ref[:, pl.ds(key_start, span)]) & (key_pos <= query_pos)
        bias = jnp.where(allowed, 0.0, -1e30)
        alive = begin + lax.broadcasted_iota(jnp.int32, (BLOCK, HEAD_DIM), 0) < live
        queries = jnp.concatenate(
            [packed[:, i * HEAD_DIM : (i + 1) * HEAD_DIM] for i in range(heads)], axis=0
        )
        scores = lax.dot_general(
            queries, keys, (((1,), (1,)), ((), ())), preferred_element_type=jnp.float32
        )
        masked = scores.reshape(heads, BLOCK, span) + bias[None]
        top = jnp.max(masked, axis=2, keepdims=True)
        weights = jnp.exp2((masked - top) * scale).astype(jnp.bfloat16)
        mixed = jnp.dot(
            weights.reshape(heads * BLOCK, span), values, preferred_element_type=jnp.float32
        )
        result = mixed[:, :HEAD_DIM] / mixed[:, HEAD_DIM:]
        for i in range(heads):
            head = jnp.where(alive, result[i * BLOCK : (i + 1) * BLOCK], 0.0)
            acc[rows, i * HEAD_DIM : (i + 1) * HEAD_DIM] = head.astype(jnp.bfloat16)
    part = pack_len // ctx_size
    for step in range(ctx_size):
        first = pl.multiple_of((me ^ step) * part, part)
        outs[step][...] = acc[pl.ds(first, part), :]


def attend(received, slot, live, doc_row, doc_col, kv, heads, ctx_size, after):
    pack_len = slot.shape[1]
    doc_most = pack_len // 3
    wide = heads * HEAD_DIM
    with_kv = kv is None
    part = pack_len // ctx_size
    shapes = [jax.ShapeDtypeStruct((part, wide), jnp.bfloat16)] * ctx_size
    sent = len(shapes)
    if with_kv:
        shapes = shapes + [jax.ShapeDtypeStruct((pack_len, 2 * HEAD_DIM), jnp.bfloat16)]
    work = pack_len * (doc_most + BLOCK) * heads
    outs = pl.pallas_call(
        functools.partial(
            attend_kernel,
            heads,
            doc_most,
            ctx_size,
            len(received),
            len(after),
            with_kv,
        ),
        out_shape=shapes,
        in_specs=[VMEM] * (4 + len(received)) + [ANY] * len(after) + [VMEM] * (0 if with_kv else 1),
        scratch_shapes=[pltpu.VMEM((pack_len, wide), jnp.bfloat16)],
        compiler_params=params(),
        cost_estimate=cost(
            2 * pack_len * pack_len * received[0].shape[1] + 6 * work * HEAD_DIM,
            8 * pack_len * wide,
            work,
        ),
    )(slot, live, doc_row, doc_col, *received, *after, *([] if with_kv else [kv]))
    return list(outs[:sent]), (outs[sent] if with_kv else kv)


def join_kernel(chunk, ctx_size, steps, *refs):
    offset, heads = chunk
    heads_dev = Q_HEADS // ctx_size
    out, sem = refs[-2:]
    me = lax.axis_index("ctx")
    copies = []
    for at, step in enumerate(steps):
        column = pl.multiple_of(((me ^ step) * heads_dev + offset) * HEAD_DIM, HEAD_DIM)
        copies.append(
            pltpu.make_async_copy(
                refs[at], out.at[:, pl.ds(column, heads * HEAD_DIM)], sem.at[at]
            )
        )
    for copy in copies:
        copy.start()
    for copy in copies:
        copy.wait()


def join(blocks, chunk, out, ctx_size):
    rows = blocks[0].shape[0]
    given = [] if out is None else [out]
    steps = JOIN_ORDER if len(JOIN_ORDER) == ctx_size else tuple(range(ctx_size))
    return pl.pallas_call(
        functools.partial(join_kernel, chunk, ctx_size, steps),
        out_shape=jax.ShapeDtypeStruct((rows, Q_HEADS * HEAD_DIM), jnp.bfloat16),
        in_specs=[ANY] * (ctx_size + len(given)),
        out_specs=ANY,
        scratch_shapes=[pltpu.SemaphoreType.DMA((ctx_size,))],
        input_output_aliases={ctx_size: 0} if given else {},
        compiler_params=params(),
        cost_estimate=cost(0, 4 * rows * chunk[1] * HEAD_DIM * ctx_size),
    )(*[blocks[step] for step in steps], *given)


def on_device(q_src, kv_src, route, doc_ids):
    ctx_size = lax.axis_size("ctx")
    dp_size = lax.axis_size("dp")
    length = q_src.shape[0] * ctx_size
    capacity = 3 * length // (2 * dp_size)
    pack_len = dp_size * capacity
    chunks = head_chunks(Q_HEADS // ctx_size)

    gathered, after = [], []
    for at, chunk in enumerate(chunks):
        blocks = cut(q_src, kv_src, chunk, ctx_size, at == 0, after)
        gathered.append(swap(blocks, "ctx", ctx_size))
        after = blocks[:1]
    target, slot, live = plan(route, dp_size, ctx_size, capacity)
    doc_col = jnp.broadcast_to(doc_ids.reshape(pack_len, 1), (pack_len, HEAD_DIM))

    packed = []
    for at, blocks in enumerate(gathered):
        after = [blocks[1] for blocks in gathered[at + 1 : at + 2]] + [p[0] for p in packed[-1:]]
        packed.append(deliver(target, blocks, dp_size, capacity, after))

    kv, sends = None, []
    for at, chunk in enumerate(chunks):
        after = [sends[-1][0]] if sends else [p[0] for p in packed[1:2]]
        blocks, kv = attend(
            packed[at], slot, live, doc_ids, doc_col, kv, chunk[1], ctx_size, after
        )
        sends.append(swap(blocks, "ctx", ctx_size))
    out = None
    for chunk, blocks in zip(chunks, sends):
        out = join(blocks, chunk, out, ctx_size)
    return out


def solution(mesh):
    in_specs = (P(("dp", "ctx"), None), P(("dp", "ctx"), None), P(), P("dp", None))
    out_specs = P(("dp", "ctx"), None)
    return jax.shard_map(
        on_device, mesh=mesh, in_specs=in_specs, out_specs=out_specs, check_vma=False
    )
```

time: 90 us -> 84 us (0.933); the launches traced: 88.4 us -> 83.8 us
  starting transfers between devices: 24.3 us -> 30.8 us
  Pallas kernels: 15.7 us -> 10.5 us
  local copies, waits for them, and re-layouts: 5.51 us -> 2.85 us
  waiting for transfers between devices: 41.4 us -> 38.8 us
    ppermute x15 -> x18, starting transfers between devices: 17.1 us -> 29.7 us  [swap(): lax.ppermute(blocks[step], axis, [(j, j ^ step * unit) for j in range(siz...]
    all_to_all x1 -> x0, starting transfers between devices: 6.06 us -> none  [exchange(): lax.all_to_all(blocks[0], 'ctx', split_axis=0, concat_axis=0, tiled=True)]
    all_to_all x1 -> x0, waiting for transfers between devices: 3.09 us -> none  [exchange(): lax.all_to_all(blocks[0], 'ctx', split_axis=0, concat_axis=0, tiled=True)]
    pallas_call x2, Pallas kernels: 9.15 us -> 6.43 us  [attend(): pl.pallas_call(functools.partial(attend_kernel, heads, doc_most, ctx_size...]
    unnamed x23 -> x9, local copies, waits for them, and re-layouts: 5.35 us -> 2.69 us
    pallas_call x6, Pallas kernels: 4.94 us -> 3.06 us  [the longest x2 1.81 us: join(): pl.pallas_call(functools.partial(join_kernel, chunk, ctx_size, steps), ou...]
    ppermute x15 -> x18, waiting for transfers between devices: 36 us -> 36.5 us  [swap(): lax.ppermute(blocks[step], axis, [(j, j ^ step * unit) for j in range(siz...]
  transfers between devices with their start and end apart: 20 -> 22, of which waited for: 16 -> 13; matrix products, arithmetic and copies ran while one was open for 2% -> 2% of each run, Pallas kernels for 8% -> 11%
where the time goes in v4:
time: 84 us; the launch traced here: 83.8 us
  waiting for transfers between devices  38.8 us (46%)
  starting transfers between devices  30.8 us (37%)
  Pallas kernels  10.5 us (12%)
  local copies, waits for them, and re-layouts  2.85 us (3%)
    ppermute x18, waiting for transfers between devices, swap(): lax.ppermute(blocks[step], axis, [(j, j ^ step * unit) for j in range(siz...  36.5 us
    ppermute x18, starting transfers between devices, swap(): lax.ppermute(blocks[step], axis, [(j, j ^ step * unit) for j in range(siz...  29.7 us
    pallas_call x2, Pallas kernels, attend(): pl.pallas_call(functools.partial(attend_kernel, heads, doc_most, ctx_size...  6.43 us
    unnamed x9, local copies, waits for them, and re-layouts  2.69 us
    ppermute x4, waiting for transfers between devices, deliver(): lax.ppermute(part, 'dp', [(j, j ^ 1) for j in range(dp_size)])  2.27 us
    pallas_call x2, Pallas kernels, join(): pl.pallas_call(functools.partial(join_kernel, chunk, ctx_size, steps), ou...  1.81 us
  transfers between devices with their start and end apart: 22, of which 13 were waited for; matrix products, arithmetic and copies ran while one was open for 2% of the time, Pallas kernels for 11%

profile of v4, /device:TPU:18, one launch (start us, length us, event | category | flops | bytes accessed | tf_op | source)
XLA Modules:
  0.0 83.8 jit_solution(8066206691481063717)
XLA Ops:
  0.0 1.2 %copy-done = bf16[128,4096]{1,0:T(8,128)(2,1)S(1)} copy-done((bf16[128,4096]{1,0:T(8,128)(2,1)S(1)}, bf16[128,4096]{1,0:T(8,128)(2,1)}, u32[]{:S(2)}) %copy-start) | copy-done | bytes 1048600
  1.2 0.9 %copy-done.1 = bf16[128,1024]{1,0:T(8,128)(2,1)S(1)} copy-done((bf16[128,1024]{1,0:T(8,128)(2,1)S(1)}, bf16[128,1024]{1,0:T(8,128)(2,1)}, u32[]{:S(2)}) %copy-start.1) | copy-done | bytes 262168
  2.5 1.6 %collective-permute-start.3 = (bf16[128,768]{1,0:T(8,128)(2,1)S(1)}, bf16[128,768]{1,0:T(8,128)(2,1)S(1)}, u32[]{:S(2)}, u32[]{:S(2)}) collective-permute-start(bf16[128,768]{1,0:T(8,128)(2,1)S(1)} %get-tuple-element.45), channel_id=1, source_target_pairs={{0,1},{1,0},{2,3},{3,2},{4,5},{5,4},{6,7},{7,6},{8,9},{9,8},{10,11... | collective-permute-start | bytes 589832 | tf_op jit(solution)/shard_map/ppermute | solution.py:81
  4.5 1.6 %collective-permute-start.5 = (bf16[128,768]{1,0:T(8,128)(2,1)S(1)}, bf16[128,768]{1,0:T(8,128)(2,1)S(1)}, u32[]{:S(2)}, u32[]{:S(2)}) collective-permute-start(bf16[128,768]{1,0:T(8,128)(2,1)S(1)} %get-tuple-element.47), channel_id=1, source_target_pairs={{0,3},{1,2},{2,1},{3,0},{4,7},{5,6},{6,5},{7,4},{8,11},{9,10},{10,... | collective-permute-start | bytes 589832 | tf_op jit(solution)/shard_map/ppermute | solution.py:81
  6.2 2.5 %collective-permute-start = (bf16[128,512]{1,0:T(8,128)(2,1)S(1)}, bf16[128,512]{1,0:T(8,128)(2,1)S(1)}, u32[]{:S(2)}, u32[]{:S(2)}) collective-permute-start(bf16[128,512]{1,0:T(8,128)(2,1)S(1)} %get-tuple-element.42), channel_id=1, source_target_pairs={{0,1},{1,0},{2,3},{3,2},{4,5},{5,4},{6,7},{7,6},{8,9},{9,8},{10,11... | collective-permute-start | bytes 393224 | tf_op jit(solution)/shard_map/ppermute | solution.py:81
  8.7 0.5 broadcast.4
  9.2 0.7 reduce.4
  10.1 10.3 %collective-permute-done.refs_4_.refs_1_.refs_3_ = bf16[128,512]{1,0:T(8,128)(2,1)S(1)} collective-permute-done((bf16[128,512]{1,0:T(8,128)(2,1)S(1)}, bf16[128,512]{1,0:T(8,128)(2,1)S(1)}, u32[]{:S(2)}, u32[]{:S(2)}) %collective-permute-start) | collective-permute-done | bytes 131104 | tf_op jit(solution)/shard_map/ppermute | solution.py:81
  20.5 2.6 %collective-permute-done.5.refs_3_.refs_5_ = bf16[128,768]{1,0:T(8,128)(2,1)S(1)} collective-permute-done((bf16[128,768]{1,0:T(8,128)(2,1)S(1)}, bf16[128,768]{1,0:T(8,128)(2,1)S(1)}, u32[]{:S(2)}, u32[]{:S(2)}) %collective-permute-start.5) | collective-permute-done | bytes 196640 | tf_op jit(solution)/shard_map/ppermute | solution.py:81
  24.6 0.7 collective-permute-done.6.refs_0_
  26.1 0.6 collective-permute-start.13
  26.7 1.5 %collective-permute-start.14 = (bf16[192,768]{1,0:T(8,128)(2,1)S(1)}, bf16[192,768]{1,0:T(8,128)(2,1)S(1)}, u32[]{:S(2)}, u32[]{:S(2)}) collective-permute-start(bf16[192,768]{1,0:T(8,128)(2,1)S(1)} %get-tuple-element.58), channel_id=1, source_target_pairs={{0,16},{4,20},{8,24},{12,28},{16,0},{20,4},{24,8},{28,12},{1,17},{... | collective-permute-start | bytes 884744 | tf_op jit(solution)/shard_map/ppermute | solution.py:81
  28.2 1.4 %collective-permute-start.15 = (bf16[192,768]{1,0:T(8,128)(2,1)S(1)}, bf16[192,768]{1,0:T(8,128)(2,1)S(1)}, u32[]{:S(2)}, u32[]{:S(2)}) collective-permute-start(bf16[192,768]{1,0:T(8,128)(2,1)S(1)} %get-tuple-element.59), channel_id=1, source_target_pairs={{0,24},{4,28},{8,16},{12,20},{16,8},{20,12},{24,0},{28,4},{1,25},{... | collective-permute-start | bytes 884744 | tf_op jit(solution)/shard_map/ppermute | solution.py:81
  29.7 3.9 %collective-permute-done.1.refs_2_.refs_4_ = bf16[128,512]{1,0:T(8,128)(2,1)S(1)} collective-permute-done((bf16[128,512]{1,0:T(8,128)(2,1)S(1)}, bf16[128,512]{1,0:T(8,128)(2,1)S(1)}, u32[]{:S(2)}, u32[]{:S(2)}) %collective-permute-start.1) | collective-permute-done | bytes 131104 | tf_op jit(solution)/shard_map/ppermute | solution.py:81
  33.6 3.1 %collective-permute-done.2.refs_3_.refs_5_ = bf16[128,512]{1,0:T(8,128)(2,1)S(1)} collective-permute-done((bf16[128,512]{1,0:T(8,128)(2,1)S(1)}, bf16[128,512]{1,0:T(8,128)(2,1)S(1)}, u32[]{:S(2)}, u32[]{:S(2)}) %collective-permute-start.2) | collective-permute-done | bytes 131104 | tf_op jit(solution)/shard_map/ppermute | solution.py:81
  37.7 0.9 %collective-permute-done.8.refs_0_ = bf16[192,512]{1,0:T(8,128)(2,1)S(1)} collective-permute-done((bf16[192,512]{1,0:T(8,128)(2,1)S(1)}, bf16[192,512]{1,0:T(8,128)(2,1)S(1)}, u32[]{:S(2)}, u32[]{:S(2)}) %collective-permute-start.8) | collective-permute-done | bytes 196640 | tf_op jit(solution)/shard_map/ppermute | solution.py:184
  39.3 0.6 collective-permute-start.10
  39.9 1.5 %collective-permute-start.11 = (bf16[192,512]{1,0:T(8,128)(2,1)S(1)}, bf16[192,512]{1,0:T(8,128)(2,1)S(1)}, u32[]{:S(2)}, u32[]{:S(2)}) collective-permute-start(bf16[192,512]{1,0:T(8,128)(2,1)S(1)} %get-tuple-element.55), channel_id=1, source_target_pairs={{0,16},{4,20},{8,24},{12,28},{16,0},{20,4},{24,8},{28,12},{1,17},{... | collective-permute-start | bytes 589832 | tf_op jit(solution)/shard_map/ppermute | solution.py:81
  41.4 1.4 %collective-permute-start.12 = (bf16[192,512]{1,0:T(8,128)(2,1)S(1)}, bf16[192,512]{1,0:T(8,128)(2,1)S(1)}, u32[]{:S(2)}, u32[]{:S(2)}) collective-permute-start(bf16[192,512]{1,0:T(8,128)(2,1)S(1)} %get-tuple-element.56), channel_id=1, source_target_pairs={{0,24},{4,28},{8,16},{12,20},{16,8},{20,12},{24,0},{28,4},{1,25},{... | collective-permute-start | bytes 589832 | tf_op jit(solution)/shard_map/ppermute | solution.py:81
  43.0 3.4 %shard_map.53 = (bf16[192,512]{1,0:T(8,128)(2,1)S(1)}, bf16[192,512]{1,0:T(8,128)(2,1)S(1)}, bf16[192,512]{1,0:T(8,128)(2,1)S(1)}, bf16[192,512]{1,0:T(8,128)(2,1)S(1)}, bf16[768,256]{1,0:T(8,128)(2,1)S(1)}) custom-call(s32[1,768]{1,0:T(1,128)S(1)} %get-tuple-element.37.refs_0_, s32[1,128]{1,0:T(1,128)S(1)} %get-tuple-element.38.refs_1_, ...), custom_call_target="tpu_custom_call" | custom-call | flops 1811939328 | bytes 3145728 | tf_op jit(solution)/shard_map/pallas_call | solution.py:266
  46.4 3.1 %collective-permute-start.19 = (bf16[192,512]{1,0:T(8,128)(2,1)S(1)}, bf16[192,512]{1,0:T(8,128)(2,1)S(1)}, u32[]{:S(2)}, u32[]{:S(2)}) collective-permute-start(bf16[192,512]{1,0:T(8,128)(2,1)S(1)} %get-tuple-element.66), channel_id=1, source_target_pairs={{0,2},{1,3},{2,0},{3,1},{4,6},{5,7},{6,4},{7,5},{8,10},{9,11},{10,... | collective-permute-start | bytes 589832 | tf_op jit(solution)/shard_map/ppermute | solution.py:81
  49.5 2.0 %collective-permute-start.20 = (bf16[192,512]{1,0:T(8,128)(2,1)S(1)}, bf16[192,512]{1,0:T(8,128)(2,1)S(1)}, u32[]{:S(2)}, u32[]{:S(2)}) collective-permute-start(bf16[192,512]{1,0:T(8,128)(2,1)S(1)} %get-tuple-element.67), channel_id=1, source_target_pairs={{0,3},{1,2},{2,1},{3,0},{4,7},{5,6},{6,5},{7,4},{8,11},{9,10},{10,... | collective-permute-start | bytes 589832 | tf_op jit(solution)/shard_map/ppermute | solution.py:81
  51.5 3.1 %shard_map.54 = (bf16[192,512]{1,0:T(8,128)(2,1)S(1)}, bf16[192,512]{1,0:T(8,128)(2,1)S(1)}, bf16[192,512]{1,0:T(8,128)(2,1)S(1)}, bf16[192,512]{1,0:T(8,128)(2,1)S(1)}) custom-call(s32[1,768]{1,0:T(1,128)S(1)} %get-tuple-element.37.refs_0_, s32[1,128]{1,0:T(1,128)S(1)} %get-tuple-element.38.refs_1_, s32[1,768]{1,0:T(1,128)S(1)} %copy-done.2, ...), custom_call_target="tpu_custom_call" | custom-call | flops 1509949440 | bytes 3145728 | tf_op jit(solution)/shard_map/pallas_call | solution.py:266
  54.6 1.6 %collective-permute-start.16 = (bf16[192,512]{1,0:T(8,128)(2,1)S(1)}, bf16[192,512]{1,0:T(8,128)(2,1)S(1)}, u32[]{:S(2)}, u32[]{:S(2)}) collective-permute-start(bf16[192,512]{1,0:T(8,128)(2,1)S(1)} %get-tuple-element.62), channel_id=1, source_target_pairs={{0,2},{1,3},{2,0},{3,1},{4,6},{5,7},{6,4},{7,5},{8,10},{9,11},{10,... | collective-permute-start | bytes 589832 | tf_op jit(solution)/shard_map/ppermute | solution.py:81
  56.2 1.8 %collective-permute-start.17 = (bf16[192,512]{1,0:T(8,128)(2,1)S(1)}, bf16[192,512]{1,0:T(8,128)(2,1)S(1)}, u32[]{:S(2)}, u32[]{:S(2)}) collective-permute-start(bf16[192,512]{1,0:T(8,128)(2,1)S(1)} %get-tuple-element.63), channel_id=1, source_target_pairs={{0,3},{1,2},{2,1},{3,0},{4,7},{5,6},{6,5},{7,4},{8,11},{9,10},{10,... | collective-permute-start | bytes 589832 | tf_op jit(solution)/shard_map/ppermute | solution.py:81
  58.1 4.9 %collective-permute-done.19.refs_0_ = bf16[192,512]{1,0:T(8,128)(2,1)S(1)} collective-permute-done((bf16[192,512]{1,0:T(8,128)(2,1)S(1)}, bf16[192,512]{1,0:T(8,128)(2,1)S(1)}, u32[]{:S(2)}, u32[]{:S(2)}) %collective-permute-start.19) | collective-permute-done | bytes 196640 | tf_op jit(solution)/shard_map/ppermute | solution.py:81
  63.0 7.5 %collective-permute-start.18 = (bf16[192,512]{1,0:T(8,128)(2,1)S(1)}, bf16[192,512]{1,0:T(8,128)(2,1)S(1)}, u32[]{:S(2)}, u32[]{:S(2)}) collective-permute-start(bf16[192,512]{1,0:T(8,128)(2,1)S(1)} %get-tuple-element.64), channel_id=1, source_target_pairs={{0,1},{1,0},{2,3},{3,2},{4,5},{5,4},{6,7},{7,6},{8,9},{9,8},{10,11... | collective-permute-start | bytes 589832 | tf_op jit(solution)/shard_map/ppermute | solution.py:81
  70.5 4.3 %collective-permute-done.20.refs_1_ = bf16[192,512]{1,0:T(8,128)(2,1)S(1)} collective-permute-done((bf16[192,512]{1,0:T(8,128)(2,1)S(1)}, bf16[192,512]{1,0:T(8,128)(2,1)S(1)}, u32[]{:S(2)}, u32[]{:S(2)}) %collective-permute-start.20) | collective-permute-done | bytes 196640 | tf_op jit(solution)/shard_map/ppermute | solution.py:81
  74.8 0.9 %shard_map.55.refs_4_ = bf16[192,4096]{1,0:T(8,128)(2,1)} custom-call(bf16[192,512]{1,0:T(8,128)(2,1)S(1)} %collective-permute-done.19.refs_0_, bf16[192,512]{1,0:T(8,128)(2,1)S(1)} %collective-permute-done.20.refs_1_, bf16[192,512]{1,0:T(8,128)(2,1)S(1)} %collective-permute-done.21.refs_2_, bf16[192,512]{1,0:T(8,128)(2,1)S(1)} %get-tuple-element.60.refs_8_.refs_3_), custom_call_target="tpu_custom_call" | custom-call | bytes 1572864 | tf_op jit(solution)/shard_map/pallas_call | solution.py:312
  75.7 2.4 %collective-permute-done.16.refs_0_ = bf16[192,512]{1,0:T(8,128)(2,1)S(1)} collective-permute-done((bf16[192,512]{1,0:T(8,128)(2,1)S(1)}, bf16[192,512]{1,0:T(8,128)(2,1)S(1)}, u32[]{:S(2)}, u32[]{:S(2)}) %collective-permute-start.16) | collective-permute-done | bytes 196640 | tf_op jit(solution)/shard_map/ppermute | solution.py:81
  78.2 4.7 %collective-permute-done.17.refs_1_ = bf16[192,512]{1,0:T(8,128)(2,1)S(1)} collective-permute-done((bf16[192,512]{1,0:T(8,128)(2,1)S(1)}, bf16[192,512]{1,0:T(8,128)(2,1)S(1)}, u32[]{:S(2)}, u32[]{:S(2)}) %collective-permute-start.17) | collective-permute-done | bytes 196640 | tf_op jit(solution)/shard_map/ppermute | solution.py:81
  82.9 0.9 %shard_map.56 = bf16[192,4096]{1,0:T(8,128)(2,1)} custom-call(bf16[192,512]{1,0:T(8,128)(2,1)S(1)} %collective-permute-done.16.refs_0_, bf16[192,512]{1,0:T(8,128)(2,1)S(1)} %collective-permute-done.17.refs_1_, bf16[192,512]{1,0:T(8,128)(2,1)S(1)} %collective-permute-done.18.refs_2_, ...), custom_call_target="tpu_custom_call", output_to_operand_aliasing={{}: (4, {})} | custom-call | bytes 1572864 | tf_op jit(solution)/shard_map/pallas_call | solution.py:312
  (36 shorter events, 5.2 us)
Async XLA Ops:
  0.0 1.2 %copy-start = (bf16[128,4096]{1,0:T(8,128)(2,1)S(1)}, bf16[128,4096]{1,0:T(8,128)(2,1)}, u32[]{:S(2)}) copy-start(bf16[128,4096]{1,0:T(8,128)(2,1)} %q_ref.3) | copy-start | bytes 3145732
  1.2 0.9 %copy-start.1 = (bf16[128,1024]{1,0:T(8,128)(2,1)S(1)}, bf16[128,1024]{1,0:T(8,128)(2,1)}, u32[]{:S(2)}) copy-start(bf16[128,1024]{1,0:T(8,128)(2,1)} %kv_ref.3) | copy-start | bytes 786436
  2.2 7.0 %copy-start.3 = (s32[4096,1]{0,1:T(1,128)S(1)}, s32[4096,1]{0,1:T(1,128)}, u32[]{:S(2)}) copy-start(s32[4096,1]{0,1:T(1,128)} %param.6) | copy-start | bytes 49156
  2.5 18.0 %collective-permute-start.3 = (bf16[128,768]{1,0:T(8,128)(2,1)S(1)}, bf16[128,768]{1,0:T(8,128)(2,1)S(1)}, u32[]{:S(2)}, u32[]{:S(2)}) collective-permute-start(bf16[128,768]{1,0:T(8,128)(2,1)S(1)} %get-tuple-element.45), channel_id=1, source_target_pairs={{0,1},{1,0},{2,3},{3,2},{4,5},{5,4},{6,7},{7,6},{8,9},{9,8},{10,11... | collective-permute-start | bytes 589832 | tf_op jit(solution)/shard_map/ppermute | solution.py:81
  4.1 16.4 %collective-permute-start.4 = (bf16[128,768]{1,0:T(8,128)(2,1)S(1)}, bf16[128,768]{1,0:T(8,128)(2,1)S(1)}, u32[]{:S(2)}, u32[]{:S(2)}) collective-permute-start(bf16[128,768]{1,0:T(8,128)(2,1)S(1)} %get-tuple-element.46), channel_id=1, source_target_pairs={{0,2},{1,3},{2,0},{3,1},{4,6},{5,7},{6,4},{7,5},{8,10},{9,11},{10,... | collective-permute-start | bytes 589832 | tf_op jit(solution)/shard_map/ppermute | solution.py:81
  4.5 18.6 %collective-permute-start.5 = (bf16[128,768]{1,0:T(8,128)(2,1)S(1)}, bf16[128,768]{1,0:T(8,128)(2,1)S(1)}, u32[]{:S(2)}, u32[]{:S(2)}) collective-permute-start(bf16[128,768]{1,0:T(8,128)(2,1)S(1)} %get-tuple-element.47), channel_id=1, source_target_pairs={{0,3},{1,2},{2,1},{3,0},{4,7},{5,6},{6,5},{7,4},{8,11},{9,10},{10,... | collective-permute-start | bytes 589832 | tf_op jit(solution)/shard_map/ppermute | solution.py:81
  6.2 14.3 %collective-permute-start = (bf16[128,512]{1,0:T(8,128)(2,1)S(1)}, bf16[128,512]{1,0:T(8,128)(2,1)S(1)}, u32[]{:S(2)}, u32[]{:S(2)}) collective-permute-start(bf16[128,512]{1,0:T(8,128)(2,1)S(1)} %get-tuple-element.42), channel_id=1, source_target_pairs={{0,1},{1,0},{2,3},{3,2},{4,5},{5,4},{6,7},{7,6},{8,9},{9,8},{10,11... | collective-permute-start | bytes 393224 | tf_op jit(solution)/shard_map/ppermute | solution.py:81
  23.1 14.6 %copy-start.2 = (s32[1,768]{1,0:T(1,128)S(1)}, s32[1,768]{1,0:T(1,128)}, u32[]{:S(2)}) copy-start(s32[1,768]{1,0:T(1,128)} %refs_2_.3) | copy-start | bytes 9220
  23.6 1.6 %collective-permute-start.6 = (bf16[192,768]{1,0:T(8,128)(2,1)S(1)}, bf16[192,768]{1,0:T(8,128)(2,1)S(1)}, u32[]{:S(2)}, u32[]{:S(2)}) collective-permute-start(bf16[192,768]{1,0:T(8,128)(2,1)S(1)} %get-tuple-element.48), channel_id=1, source_target_pairs={{0,4},{4,0},{8,12},{12,8},{16,20},{20,16},{24,28},{28,24},{1,5},{5... | collective-permute-start | bytes 884744 | tf_op jit(solution)/shard_map/ppermute | solution.py:184
  23.7 2.0 %collective-permute-start.7 = (bf16[192,768]{1,0:T(8,128)(2,1)S(1)}, bf16[192,768]{1,0:T(8,128)(2,1)S(1)}, u32[]{:S(2)}, u32[]{:S(2)}) collective-permute-start(bf16[192,768]{1,0:T(8,128)(2,1)S(1)} %get-tuple-element.49), channel_id=1, source_target_pairs={{0,4},{4,0},{8,12},{12,8},{16,20},{20,16},{24,28},{28,24},{1,5},{5... | collective-permute-start | bytes 884744 | tf_op jit(solution)/shard_map/ppermute | solution.py:184
  24.2 9.5 %collective-permute-start.1 = (bf16[128,512]{1,0:T(8,128)(2,1)S(1)}, bf16[128,512]{1,0:T(8,128)(2,1)S(1)}, u32[]{:S(2)}, u32[]{:S(2)}) collective-permute-start(bf16[128,512]{1,0:T(8,128)(2,1)S(1)} %get-tuple-element.43), channel_id=1, source_target_pairs={{0,2},{1,3},{2,0},{3,1},{4,6},{5,7},{6,4},{7,5},{8,10},{9,11},{10,... | collective-permute-start | bytes 393224 | tf_op jit(solution)/shard_map/ppermute | solution.py:81
  24.2 12.6 %collective-permute-start.2 = (bf16[128,512]{1,0:T(8,128)(2,1)S(1)}, bf16[128,512]{1,0:T(8,128)(2,1)S(1)}, u32[]{:S(2)}, u32[]{:S(2)}) collective-permute-start(bf16[128,512]{1,0:T(8,128)(2,1)S(1)} %get-tuple-element.44), channel_id=1, source_target_pairs={{0,3},{1,2},{2,1},{3,0},{4,7},{5,6},{6,5},{7,4},{8,11},{9,10},{10,... | collective-permute-start | bytes 393224 | tf_op jit(solution)/shard_map/ppermute | solution.py:81
  26.1 15.3 %collective-permute-start.13 = (bf16[192,768]{1,0:T(8,128)(2,1)S(1)}, bf16[192,768]{1,0:T(8,128)(2,1)S(1)}, u32[]{:S(2)}, u32[]{:S(2)}) collective-permute-start(bf16[192,768]{1,0:T(8,128)(2,1)S(1)} %get-tuple-element.57), channel_id=1, source_target_pairs={{0,8},{4,12},{8,0},{12,4},{16,24},{20,28},{24,16},{28,20},{1,9},{5... | collective-permute-start | bytes 884744 | tf_op jit(solution)/shard_map/ppermute | solution.py:81
  26.7 16.1 %collective-permute-start.14 = (bf16[192,768]{1,0:T(8,128)(2,1)S(1)}, bf16[192,768]{1,0:T(8,128)(2,1)S(1)}, u32[]{:S(2)}, u32[]{:S(2)}) collective-permute-start(bf16[192,768]{1,0:T(8,128)(2,1)S(1)} %get-tuple-element.58), channel_id=1, source_target_pairs={{0,16},{4,20},{8,24},{12,28},{16,0},{20,4},{24,8},{28,12},{1,17},{... | collective-permute-start | bytes 884744 | tf_op jit(solution)/shard_map/ppermute | solution.py:81
  28.2 14.6 %collective-permute-start.15 = (bf16[192,768]{1,0:T(8,128)(2,1)S(1)}, bf16[192,768]{1,0:T(8,128)(2,1)S(1)}, u32[]{:S(2)}, u32[]{:S(2)}) collective-permute-start(bf16[192,768]{1,0:T(8,128)(2,1)S(1)} %get-tuple-element.59), channel_id=1, source_target_pairs={{0,24},{4,28},{8,16},{12,20},{16,8},{20,12},{24,0},{28,4},{1,25},{... | collective-permute-start | bytes 884744 | tf_op jit(solution)/shard_map/ppermute | solution.py:81
  37.1 1.5 %collective-permute-start.8 = (bf16[192,512]{1,0:T(8,128)(2,1)S(1)}, bf16[192,512]{1,0:T(8,128)(2,1)S(1)}, u32[]{:S(2)}, u32[]{:S(2)}) collective-permute-start(bf16[192,512]{1,0:T(8,128)(2,1)S(1)} %get-tuple-element.51), channel_id=1, source_target_pairs={{0,4},{4,0},{8,12},{12,8},{16,20},{20,16},{24,28},{28,24},{1,5},{5... | collective-permute-start | bytes 589832 | tf_op jit(solution)/shard_map/ppermute | solution.py:184
  37.2 1.7 %collective-permute-start.9 = (bf16[192,512]{1,0:T(8,128)(2,1)S(1)}, bf16[192,512]{1,0:T(8,128)(2,1)S(1)}, u32[]{:S(2)}, u32[]{:S(2)}) collective-permute-start(bf16[192,512]{1,0:T(8,128)(2,1)S(1)} %get-tuple-element.52), channel_id=1, source_target_pairs={{0,4},{4,0},{8,12},{12,8},{16,20},{20,16},{24,28},{28,24},{1,5},{5... | collective-permute-start | bytes 589832 | tf_op jit(solution)/shard_map/ppermute | solution.py:184
  39.3 12.1 %collective-permute-start.10 = (bf16[192,512]{1,0:T(8,128)(2,1)S(1)}, bf16[192,512]{1,0:T(8,128)(2,1)S(1)}, u32[]{:S(2)}, u32[]{:S(2)}) collective-permute-start(bf16[192,512]{1,0:T(8,128)(2,1)S(1)} %get-tuple-element.54), channel_id=1, source_target_pairs={{0,8},{4,12},{8,0},{12,4},{16,24},{20,28},{24,16},{28,20},{1,9},{5... | collective-permute-start | bytes 589832 | tf_op jit(solution)/shard_map/ppermute | solution.py:81
  39.9 11.5 %collective-permute-start.11 = (bf16[192,512]{1,0:T(8,128)(2,1)S(1)}, bf16[192,512]{1,0:T(8,128)(2,1)S(1)}, u32[]{:S(2)}, u32[]{:S(2)}) collective-permute-start(bf16[192,512]{1,0:T(8,128)(2,1)S(1)} %get-tuple-element.55), channel_id=1, source_target_pairs={{0,16},{4,20},{8,24},{12,28},{16,0},{20,4},{24,8},{28,12},{1,17},{... | collective-permute-start | bytes 589832 | tf_op jit(solution)/shard_map/ppermute | solution.py:81
  41.4 10.1 %collective-permute-start.12 = (bf16[192,512]{1,0:T(8,128)(2,1)S(1)}, bf16[192,512]{1,0:T(8,128)(2,1)S(1)}, u32[]{:S(2)}, u32[]{:S(2)}) collective-permute-start(bf16[192,512]{1,0:T(8,128)(2,1)S(1)} %get-tuple-element.56), channel_id=1, source_target_pairs={{0,24},{4,28},{8,16},{12,20},{16,8},{20,12},{24,0},{28,4},{1,25},{... | collective-permute-start | bytes 589832 | tf_op jit(solution)/shard_map/ppermute | solution.py:81
  46.4 16.6 %collective-permute-start.19 = (bf16[192,512]{1,0:T(8,128)(2,1)S(1)}, bf16[192,512]{1,0:T(8,128)(2,1)S(1)}, u32[]{:S(2)}, u32[]{:S(2)}) collective-permute-start(bf16[192,512]{1,0:T(8,128)(2,1)S(1)} %get-tuple-element.66), channel_id=1, source_target_pairs={{0,2},{1,3},{2,0},{3,1},{4,6},{5,7},{6,4},{7,5},{8,10},{9,11},{10,... | collective-permute-start | bytes 589832 | tf_op jit(solution)/shard_map/ppermute | solution.py:81
  49.5 25.3 %collective-permute-start.20 = (bf16[192,512]{1,0:T(8,128)(2,1)S(1)}, bf16[192,512]{1,0:T(8,128)(2,1)S(1)}, u32[]{:S(2)}, u32[]{:S(2)}) collective-permute-start(bf16[192,512]{1,0:T(8,128)(2,1)S(1)} %get-tuple-element.67), channel_id=1, source_target_pairs={{0,3},{1,2},{2,1},{3,0},{4,7},{5,6},{6,5},{7,4},{8,11},{9,10},{10,... | collective-permute-start | bytes 589832 | tf_op jit(solution)/shard_map/ppermute | solution.py:81
  51.4 23.4 %collective-permute-start.21 = (bf16[192,512]{1,0:T(8,128)(2,1)S(1)}, bf16[192,512]{1,0:T(8,128)(2,1)S(1)}, u32[]{:S(2)}, u32[]{:S(2)}) collective-permute-start(bf16[192,512]{1,0:T(8,128)(2,1)S(1)} %get-tuple-element.68), channel_id=1, source_target_pairs={{0,1},{1,0},{2,3},{3,2},{4,5},{5,4},{6,7},{7,6},{8,9},{9,8},{10,11... | collective-permute-start | bytes 589832 | tf_op jit(solution)/shard_map/ppermute | solution.py:81
  54.6 23.6 %collective-permute-start.16 = (bf16[192,512]{1,0:T(8,128)(2,1)S(1)}, bf16[192,512]{1,0:T(8,128)(2,1)S(1)}, u32[]{:S(2)}, u32[]{:S(2)}) collective-permute-start(bf16[192,512]{1,0:T(8,128)(2,1)S(1)} %get-tuple-element.62), channel_id=1, source_target_pairs={{0,2},{1,3},{2,0},{3,1},{4,6},{5,7},{6,4},{7,5},{8,10},{9,11},{10,... | collective-permute-start | bytes 589832 | tf_op jit(solution)/shard_map/ppermute | solution.py:81
  56.2 26.7 %collective-permute-start.17 = (bf16[192,512]{1,0:T(8,128)(2,1)S(1)}, bf16[192,512]{1,0:T(8,128)(2,1)S(1)}, u32[]{:S(2)}, u32[]{:S(2)}) collective-permute-start(bf16[192,512]{1,0:T(8,128)(2,1)S(1)} %get-tuple-element.63), channel_id=1, source_target_pairs={{0,3},{1,2},{2,1},{3,0},{4,7},{5,6},{6,5},{7,4},{8,11},{9,10},{10,... | collective-permute-start | bytes 589832 | tf_op jit(solution)/shard_map/ppermute | solution.py:81
  63.0 19.9 %collective-permute-start.18 = (bf16[192,512]{1,0:T(8,128)(2,1)S(1)}, bf16[192,512]{1,0:T(8,128)(2,1)S(1)}, u32[]{:S(2)}, u32[]{:S(2)}) collective-permute-start(bf16[192,512]{1,0:T(8,128)(2,1)S(1)} %get-tuple-element.64), channel_id=1, source_target_pairs={{0,1},{1,0},{2,3},{3,2},{4,5},{5,4},{6,7},{7,6},{8,9},{9,8},{10,11... | collective-permute-start | bytes 589832 | tf_op jit(solution)/shard_map/ppermute | solution.py:81

commit v5 on v4

--- a/solution.py
+++ b/solution.py
@@ -32,8 +32,9 @@
     return [(0, first)] + ([(first, heads_dev - first)] if heads_dev > first else [])
 
 
-def cut_kernel(chunk, ctx_size, with_kv, waits, q_ref, kv_ref, *refs):
+def cut_kernel(chunk, ctx_size, with_kv, waits, q_ref, *refs):
     offset, heads = chunk
+    kv_ref, refs = (refs[0], refs[1:]) if with_kv else (None, refs)
     outs, sem = refs[waits:-1], refs[-1]
     me = lax.axis_index("ctx")
     heads_dev = Q_HEADS // ctx_size
@@ -64,15 +65,17 @@
     rows = q_src.shape[0]
     wide = (chunk[1] + (2 if with_kv else 0)) * HEAD_DIM
     shapes = [jax.ShapeDtypeStruct((rows, wide), jnp.bfloat16)] * ctx_size
+    sources = [q_src, kv_src] if with_kv else [q_src]
+    sources = [pltpu.with_memory_space_constraint(x, pltpu.HBM) for x in sources]
     outs = pl.pallas_call(
         functools.partial(cut_kernel, chunk, ctx_size, with_kv, len(after)),
         out_shape=shapes,
-        in_specs=[ANY] * (2 + len(after)),
+        in_specs=[ANY] * (len(sources) + len(after)),
         out_specs=[VMEM] * len(shapes),
         scratch_shapes=[pltpu.SemaphoreType.DMA((ctx_size * (3 if with_kv else 1),))],
         compiler_params=params(),
         cost_estimate=cost(0, 4 * ctx_size * rows * wide),
-    )(q_src, kv_src, *after)
+    )(*sources, *after)
     return list(outs)
 
 

time: 84 us -> 82.8 us (0.986)
  local copies, waits for them, and re-layouts: 2.85 us -> 0.68 us
  Pallas kernels: 10.5 us -> 12.6 us
  waiting for transfers between devices: 38.8 us -> 37.8 us
    unnamed x9 -> x5, local copies, waits for them, and re-layouts: 2.69 us -> 0.52 us
    pallas_call x2, Pallas kernels: 0.4 us -> 2.44 us  [cut(): pl.pallas_call(functools.partial(cut_kernel, chunk, ctx_size, with_kv, le...]
    ppermute x18, waiting for transfers between devices: 36.5 us -> 35.5 us  [swap(): lax.ppermute(blocks[step], axis, [(j, j ^ step * unit) for j in range(siz...]
  transfers between devices with their start and end apart: 22 -> 22, of which waited for: 13 -> 13; matrix products, arithmetic and copies ran while one was open for 2% -> 2% of each run, Pallas kernels for 11% -> 12%
where the time goes in v5:
time: 82.8 us; the launch traced here: 82.6 us
  waiting for transfers between devices  37.8 us (46%)
  starting transfers between devices  30.8 us (37%)
  Pallas kernels  12.6 us (15%)
    ppermute x18, waiting for transfers between devices, swap(): lax.ppermute(blocks[step], axis, [(j, j ^ step * unit) for j in range(siz...  35.5 us
    ppermute x18, starting transfers between devices, swap(): lax.ppermute(blocks[step], axis, [(j, j ^ step * unit) for j in range(siz...  29.6 us
    pallas_call x2, Pallas kernels, attend(): pl.pallas_call(functools.partial(attend_kernel, heads, doc_most, ctx_size...  6.43 us
    pallas_call x2, Pallas kernels, cut(): pl.pallas_call(functools.partial(cut_kernel, chunk, ctx_size, with_kv, le...  2.44 us
    ppermute x4, waiting for transfers between devices, deliver(): lax.ppermute(part, 'dp', [(j, j ^ 1) for j in range(dp_size)])  2.27 us
    pallas_call x2, Pallas kernels, join(): pl.pallas_call(functools.partial(join_kernel, chunk, ctx_size, steps), ou...  1.81 us
  transfers between devices with their start and end apart: 22, of which 13 were waited for; matrix products, arithmetic and copies ran while one was open for 2% of the time, Pallas kernels for 12%

profile of v5, /device:TPU:18, one launch (start us, length us, event | category | flops | bytes accessed | tf_op | source)
XLA Modules:
  0.0 82.6 jit_solution(17326233087593019387)
XLA Ops:
  0.0 1.3 %shard_map.47 = (bf16[128,768]{1,0:T(8,128)(2,1)S(1)}, bf16[128,768]{1,0:T(8,128)(2,1)S(1)}, bf16[128,768]{1,0:T(8,128)(2,1)S(1)}, bf16[128,768]{1,0:T(8,128)(2,1)S(1)}) custom-call(bf16[128,4096]{1,0:T(8,128)(2,1)} %q_ref.3, bf16[128,1024]{1,0:T(8,128)(2,1)} %refs_0_.1), custom_call_target="tpu_custom_call" | custom-call | bytes 1572864 | tf_op jit(solution)/shard_map/pallas_call | solution.py:70
  1.3 1.6 %collective-permute-start.3 = (bf16[128,768]{1,0:T(8,128)(2,1)S(1)}, bf16[128,768]{1,0:T(8,128)(2,1)S(1)}, u32[]{:S(2)}, u32[]{:S(2)}) collective-permute-start(bf16[128,768]{1,0:T(8,128)(2,1)S(1)} %get-tuple-element.45), channel_id=1, source_target_pairs={{0,1},{1,0},{2,3},{3,2},{4,5},{5,4},{6,7},{7,6},{8,9},{9,8},{10,11... | collective-permute-start | bytes 589832 | tf_op jit(solution)/shard_map/ppermute | solution.py:84
  3.3 1.6 %collective-permute-start.5 = (bf16[128,768]{1,0:T(8,128)(2,1)S(1)}, bf16[128,768]{1,0:T(8,128)(2,1)S(1)}, u32[]{:S(2)}, u32[]{:S(2)}) collective-permute-start(bf16[128,768]{1,0:T(8,128)(2,1)S(1)} %get-tuple-element.47), channel_id=1, source_target_pairs={{0,3},{1,2},{2,1},{3,0},{4,7},{5,6},{6,5},{7,4},{8,11},{9,10},{10,... | collective-permute-start | bytes 589832 | tf_op jit(solution)/shard_map/ppermute | solution.py:84
  4.9 1.1 %shard_map.48 = (bf16[128,512]{1,0:T(8,128)(2,1)S(1)}, bf16[128,512]{1,0:T(8,128)(2,1)S(1)}, bf16[128,512]{1,0:T(8,128)(2,1)S(1)}, bf16[128,512]{1,0:T(8,128)(2,1)S(1)}) custom-call(bf16[128,4096]{1,0:T(8,128)(2,1)} %q_ref.3, bf16[128,768]{1,0:T(8,128)(2,1)S(1)} %get-tuple-element.40.refs_0_.refs_2_), custom_call_target="tpu_custom_call" | custom-call | bytes 1048576 | tf_op jit(solution)/shard_map/pallas_call | solution.py:70
  6.0 2.5 %collective-permute-start = (bf16[128,512]{1,0:T(8,128)(2,1)S(1)}, bf16[128,512]{1,0:T(8,128)(2,1)S(1)}, u32[]{:S(2)}, u32[]{:S(2)}) collective-permute-start(bf16[128,512]{1,0:T(8,128)(2,1)S(1)} %get-tuple-element.42), channel_id=1, source_target_pairs={{0,1},{1,0},{2,3},{3,2},{4,5},{5,4},{6,7},{7,6},{8,9},{9,8},{10,11... | collective-permute-start | bytes 393224 | tf_op jit(solution)/shard_map/ppermute | solution.py:84
  8.6 0.5 broadcast.4
  9.1 0.7 reduce.4
  10.0 9.3 %collective-permute-done.refs_4_.refs_1_.refs_3_ = bf16[128,512]{1,0:T(8,128)(2,1)S(1)} collective-permute-done((bf16[128,512]{1,0:T(8,128)(2,1)S(1)}, bf16[128,512]{1,0:T(8,128)(2,1)S(1)}, u32[]{:S(2)}, u32[]{:S(2)}) %collective-permute-start) | collective-permute-done | bytes 131104 | tf_op jit(solution)/shard_map/ppermute | solution.py:84
  19.3 2.6 %collective-permute-done.5.refs_3_.refs_5_ = bf16[128,768]{1,0:T(8,128)(2,1)S(1)} collective-permute-done((bf16[128,768]{1,0:T(8,128)(2,1)S(1)}, bf16[128,768]{1,0:T(8,128)(2,1)S(1)}, u32[]{:S(2)}, u32[]{:S(2)}) %collective-permute-start.5) | collective-permute-done | bytes 196640 | tf_op jit(solution)/shard_map/ppermute | solution.py:84
  23.4 0.7 collective-permute-done.6.refs_0_
  25.0 0.6 collective-permute-start.13
  25.6 1.5 %collective-permute-start.14 = (bf16[192,768]{1,0:T(8,128)(2,1)S(1)}, bf16[192,768]{1,0:T(8,128)(2,1)S(1)}, u32[]{:S(2)}, u32[]{:S(2)}) collective-permute-start(bf16[192,768]{1,0:T(8,128)(2,1)S(1)} %get-tuple-element.58), channel_id=1, source_target_pairs={{0,16},{4,20},{8,24},{12,28},{16,0},{20,4},{24,8},{28,12},{1,17},{... | collective-permute-start | bytes 884744 | tf_op jit(solution)/shard_map/ppermute | solution.py:84
  27.1 1.4 %collective-permute-start.15 = (bf16[192,768]{1,0:T(8,128)(2,1)S(1)}, bf16[192,768]{1,0:T(8,128)(2,1)S(1)}, u32[]{:S(2)}, u32[]{:S(2)}) collective-permute-start(bf16[192,768]{1,0:T(8,128)(2,1)S(1)} %get-tuple-element.59), channel_id=1, source_target_pairs={{0,24},{4,28},{8,16},{12,20},{16,8},{20,12},{24,0},{28,4},{1,25},{... | collective-permute-start | bytes 884744 | tf_op jit(solution)/shard_map/ppermute | solution.py:84
  28.5 3.9 %collective-permute-done.1.refs_2_.refs_4_ = bf16[128,512]{1,0:T(8,128)(2,1)S(1)} collective-permute-done((bf16[128,512]{1,0:T(8,128)(2,1)S(1)}, bf16[128,512]{1,0:T(8,128)(2,1)S(1)}, u32[]{:S(2)}, u32[]{:S(2)}) %collective-permute-start.1) | collective-permute-done | bytes 131104 | tf_op jit(solution)/shard_map/ppermute | solution.py:84
  32.5 3.1 %collective-permute-done.2.refs_3_.refs_5_ = bf16[128,512]{1,0:T(8,128)(2,1)S(1)} collective-permute-done((bf16[128,512]{1,0:T(8,128)(2,1)S(1)}, bf16[128,512]{1,0:T(8,128)(2,1)S(1)}, u32[]{:S(2)}, u32[]{:S(2)}) %collective-permute-start.2) | collective-permute-done | bytes 131104 | tf_op jit(solution)/shard_map/ppermute | solution.py:84
  36.5 0.9 %collective-permute-done.8.refs_0_ = bf16[192,512]{1,0:T(8,128)(2,1)S(1)} collective-permute-done((bf16[192,512]{1,0:T(8,128)(2,1)S(1)}, bf16[192,512]{1,0:T(8,128)(2,1)S(1)}, u32[]{:S(2)}, u32[]{:S(2)}) %collective-permute-start.8) | collective-permute-done | bytes 196640 | tf_op jit(solution)/shard_map/ppermute | solution.py:187
  38.1 0.6 collective-permute-start.10
  38.7 1.5 %collective-permute-start.11 = (bf16[192,512]{1,0:T(8,128)(2,1)S(1)}, bf16[192,512]{1,0:T(8,128)(2,1)S(1)}, u32[]{:S(2)}, u32[]{:S(2)}) collective-permute-start(bf16[192,512]{1,0:T(8,128)(2,1)S(1)} %get-tuple-element.55), channel_id=1, source_target_pairs={{0,16},{4,20},{8,24},{12,28},{16,0},{20,4},{24,8},{28,12},{1,17},{... | collective-permute-start | bytes 589832 | tf_op jit(solution)/shard_map/ppermute | solution.py:84
  40.2 1.4 %collective-permute-start.12 = (bf16[192,512]{1,0:T(8,128)(2,1)S(1)}, bf16[192,512]{1,0:T(8,128)(2,1)S(1)}, u32[]{:S(2)}, u32[]{:S(2)}) collective-permute-start(bf16[192,512]{1,0:T(8,128)(2,1)S(1)} %get-tuple-element.56), channel_id=1, source_target_pairs={{0,24},{4,28},{8,16},{12,20},{16,8},{20,12},{24,0},{28,4},{1,25},{... | collective-permute-start | bytes 589832 | tf_op jit(solution)/shard_map/ppermute | solution.py:84
  41.8 3.4 %shard_map.53 = (bf16[192,512]{1,0:T(8,128)(2,1)S(1)}, bf16[192,512]{1,0:T(8,128)(2,1)S(1)}, bf16[192,512]{1,0:T(8,128)(2,1)S(1)}, bf16[192,512]{1,0:T(8,128)(2,1)S(1)}, bf16[768,256]{1,0:T(8,128)(2,1)S(1)}) custom-call(s32[1,768]{1,0:T(1,128)S(1)} %get-tuple-element.37.refs_0_, s32[1,128]{1,0:T(1,128)S(1)} %get-tuple-element.38.refs_1_, ...), custom_call_target="tpu_custom_call" | custom-call | flops 1811939328 | bytes 3145728 | tf_op jit(solution)/shard_map/pallas_call | solution.py:269
  45.2 3.1 %collective-permute-start.19 = (bf16[192,512]{1,0:T(8,128)(2,1)S(1)}, bf16[192,512]{1,0:T(8,128)(2,1)S(1)}, u32[]{:S(2)}, u32[]{:S(2)}) collective-permute-start(bf16[192,512]{1,0:T(8,128)(2,1)S(1)} %get-tuple-element.66), channel_id=1, source_target_pairs={{0,2},{1,3},{2,0},{3,1},{4,6},{5,7},{6,4},{7,5},{8,10},{9,11},{10,... | collective-permute-start | bytes 589832 | tf_op jit(solution)/shard_map/ppermute | solution.py:84
  48.3 1.9 %collective-permute-start.20 = (bf16[192,512]{1,0:T(8,128)(2,1)S(1)}, bf16[192,512]{1,0:T(8,128)(2,1)S(1)}, u32[]{:S(2)}, u32[]{:S(2)}) collective-permute-start(bf16[192,512]{1,0:T(8,128)(2,1)S(1)} %get-tuple-element.67), channel_id=1, source_target_pairs={{0,3},{1,2},{2,1},{3,0},{4,7},{5,6},{6,5},{7,4},{8,11},{9,10},{10,... | collective-permute-start | bytes 589832 | tf_op jit(solution)/shard_map/ppermute | solution.py:84
  50.4 3.1 %shard_map.54 = (bf16[192,512]{1,0:T(8,128)(2,1)S(1)}, bf16[192,512]{1,0:T(8,128)(2,1)S(1)}, bf16[192,512]{1,0:T(8,128)(2,1)S(1)}, bf16[192,512]{1,0:T(8,128)(2,1)S(1)}) custom-call(s32[1,768]{1,0:T(1,128)S(1)} %get-tuple-element.37.refs_0_, s32[1,128]{1,0:T(1,128)S(1)} %get-tuple-element.38.refs_1_, s32[1,768]{1,0:T(1,128)S(1)} %copy-done, ...), custom_call_target="tpu_custom_call" | custom-call | flops 1509949440 | bytes 3145728 | tf_op jit(solution)/shard_map/pallas_call | solution.py:269
  53.5 1.6 %collective-permute-start.16 = (bf16[192,512]{1,0:T(8,128)(2,1)S(1)}, bf16[192,512]{1,0:T(8,128)(2,1)S(1)}, u32[]{:S(2)}, u32[]{:S(2)}) collective-permute-start(bf16[192,512]{1,0:T(8,128)(2,1)S(1)} %get-tuple-element.62), channel_id=1, source_target_pairs={{0,2},{1,3},{2,0},{3,1},{4,6},{5,7},{6,4},{7,5},{8,10},{9,11},{10,... | collective-permute-start | bytes 589832 | tf_op jit(solution)/shard_map/ppermute | solution.py:84
  55.1 1.8 %collective-permute-start.17 = (bf16[192,512]{1,0:T(8,128)(2,1)S(1)}, bf16[192,512]{1,0:T(8,128)(2,1)S(1)}, u32[]{:S(2)}, u32[]{:S(2)}) collective-permute-start(bf16[192,512]{1,0:T(8,128)(2,1)S(1)} %get-tuple-element.63), channel_id=1, source_target_pairs={{0,3},{1,2},{2,1},{3,0},{4,7},{5,6},{6,5},{7,4},{8,11},{9,10},{10,... | collective-permute-start | bytes 589832 | tf_op jit(solution)/shard_map/ppermute | solution.py:84
  56.9 4.9 %collective-permute-done.19.refs_0_ = bf16[192,512]{1,0:T(8,128)(2,1)S(1)} collective-permute-done((bf16[192,512]{1,0:T(8,128)(2,1)S(1)}, bf16[192,512]{1,0:T(8,128)(2,1)S(1)}, u32[]{:S(2)}, u32[]{:S(2)}) %collective-permute-start.19) | collective-permute-done | bytes 196640 | tf_op jit(solution)/shard_map/ppermute | solution.py:84
  61.9 7.5 %collective-permute-start.18 = (bf16[192,512]{1,0:T(8,128)(2,1)S(1)}, bf16[192,512]{1,0:T(8,128)(2,1)S(1)}, u32[]{:S(2)}, u32[]{:S(2)}) collective-permute-start(bf16[192,512]{1,0:T(8,128)(2,1)S(1)} %get-tuple-element.64), channel_id=1, source_target_pairs={{0,1},{1,0},{2,3},{3,2},{4,5},{5,4},{6,7},{7,6},{8,9},{9,8},{10,11... | collective-permute-start | bytes 589832 | tf_op jit(solution)/shard_map/ppermute | solution.py:84
  69.4 4.3 %collective-permute-done.20.refs_1_ = bf16[192,512]{1,0:T(8,128)(2,1)S(1)} collective-permute-done((bf16[192,512]{1,0:T(8,128)(2,1)S(1)}, bf16[192,512]{1,0:T(8,128)(2,1)S(1)}, u32[]{:S(2)}, u32[]{:S(2)}) %collective-permute-start.20) | collective-permute-done | bytes 196640 | tf_op jit(solution)/shard_map/ppermute | solution.py:84
  73.7 0.9 %shard_map.55.refs_4_ = bf16[192,4096]{1,0:T(8,128)(2,1)} custom-call(bf16[192,512]{1,0:T(8,128)(2,1)S(1)} %collective-permute-done.19.refs_0_, bf16[192,512]{1,0:T(8,128)(2,1)S(1)} %collective-permute-done.20.refs_1_, bf16[192,512]{1,0:T(8,128)(2,1)S(1)} %collective-permute-done.21.refs_2_, bf16[192,512]{1,0:T(8,128)(2,1)S(1)} %get-tuple-element.60.refs_8_.refs_3_), custom_call_target="tpu_custom_call" | custom-call | bytes 1572864 | tf_op jit(solution)/shard_map/pallas_call | solution.py:315
  74.6 2.4 %collective-permute-done.16.refs_0_ = bf16[192,512]{1,0:T(8,128)(2,1)S(1)} collective-permute-done((bf16[192,512]{1,0:T(8,128)(2,1)S(1)}, bf16[192,512]{1,0:T(8,128)(2,1)S(1)}, u32[]{:S(2)}, u32[]{:S(2)}) %collective-permute-start.16) | collective-permute-done | bytes 196640 | tf_op jit(solution)/shard_map/ppermute | solution.py:84
  77.0 4.7 %collective-permute-done.17.refs_1_ = bf16[192,512]{1,0:T(8,128)(2,1)S(1)} collective-permute-done((bf16[192,512]{1,0:T(8,128)(2,1)S(1)}, bf16[192,512]{1,0:T(8,128)(2,1)S(1)}, u32[]{:S(2)}, u32[]{:S(2)}) %collective-permute-start.17) | collective-permute-done | bytes 196640 | tf_op jit(solution)/shard_map/ppermute | solution.py:84
  81.7 0.9 %shard_map.56 = bf16[192,4096]{1,0:T(8,128)(2,1)} custom-call(bf16[192,512]{1,0:T(8,128)(2,1)S(1)} %collective-permute-done.16.refs_0_, bf16[192,512]{1,0:T(8,128)(2,1)S(1)} %collective-permute-done.17.refs_1_, bf16[192,512]{1,0:T(8,128)(2,1)S(1)} %collective-permute-done.18.refs_2_, ...), custom_call_target="tpu_custom_call", output_to_operand_aliasing={{}: (4, {})} | custom-call | bytes 1572864 | tf_op jit(solution)/shard_map/pallas_call | solution.py:315
  (32 shorter events, 4.8 us)
Async XLA Ops:
  0.0 9.1 %copy-start.1 = (s32[4096,1]{0,1:T(1,128)S(1)}, s32[4096,1]{0,1:T(1,128)}, u32[]{:S(2)}) copy-start(s32[4096,1]{0,1:T(1,128)} %param.6) | copy-start | bytes 49156
  1.3 18.0 %collective-permute-start.3 = (bf16[128,768]{1,0:T(8,128)(2,1)S(1)}, bf16[128,768]{1,0:T(8,128)(2,1)S(1)}, u32[]{:S(2)}, u32[]{:S(2)}) collective-permute-start(bf16[128,768]{1,0:T(8,128)(2,1)S(1)} %get-tuple-element.45), channel_id=1, source_target_pairs={{0,1},{1,0},{2,3},{3,2},{4,5},{5,4},{6,7},{7,6},{8,9},{9,8},{10,11... | collective-permute-start | bytes 589832 | tf_op jit(solution)/shard_map/ppermute | solution.py:84
  3.0 16.4 %collective-permute-start.4 = (bf16[128,768]{1,0:T(8,128)(2,1)S(1)}, bf16[128,768]{1,0:T(8,128)(2,1)S(1)}, u32[]{:S(2)}, u32[]{:S(2)}) collective-permute-start(bf16[128,768]{1,0:T(8,128)(2,1)S(1)} %get-tuple-element.46), channel_id=1, source_target_pairs={{0,2},{1,3},{2,0},{3,1},{4,6},{5,7},{6,4},{7,5},{8,10},{9,11},{10,... | collective-permute-start | bytes 589832 | tf_op jit(solution)/shard_map/ppermute | solution.py:84
  3.3 18.6 %collective-permute-start.5 = (bf16[128,768]{1,0:T(8,128)(2,1)S(1)}, bf16[128,768]{1,0:T(8,128)(2,1)S(1)}, u32[]{:S(2)}, u32[]{:S(2)}) collective-permute-start(bf16[128,768]{1,0:T(8,128)(2,1)S(1)} %get-tuple-element.47), channel_id=1, source_target_pairs={{0,3},{1,2},{2,1},{3,0},{4,7},{5,6},{6,5},{7,4},{8,11},{9,10},{10,... | collective-permute-start | bytes 589832 | tf_op jit(solution)/shard_map/ppermute | solution.py:84
  6.0 13.3 %collective-permute-start = (bf16[128,512]{1,0:T(8,128)(2,1)S(1)}, bf16[128,512]{1,0:T(8,128)(2,1)S(1)}, u32[]{:S(2)}, u32[]{:S(2)}) collective-permute-start(bf16[128,512]{1,0:T(8,128)(2,1)S(1)} %get-tuple-element.42), channel_id=1, source_target_pairs={{0,1},{1,0},{2,3},{3,2},{4,5},{5,4},{6,7},{7,6},{8,9},{9,8},{10,11... | collective-permute-start | bytes 393224 | tf_op jit(solution)/shard_map/ppermute | solution.py:84
  21.9 14.6 %copy-start = (s32[1,768]{1,0:T(1,128)S(1)}, s32[1,768]{1,0:T(1,128)}, u32[]{:S(2)}) copy-start(s32[1,768]{1,0:T(1,128)} %refs_2_.3) | copy-start | bytes 9220
  22.4 1.6 %collective-permute-start.6 = (bf16[192,768]{1,0:T(8,128)(2,1)S(1)}, bf16[192,768]{1,0:T(8,128)(2,1)S(1)}, u32[]{:S(2)}, u32[]{:S(2)}) collective-permute-start(bf16[192,768]{1,0:T(8,128)(2,1)S(1)} %get-tuple-element.48), channel_id=1, source_target_pairs={{0,4},{4,0},{8,12},{12,8},{16,20},{20,16},{24,28},{28,24},{1,5},{5... | collective-permute-start | bytes 884744 | tf_op jit(solution)/shard_map/ppermute | solution.py:187
  22.5 2.0 %collective-permute-start.7 = (bf16[192,768]{1,0:T(8,128)(2,1)S(1)}, bf16[192,768]{1,0:T(8,128)(2,1)S(1)}, u32[]{:S(2)}, u32[]{:S(2)}) collective-permute-start(bf16[192,768]{1,0:T(8,128)(2,1)S(1)} %get-tuple-element.49), channel_id=1, source_target_pairs={{0,4},{4,0},{8,12},{12,8},{16,20},{20,16},{24,28},{28,24},{1,5},{5... | collective-permute-start | bytes 884744 | tf_op jit(solution)/shard_map/ppermute | solution.py:187
  23.0 9.5 %collective-permute-start.1 = (bf16[128,512]{1,0:T(8,128)(2,1)S(1)}, bf16[128,512]{1,0:T(8,128)(2,1)S(1)}, u32[]{:S(2)}, u32[]{:S(2)}) collective-permute-start(bf16[128,512]{1,0:T(8,128)(2,1)S(1)} %get-tuple-element.43), channel_id=1, source_target_pairs={{0,2},{1,3},{2,0},{3,1},{4,6},{5,7},{6,4},{7,5},{8,10},{9,11},{10,... | collective-permute-start | bytes 393224 | tf_op jit(solution)/shard_map/ppermute | solution.py:84
  23.0 12.6 %collective-permute-start.2 = (bf16[128,512]{1,0:T(8,128)(2,1)S(1)}, bf16[128,512]{1,0:T(8,128)(2,1)S(1)}, u32[]{:S(2)}, u32[]{:S(2)}) collective-permute-start(bf16[128,512]{1,0:T(8,128)(2,1)S(1)} %get-tuple-element.44), channel_id=1, source_target_pairs={{0,3},{1,2},{2,1},{3,0},{4,7},{5,6},{6,5},{7,4},{8,11},{9,10},{10,... | collective-permute-start | bytes 393224 | tf_op jit(solution)/shard_map/ppermute | solution.py:84
  25.0 15.3 %collective-permute-start.13 = (bf16[192,768]{1,0:T(8,128)(2,1)S(1)}, bf16[192,768]{1,0:T(8,128)(2,1)S(1)}, u32[]{:S(2)}, u32[]{:S(2)}) collective-permute-start(bf16[192,768]{1,0:T(8,128)(2,1)S(1)} %get-tuple-element.57), channel_id=1, source_target_pairs={{0,8},{4,12},{8,0},{12,4},{16,24},{20,28},{24,16},{28,20},{1,9},{5... | collective-permute-start | bytes 884744 | tf_op jit(solution)/shard_map/ppermute | solution.py:84
  25.6 16.1 %collective-permute-start.14 = (bf16[192,768]{1,0:T(8,128)(2,1)S(1)}, bf16[192,768]{1,0:T(8,128)(2,1)S(1)}, u32[]{:S(2)}, u32[]{:S(2)}) collective-permute-start(bf16[192,768]{1,0:T(8,128)(2,1)S(1)} %get-tuple-element.58), channel_id=1, source_target_pairs={{0,16},{4,20},{8,24},{12,28},{16,0},{20,4},{24,8},{28,12},{1,17},{... | collective-permute-start | bytes 884744 | tf_op jit(solution)/shard_map/ppermute | solution.py:84
  27.1 14.6 %collective-permute-start.15 = (bf16[192,768]{1,0:T(8,128)(2,1)S(1)}, bf16[192,768]{1,0:T(8,128)(2,1)S(1)}, u32[]{:S(2)}, u32[]{:S(2)}) collective-permute-start(bf16[192,768]{1,0:T(8,128)(2,1)S(1)} %get-tuple-element.59), channel_id=1, source_target_pairs={{0,24},{4,28},{8,16},{12,20},{16,8},{20,12},{24,0},{28,4},{1,25},{... | collective-permute-start | bytes 884744 | tf_op jit(solution)/shard_map/ppermute | solution.py:84
  36.0 1.5 %collective-permute-start.8 = (bf16[192,512]{1,0:T(8,128)(2,1)S(1)}, bf16[192,512]{1,0:T(8,128)(2,1)S(1)}, u32[]{:S(2)}, u32[]{:S(2)}) collective-permute-start(bf16[192,512]{1,0:T(8,128)(2,1)S(1)} %get-tuple-element.51), channel_id=1, source_target_pairs={{0,4},{4,0},{8,12},{12,8},{16,20},{20,16},{24,28},{28,24},{1,5},{5... | collective-permute-start | bytes 589832 | tf_op jit(solution)/shard_map/ppermute | solution.py:187
  36.0 1.7 %collective-permute-start.9 = (bf16[192,512]{1,0:T(8,128)(2,1)S(1)}, bf16[192,512]{1,0:T(8,128)(2,1)S(1)}, u32[]{:S(2)}, u32[]{:S(2)}) collective-permute-start(bf16[192,512]{1,0:T(8,128)(2,1)S(1)} %get-tuple-element.52), channel_id=1, source_target_pairs={{0,4},{4,0},{8,12},{12,8},{16,20},{20,16},{24,28},{28,24},{1,5},{5... | collective-permute-start | bytes 589832 | tf_op jit(solution)/shard_map/ppermute | solution.py:187
  38.1 12.1 %collective-permute-start.10 = (bf16[192,512]{1,0:T(8,128)(2,1)S(1)}, bf16[192,512]{1,0:T(8,128)(2,1)S(1)}, u32[]{:S(2)}, u32[]{:S(2)}) collective-permute-start(bf16[192,512]{1,0:T(8,128)(2,1)S(1)} %get-tuple-element.54), channel_id=1, source_target_pairs={{0,8},{4,12},{8,0},{12,4},{16,24},{20,28},{24,16},{28,20},{1,9},{5... | collective-permute-start | bytes 589832 | tf_op jit(solution)/shard_map/ppermute | solution.py:84
  38.7 11.6 %collective-permute-start.11 = (bf16[192,512]{1,0:T(8,128)(2,1)S(1)}, bf16[192,512]{1,0:T(8,128)(2,1)S(1)}, u32[]{:S(2)}, u32[]{:S(2)}) collective-permute-start(bf16[192,512]{1,0:T(8,128)(2,1)S(1)} %get-tuple-element.55), channel_id=1, source_target_pairs={{0,16},{4,20},{8,24},{12,28},{16,0},{20,4},{24,8},{28,12},{1,17},{... | collective-permute-start | bytes 589832 | tf_op jit(solution)/shard_map/ppermute | solution.py:84
  40.2 10.1 %collective-permute-start.12 = (bf16[192,512]{1,0:T(8,128)(2,1)S(1)}, bf16[192,512]{1,0:T(8,128)(2,1)S(1)}, u32[]{:S(2)}, u32[]{:S(2)}) collective-permute-start(bf16[192,512]{1,0:T(8,128)(2,1)S(1)} %get-tuple-element.56), channel_id=1, source_target_pairs={{0,24},{4,28},{8,16},{12,20},{16,8},{20,12},{24,0},{28,4},{1,25},{... | collective-permute-start | bytes 589832 | tf_op jit(solution)/shard_map/ppermute | solution.py:84
  45.2 16.6 %collective-permute-start.19 = (bf16[192,512]{1,0:T(8,128)(2,1)S(1)}, bf16[192,512]{1,0:T(8,128)(2,1)S(1)}, u32[]{:S(2)}, u32[]{:S(2)}) collective-permute-start(bf16[192,512]{1,0:T(8,128)(2,1)S(1)} %get-tuple-element.66), channel_id=1, source_target_pairs={{0,2},{1,3},{2,0},{3,1},{4,6},{5,7},{6,4},{7,5},{8,10},{9,11},{10,... | collective-permute-start | bytes 589832 | tf_op jit(solution)/shard_map/ppermute | solution.py:84
  48.3 25.3 %collective-permute-start.20 = (bf16[192,512]{1,0:T(8,128)(2,1)S(1)}, bf16[192,512]{1,0:T(8,128)(2,1)S(1)}, u32[]{:S(2)}, u32[]{:S(2)}) collective-permute-start(bf16[192,512]{1,0:T(8,128)(2,1)S(1)} %get-tuple-element.67), channel_id=1, source_target_pairs={{0,3},{1,2},{2,1},{3,0},{4,7},{5,6},{6,5},{7,4},{8,11},{9,10},{10,... | collective-permute-start | bytes 589832 | tf_op jit(solution)/shard_map/ppermute | solution.py:84
  50.3 23.4 %collective-permute-start.21 = (bf16[192,512]{1,0:T(8,128)(2,1)S(1)}, bf16[192,512]{1,0:T(8,128)(2,1)S(1)}, u32[]{:S(2)}, u32[]{:S(2)}) collective-permute-start(bf16[192,512]{1,0:T(8,128)(2,1)S(1)} %get-tuple-element.68), channel_id=1, source_target_pairs={{0,1},{1,0},{2,3},{3,2},{4,5},{5,4},{6,7},{7,6},{8,9},{9,8},{10,11... | collective-permute-start | bytes 589832 | tf_op jit(solution)/shard_map/ppermute | solution.py:84
  53.5 23.6 %collective-permute-start.16 = (bf16[192,512]{1,0:T(8,128)(2,1)S(1)}, bf16[192,512]{1,0:T(8,128)(2,1)S(1)}, u32[]{:S(2)}, u32[]{:S(2)}) collective-permute-start(bf16[192,512]{1,0:T(8,128)(2,1)S(1)} %get-tuple-element.62), channel_id=1, source_target_pairs={{0,2},{1,3},{2,0},{3,1},{4,6},{5,7},{6,4},{7,5},{8,10},{9,11},{10,... | collective-permute-start | bytes 589832 | tf_op jit(solution)/shard_map/ppermute | solution.py:84
  55.1 26.6 %collective-permute-start.17 = (bf16[192,512]{1,0:T(8,128)(2,1)S(1)}, bf16[192,512]{1,0:T(8,128)(2,1)S(1)}, u32[]{:S(2)}, u32[]{:S(2)}) collective-permute-start(bf16[192,512]{1,0:T(8,128)(2,1)S(1)} %get-tuple-element.63), channel_id=1, source_target_pairs={{0,3},{1,2},{2,1},{3,0},{4,7},{5,6},{6,5},{7,4},{8,11},{9,10},{10,... | collective-permute-start | bytes 589832 | tf_op jit(solution)/shard_map/ppermute | solution.py:84
  61.9 19.9 %collective-permute-start.18 = (bf16[192,512]{1,0:T(8,128)(2,1)S(1)}, bf16[192,512]{1,0:T(8,128)(2,1)S(1)}, u32[]{:S(2)}, u32[]{:S(2)}) collective-permute-start(bf16[192,512]{1,0:T(8,128)(2,1)S(1)} %get-tuple-element.64), channel_id=1, source_target_pairs={{0,1},{1,0},{2,3},{3,2},{4,5},{5,4},{6,7},{7,6},{8,9},{9,8},{10,11... | collective-permute-start | bytes 589832 | tf_op jit(solution)/shard_map/ppermute | solution.py:84

commit v6 on v5

--- a/solution.py
+++ b/solution.py
@@ -86,7 +86,7 @@
     ]
 
 
-def plan_kernel(capacity, ctx_size, route_ref, target_ref, slot_ref, live_ref, natural):
+def plan_kernel(capacity, ctx_size, route_ref, _, target_ref, slot_ref, live_ref, natural):
     dp_size, length = route_ref.shape
     rows = length // ctx_size
     pack_len = dp_size * capacity
@@ -124,7 +124,7 @@
     live_ref[...] = jnp.broadcast_to(live, live_ref.shape)
 
 
-def plan(route, dp_size, ctx_size, capacity):
+def plan(route, dp_size, ctx_size, capacity, after):
     length = route.shape[0] // dp_size
     return pl.pallas_call(
         functools.partial(plan_kernel, capacity, ctx_size),
@@ -133,10 +133,11 @@
             jax.ShapeDtypeStruct((1, dp_size * capacity), jnp.int32),
             jax.ShapeDtypeStruct((1, HEAD_DIM), jnp.int32),
         ],
+        in_specs=[VMEM, ANY],
         scratch_shapes=[pltpu.VMEM((1, length), jnp.int32)],
         compiler_params=params(),
         cost_estimate=cost(2 * dp_size * length * length, 8 * length * dp_size),
-    )(route.reshape(dp_size, length))
+    )(route.reshape(dp_size, length), after)
 
 
 def rows_of(blocks):
@@ -158,16 +159,17 @@
         out[...] = packed[at * size : (at + 1) * size]
 
 
-def pack_own_kernel(number, target_ref, *refs):
-    got, refs = refs[:SWAPS], refs[SWAPS:]
-    blocks, outs = refs[:number], refs[number:]
+def pack_own_kernel(target_ref, *refs):
+    refs[-1][...] = place_rows(target_ref, rows_of(refs[:-1]), 0, refs[-1].shape[0])
+
+
+def merge_kernel(own_ref, *refs):
+    got, outs = refs[:SWAPS], refs[SWAPS:]
     size = got[0].shape[0]
-    half = size * SWAPS
     capacity = outs[0].shape[0] // 2
-    packed = place_rows(target_ref, rows_of(blocks), 0, half)
     for step, out in enumerate(outs):
         first = step * capacity
-        out[:capacity, :] = packed[first : first + capacity]
+        out[:capacity, :] = own_ref[first : first + capacity, :]
         begin = first % size
         out[capacity:, :] = got[first // size][begin : begin + capacity, :]
 
@@ -185,12 +187,18 @@
         cost_estimate=estimate,
     )(target, *blocks, *after)
     got = [lax.ppermute(part, "dp", [(j, j ^ 1) for j in range(dp_size)]) for part in other]
+    own = pl.pallas_call(
+        pack_own_kernel,
+        out_shape=jax.ShapeDtypeStruct((half, wide), jnp.bfloat16),
+        compiler_params=params(),
+        cost_estimate=estimate,
+    )(target, *blocks)
     outs = pl.pallas_call(
-        functools.partial(pack_own_kernel, len(blocks)),
+        merge_kernel,
         out_shape=[jax.ShapeDtypeStruct((2 * capacity, wide), jnp.bfloat16)] * (dp_size // 2),
         compiler_params=params(),
-        cost_estimate=estimate,
-    )(target, *got, *blocks)
+        cost_estimate=cost(0, 8 * half * wide),
+    )(own, *got)
     return swap(list(outs), "dp", dp_size, 2)
 
 
@@ -337,8 +345,8 @@
         blocks = cut(q_src, kv_src, chunk, ctx_size, at == 0, after)
         gathered.append(swap(blocks, "ctx", ctx_size))
         after = blocks[:1]
-    target, slot, live = plan(route, dp_size, ctx_size, capacity)
     doc_col = jnp.broadcast_to(doc_ids.reshape(pack_len, 1), (pack_len, HEAD_DIM))
+    target, slot, live = plan(route, dp_size, ctx_size, capacity, doc_col)
 
     packed = []
     for at, blocks in enumerate(gathered):

time: 82.8 us -> 82.6 us (level)
  starting transfers between devices: 30.8 us -> 26.3 us
  waiting for transfers between devices: 37.8 us -> 41.8 us
    ppermute x18, waiting for transfers between devices: 35.5 us -> 40.4 us  [swap(): lax.ppermute(blocks[step], axis, [(j, j ^ step * unit) for j in range(siz...]
    ppermute x18, starting transfers between devices: 29.6 us -> 25.1 us  [swap(): lax.ppermute(blocks[step], axis, [(j, j ^ step * unit) for j in range(siz...]
    ppermute x4, waiting for transfers between devices: 2.27 us -> 1.44 us  [deliver(): lax.ppermute(part, 'dp', [(j, j ^ 1) for j in range(dp_size)])]
  transfers between devices with their start and end apart: 22 -> 22, of which waited for: 13 -> 12; matrix products, arithmetic and copies ran while one was open for 2% -> 2% of each run, Pallas kernels for 12% -> 12%
where the time goes in v6:
time: 82.6 us; the launch traced here: 82.3 us
  waiting for transfers between devices  41.8 us (51%)
  starting transfers between devices  26.3 us (32%)
  Pallas kernels  12.7 us (15%)
    ppermute x18, waiting for transfers between devices, swap(): lax.ppermute(blocks[step], axis, [(j, j ^ step * unit) for j in range(siz...  40.4 us
    ppermute x18, starting transfers between devices, swap(): lax.ppermute(blocks[step], axis, [(j, j ^ step * unit) for j in range(siz...  25.1 us
    pallas_call x2, Pallas kernels, attend(): pl.pallas_call(functools.partial(attend_kernel, heads, doc_most, ctx_size...  6.41 us
    pallas_call x2, Pallas kernels, cut(): pl.pallas_call(functools.partial(cut_kernel, chunk, ctx_size, with_kv, le...  2.46 us
    pallas_call x2, Pallas kernels, join(): pl.pallas_call(functools.partial(join_kernel, chunk, ctx_size, steps), ou...  1.81 us
  transfers between devices with their start and end apart: 22, of which 12 were waited for; matrix products, arithmetic and copies ran while one was open for 2% of the time, Pallas kernels for 12%

profile of v6, /device:TPU:18, one launch (start us, length us, event | category | flops | bytes accessed | tf_op | source)
XLA Modules:
  0.0 82.3 jit_solution(7617501769633276852)
XLA Ops:
  0.0 1.3 %shard_map.47 = (bf16[128,768]{1,0:T(8,128)(2,1)S(1)}, bf16[128,768]{1,0:T(8,128)(2,1)S(1)}, bf16[128,768]{1,0:T(8,128)(2,1)S(1)}, bf16[128,768]{1,0:T(8,128)(2,1)S(1)}) custom-call(bf16[128,4096]{1,0:T(8,128)(2,1)} %q_ref.3, bf16[128,1024]{1,0:T(8,128)(2,1)} %refs_0_.1), custom_call_target="tpu_custom_call" | custom-call | bytes 1572864 | tf_op jit(solution)/shard_map/pallas_call | solution.py:70
  1.3 1.6 %collective-permute-start.3 = (bf16[128,768]{1,0:T(8,128)(2,1)S(1)}, bf16[128,768]{1,0:T(8,128)(2,1)S(1)}, u32[]{:S(2)}, u32[]{:S(2)}) collective-permute-start(bf16[128,768]{1,0:T(8,128)(2,1)S(1)} %get-tuple-element.45), channel_id=1, source_target_pairs={{0,1},{1,0},{2,3},{3,2},{4,5},{5,4},{6,7},{7,6},{8,9},{9,8},{10,11... | collective-permute-start | bytes 589832 | tf_op jit(solution)/shard_map/ppermute | solution.py:84
  3.3 1.6 %collective-permute-start.5 = (bf16[128,768]{1,0:T(8,128)(2,1)S(1)}, bf16[128,768]{1,0:T(8,128)(2,1)S(1)}, u32[]{:S(2)}, u32[]{:S(2)}) collective-permute-start(bf16[128,768]{1,0:T(8,128)(2,1)S(1)} %get-tuple-element.47), channel_id=1, source_target_pairs={{0,3},{1,2},{2,1},{3,0},{4,7},{5,6},{6,5},{7,4},{8,11},{9,10},{10,... | collective-permute-start | bytes 589832 | tf_op jit(solution)/shard_map/ppermute | solution.py:84
  4.9 1.1 %shard_map.48 = (bf16[128,512]{1,0:T(8,128)(2,1)S(1)}, bf16[128,512]{1,0:T(8,128)(2,1)S(1)}, bf16[128,512]{1,0:T(8,128)(2,1)S(1)}, bf16[128,512]{1,0:T(8,128)(2,1)S(1)}) custom-call(bf16[128,4096]{1,0:T(8,128)(2,1)} %q_ref.3, bf16[128,768]{1,0:T(8,128)(2,1)S(1)} %get-tuple-element.40.refs_0_), custom_call_target="tpu_custom_call" | custom-call | bytes 1048576 | tf_op jit(solution)/shard_map/pallas_call | solution.py:70
  6.0 2.5 %collective-permute-start = (bf16[128,512]{1,0:T(8,128)(2,1)S(1)}, bf16[128,512]{1,0:T(8,128)(2,1)S(1)}, u32[]{:S(2)}, u32[]{:S(2)}) collective-permute-start(bf16[128,512]{1,0:T(8,128)(2,1)S(1)} %get-tuple-element.42), channel_id=1, source_target_pairs={{0,1},{1,0},{2,3},{3,2},{4,5},{5,4},{6,7},{7,6},{8,9},{9,8},{10,11... | collective-permute-start | bytes 393224 | tf_op jit(solution)/shard_map/ppermute | solution.py:84
  8.6 0.5 broadcast.4
  9.1 0.7 reduce.4
  10.2 9.1 %collective-permute-done.refs_1_.refs_4_ = bf16[128,512]{1,0:T(8,128)(2,1)S(1)} collective-permute-done((bf16[128,512]{1,0:T(8,128)(2,1)S(1)}, bf16[128,512]{1,0:T(8,128)(2,1)S(1)}, u32[]{:S(2)}, u32[]{:S(2)}) %collective-permute-start) | collective-permute-done | bytes 131104 | tf_op jit(solution)/shard_map/ppermute | solution.py:84
  19.3 2.6 %collective-permute-done.5.refs_3_ = bf16[128,768]{1,0:T(8,128)(2,1)S(1)} collective-permute-done((bf16[128,768]{1,0:T(8,128)(2,1)S(1)}, bf16[128,768]{1,0:T(8,128)(2,1)S(1)}, u32[]{:S(2)}, u32[]{:S(2)}) %collective-permute-start.5) | collective-permute-done | bytes 196640 | tf_op jit(solution)/shard_map/ppermute | solution.py:84
  22.5 0.5 collective-permute-start.7
  24.6 0.6 collective-permute-start.13
  25.2 1.5 %collective-permute-start.14 = (bf16[192,768]{1,0:T(8,128)(2,1)S(1)}, bf16[192,768]{1,0:T(8,128)(2,1)S(1)}, u32[]{:S(2)}, u32[]{:S(2)}) collective-permute-start(bf16[192,768]{1,0:T(8,128)(2,1)S(1)} %get-tuple-element.58), channel_id=1, source_target_pairs={{0,16},{4,20},{8,24},{12,28},{16,0},{20,4},{24,8},{28,12},{1,17},{... | collective-permute-start | bytes 884744 | tf_op jit(solution)/shard_map/ppermute | solution.py:84
  26.7 1.4 %collective-permute-start.15 = (bf16[192,768]{1,0:T(8,128)(2,1)S(1)}, bf16[192,768]{1,0:T(8,128)(2,1)S(1)}, u32[]{:S(2)}, u32[]{:S(2)}) collective-permute-start(bf16[192,768]{1,0:T(8,128)(2,1)S(1)} %get-tuple-element.59), channel_id=1, source_target_pairs={{0,24},{4,28},{8,16},{12,20},{16,8},{20,12},{24,0},{28,4},{1,25},{... | collective-permute-start | bytes 884744 | tf_op jit(solution)/shard_map/ppermute | solution.py:84
  28.1 4.3 %collective-permute-done.1.refs_2_ = bf16[128,512]{1,0:T(8,128)(2,1)S(1)} collective-permute-done((bf16[128,512]{1,0:T(8,128)(2,1)S(1)}, bf16[128,512]{1,0:T(8,128)(2,1)S(1)}, u32[]{:S(2)}, u32[]{:S(2)}) %collective-permute-start.1) | collective-permute-done | bytes 131104 | tf_op jit(solution)/shard_map/ppermute | solution.py:84
  32.5 3.1 %collective-permute-done.2.refs_3_ = bf16[128,512]{1,0:T(8,128)(2,1)S(1)} collective-permute-done((bf16[128,512]{1,0:T(8,128)(2,1)S(1)}, bf16[128,512]{1,0:T(8,128)(2,1)S(1)}, u32[]{:S(2)}, u32[]{:S(2)}) %collective-permute-start.2) | collective-permute-done | bytes 131104 | tf_op jit(solution)/shard_map/ppermute | solution.py:84
  36.9 0.6 collective-permute-done.8.refs_0_
  37.8 0.6 collective-permute-start.10
  38.4 1.5 %collective-permute-start.11 = (bf16[192,512]{1,0:T(8,128)(2,1)S(1)}, bf16[192,512]{1,0:T(8,128)(2,1)S(1)}, u32[]{:S(2)}, u32[]{:S(2)}) collective-permute-start(bf16[192,512]{1,0:T(8,128)(2,1)S(1)} %get-tuple-element.55), channel_id=1, source_target_pairs={{0,16},{4,20},{8,24},{12,28},{16,0},{20,4},{24,8},{28,12},{1,17},{... | collective-permute-start | bytes 589832 | tf_op jit(solution)/shard_map/ppermute | solution.py:84
  39.9 1.4 %collective-permute-start.12 = (bf16[192,512]{1,0:T(8,128)(2,1)S(1)}, bf16[192,512]{1,0:T(8,128)(2,1)S(1)}, u32[]{:S(2)}, u32[]{:S(2)}) collective-permute-start(bf16[192,512]{1,0:T(8,128)(2,1)S(1)} %get-tuple-element.56), channel_id=1, source_target_pairs={{0,24},{4,28},{8,16},{12,20},{16,8},{20,12},{24,0},{28,4},{1,25},{... | collective-permute-start | bytes 589832 | tf_op jit(solution)/shard_map/ppermute | solution.py:84
  41.4 3.4 %shard_map.55 = (bf16[192,512]{1,0:T(8,128)(2,1)S(1)}, bf16[192,512]{1,0:T(8,128)(2,1)S(1)}, bf16[192,512]{1,0:T(8,128)(2,1)S(1)}, bf16[192,512]{1,0:T(8,128)(2,1)S(1)}, bf16[768,256]{1,0:T(8,128)(2,1)S(1)}) custom-call(s32[1,768]{1,0:T(1,128)S(1)} %get-tuple-element.37.refs_0_, s32[1,128]{1,0:T(1,128)S(1)} %get-tuple-element.38.refs_1_, ...), custom_call_target="tpu_custom_call" | custom-call | flops 1811939328 | bytes 3145728 | tf_op jit(solution)/shard_map/pallas_call | solution.py:277
  44.7 3.8 %collective-permute-start.19 = (bf16[192,512]{1,0:T(8,128)(2,1)S(1)}, bf16[192,512]{1,0:T(8,128)(2,1)S(1)}, u32[]{:S(2)}, u32[]{:S(2)}) collective-permute-start(bf16[192,512]{1,0:T(8,128)(2,1)S(1)} %get-tuple-element.66), channel_id=1, source_target_pairs={{0,2},{1,3},{2,0},{3,1},{4,6},{5,7},{6,4},{7,5},{8,10},{9,11},{10,... | collective-permute-start | bytes 589832 | tf_op jit(solution)/shard_map/ppermute | solution.py:84
  48.6 1.7 %collective-permute-start.20 = (bf16[192,512]{1,0:T(8,128)(2,1)S(1)}, bf16[192,512]{1,0:T(8,128)(2,1)S(1)}, u32[]{:S(2)}, u32[]{:S(2)}) collective-permute-start(bf16[192,512]{1,0:T(8,128)(2,1)S(1)} %get-tuple-element.67), channel_id=1, source_target_pairs={{0,3},{1,2},{2,1},{3,0},{4,7},{5,6},{6,5},{7,4},{8,11},{9,10},{10,... | collective-permute-start | bytes 589832 | tf_op jit(solution)/shard_map/ppermute | solution.py:84
  50.2 3.1 %shard_map.56 = (bf16[192,512]{1,0:T(8,128)(2,1)S(1)}, bf16[192,512]{1,0:T(8,128)(2,1)S(1)}, bf16[192,512]{1,0:T(8,128)(2,1)S(1)}, bf16[192,512]{1,0:T(8,128)(2,1)S(1)}) custom-call(s32[1,768]{1,0:T(1,128)S(1)} %get-tuple-element.37.refs_0_, s32[1,128]{1,0:T(1,128)S(1)} %get-tuple-element.38.refs_1_, s32[1,768]{1,0:T(1,128)S(1)} %copy-done, ...), custom_call_target="tpu_custom_call" | custom-call | flops 1509949440 | bytes 3145728 | tf_op jit(solution)/shard_map/pallas_call | solution.py:277
  53.3 1.9 %collective-permute-start.16 = (bf16[192,512]{1,0:T(8,128)(2,1)S(1)}, bf16[192,512]{1,0:T(8,128)(2,1)S(1)}, u32[]{:S(2)}, u32[]{:S(2)}) collective-permute-start(bf16[192,512]{1,0:T(8,128)(2,1)S(1)} %get-tuple-element.62), channel_id=1, source_target_pairs={{0,2},{1,3},{2,0},{3,1},{4,6},{5,7},{6,4},{7,5},{8,10},{9,11},{10,... | collective-permute-start | bytes 589832 | tf_op jit(solution)/shard_map/ppermute | solution.py:84
  55.2 1.7 %collective-permute-start.17 = (bf16[192,512]{1,0:T(8,128)(2,1)S(1)}, bf16[192,512]{1,0:T(8,128)(2,1)S(1)}, u32[]{:S(2)}, u32[]{:S(2)}) collective-permute-start(bf16[192,512]{1,0:T(8,128)(2,1)S(1)} %get-tuple-element.63), channel_id=1, source_target_pairs={{0,3},{1,2},{2,1},{3,0},{4,7},{5,6},{6,5},{7,4},{8,11},{9,10},{10,... | collective-permute-start | bytes 589832 | tf_op jit(solution)/shard_map/ppermute | solution.py:84
  56.9 4.9 %collective-permute-done.19.refs_0_ = bf16[192,512]{1,0:T(8,128)(2,1)S(1)} collective-permute-done((bf16[192,512]{1,0:T(8,128)(2,1)S(1)}, bf16[192,512]{1,0:T(8,128)(2,1)S(1)}, u32[]{:S(2)}, u32[]{:S(2)}) %collective-permute-start.19) | collective-permute-done | bytes 196640 | tf_op jit(solution)/shard_map/ppermute | solution.py:84
  61.7 2.5 %collective-permute-start.18 = (bf16[192,512]{1,0:T(8,128)(2,1)S(1)}, bf16[192,512]{1,0:T(8,128)(2,1)S(1)}, u32[]{:S(2)}, u32[]{:S(2)}) collective-permute-start(bf16[192,512]{1,0:T(8,128)(2,1)S(1)} %get-tuple-element.64), channel_id=1, source_target_pairs={{0,1},{1,0},{2,3},{3,2},{4,5},{5,4},{6,7},{7,6},{8,9},{9,8},{10,11... | collective-permute-start | bytes 589832 | tf_op jit(solution)/shard_map/ppermute | solution.py:84
  64.2 8.9 %collective-permute-done.20.refs_1_ = bf16[192,512]{1,0:T(8,128)(2,1)S(1)} collective-permute-done((bf16[192,512]{1,0:T(8,128)(2,1)S(1)}, bf16[192,512]{1,0:T(8,128)(2,1)S(1)}, u32[]{:S(2)}, u32[]{:S(2)}) %collective-permute-start.20) | collective-permute-done | bytes 196640 | tf_op jit(solution)/shard_map/ppermute | solution.py:84
  73.1 0.9 %shard_map.57.refs_4_ = bf16[192,4096]{1,0:T(8,128)(2,1)} custom-call(bf16[192,512]{1,0:T(8,128)(2,1)S(1)} %collective-permute-done.19.refs_0_, bf16[192,512]{1,0:T(8,128)(2,1)S(1)} %collective-permute-done.20.refs_1_, bf16[192,512]{1,0:T(8,128)(2,1)S(1)} %collective-permute-done.21.refs_2_, bf16[192,512]{1,0:T(8,128)(2,1)S(1)} %get-tuple-element.60.refs_8_.refs_3_), custom_call_target="tpu_custom_call" | custom-call | bytes 1572864 | tf_op jit(solution)/shard_map/pallas_call | solution.py:323
  74.0 2.5 %collective-permute-done.16.refs_0_ = bf16[192,512]{1,0:T(8,128)(2,1)S(1)} collective-permute-done((bf16[192,512]{1,0:T(8,128)(2,1)S(1)}, bf16[192,512]{1,0:T(8,128)(2,1)S(1)}, u32[]{:S(2)}, u32[]{:S(2)}) %collective-permute-start.16) | collective-permute-done | bytes 196640 | tf_op jit(solution)/shard_map/ppermute | solution.py:84
  76.5 4.9 %collective-permute-done.17.refs_1_ = bf16[192,512]{1,0:T(8,128)(2,1)S(1)} collective-permute-done((bf16[192,512]{1,0:T(8,128)(2,1)S(1)}, bf16[192,512]{1,0:T(8,128)(2,1)S(1)}, u32[]{:S(2)}, u32[]{:S(2)}) %collective-permute-start.17) | collective-permute-done | bytes 196640 | tf_op jit(solution)/shard_map/ppermute | solution.py:84
  81.4 0.9 %shard_map.58 = bf16[192,4096]{1,0:T(8,128)(2,1)} custom-call(bf16[192,512]{1,0:T(8,128)(2,1)S(1)} %collective-permute-done.16.refs_0_, bf16[192,512]{1,0:T(8,128)(2,1)S(1)} %collective-permute-done.17.refs_1_, bf16[192,512]{1,0:T(8,128)(2,1)S(1)} %collective-permute-done.18.refs_2_, ...), custom_call_target="tpu_custom_call", output_to_operand_aliasing={{}: (4, {})} | custom-call | bytes 1572864 | tf_op jit(solution)/shard_map/pallas_call | solution.py:323
  (34 shorter events, 4.5 us)
Async XLA Ops:
  0.0 8.6 %copy-start = (s32[1,768]{1,0:T(1,128)S(1)}, s32[1,768]{1,0:T(1,128)}, u32[]{:S(2)}) copy-start(s32[1,768]{1,0:T(1,128)} %refs_2_.3) | copy-start | bytes 9220
  0.0 9.1 %copy-start.1 = (s32[4096,1]{0,1:T(1,128)S(1)}, s32[4096,1]{0,1:T(1,128)}, u32[]{:S(2)}) copy-start(s32[4096,1]{0,1:T(1,128)} %param.6) | copy-start | bytes 49156
  1.3 18.0 %collective-permute-start.3 = (bf16[128,768]{1,0:T(8,128)(2,1)S(1)}, bf16[128,768]{1,0:T(8,128)(2,1)S(1)}, u32[]{:S(2)}, u32[]{:S(2)}) collective-permute-start(bf16[128,768]{1,0:T(8,128)(2,1)S(1)} %get-tuple-element.45), channel_id=1, source_target_pairs={{0,1},{1,0},{2,3},{3,2},{4,5},{5,4},{6,7},{7,6},{8,9},{9,8},{10,11... | collective-permute-start | bytes 589832 | tf_op jit(solution)/shard_map/ppermute | solution.py:84
  3.0 16.4 %collective-permute-start.4 = (bf16[128,768]{1,0:T(8,128)(2,1)S(1)}, bf16[128,768]{1,0:T(8,128)(2,1)S(1)}, u32[]{:S(2)}, u32[]{:S(2)}) collective-permute-start(bf16[128,768]{1,0:T(8,128)(2,1)S(1)} %get-tuple-element.46), channel_id=1, source_target_pairs={{0,2},{1,3},{2,0},{3,1},{4,6},{5,7},{6,4},{7,5},{8,10},{9,11},{10,... | collective-permute-start | bytes 589832 | tf_op jit(solution)/shard_map/ppermute | solution.py:84
  3.3 18.6 %collective-permute-start.5 = (bf16[128,768]{1,0:T(8,128)(2,1)S(1)}, bf16[128,768]{1,0:T(8,128)(2,1)S(1)}, u32[]{:S(2)}, u32[]{:S(2)}) collective-permute-start(bf16[128,768]{1,0:T(8,128)(2,1)S(1)} %get-tuple-element.47), channel_id=1, source_target_pairs={{0,3},{1,2},{2,1},{3,0},{4,7},{5,6},{6,5},{7,4},{8,11},{9,10},{10,... | collective-permute-start | bytes 589832 | tf_op jit(solution)/shard_map/ppermute | solution.py:84
  6.0 13.3 %collective-permute-start = (bf16[128,512]{1,0:T(8,128)(2,1)S(1)}, bf16[128,512]{1,0:T(8,128)(2,1)S(1)}, u32[]{:S(2)}, u32[]{:S(2)}) collective-permute-start(bf16[128,512]{1,0:T(8,128)(2,1)S(1)} %get-tuple-element.42), channel_id=1, source_target_pairs={{0,1},{1,0},{2,3},{3,2},{4,5},{5,4},{6,7},{7,6},{8,9},{9,8},{10,11... | collective-permute-start | bytes 393224 | tf_op jit(solution)/shard_map/ppermute | solution.py:84
  22.4 1.6 %collective-permute-start.6 = (bf16[192,768]{1,0:T(8,128)(2,1)S(1)}, bf16[192,768]{1,0:T(8,128)(2,1)S(1)}, u32[]{:S(2)}, u32[]{:S(2)}) collective-permute-start(bf16[192,768]{1,0:T(8,128)(2,1)S(1)} %get-tuple-element.48), channel_id=1, source_target_pairs={{0,4},{4,0},{8,12},{12,8},{16,20},{20,16},{24,28},{28,24},{1,5},{5... | collective-permute-start | bytes 884744 | tf_op jit(solution)/shard_map/ppermute | solution.py:189
  22.5 2.0 %collective-permute-start.7 = (bf16[192,768]{1,0:T(8,128)(2,1)S(1)}, bf16[192,768]{1,0:T(8,128)(2,1)S(1)}, u32[]{:S(2)}, u32[]{:S(2)}) collective-permute-start(bf16[192,768]{1,0:T(8,128)(2,1)S(1)} %get-tuple-element.49), channel_id=1, source_target_pairs={{0,4},{4,0},{8,12},{12,8},{16,20},{20,16},{24,28},{28,24},{1,5},{5... | collective-permute-start | bytes 884744 | tf_op jit(solution)/shard_map/ppermute | solution.py:189
  23.0 9.5 %collective-permute-start.1 = (bf16[128,512]{1,0:T(8,128)(2,1)S(1)}, bf16[128,512]{1,0:T(8,128)(2,1)S(1)}, u32[]{:S(2)}, u32[]{:S(2)}) collective-permute-start(bf16[128,512]{1,0:T(8,128)(2,1)S(1)} %get-tuple-element.43), channel_id=1, source_target_pairs={{0,2},{1,3},{2,0},{3,1},{4,6},{5,7},{6,4},{7,5},{8,10},{9,11},{10,... | collective-permute-start | bytes 393224 | tf_op jit(solution)/shard_map/ppermute | solution.py:84
  23.0 12.6 %collective-permute-start.2 = (bf16[128,512]{1,0:T(8,128)(2,1)S(1)}, bf16[128,512]{1,0:T(8,128)(2,1)S(1)}, u32[]{:S(2)}, u32[]{:S(2)}) collective-permute-start(bf16[128,512]{1,0:T(8,128)(2,1)S(1)} %get-tuple-element.44), channel_id=1, source_target_pairs={{0,3},{1,2},{2,1},{3,0},{4,7},{5,6},{6,5},{7,4},{8,11},{9,10},{10,... | collective-permute-start | bytes 393224 | tf_op jit(solution)/shard_map/ppermute | solution.py:84
  24.6 15.3 %collective-permute-start.13 = (bf16[192,768]{1,0:T(8,128)(2,1)S(1)}, bf16[192,768]{1,0:T(8,128)(2,1)S(1)}, u32[]{:S(2)}, u32[]{:S(2)}) collective-permute-start(bf16[192,768]{1,0:T(8,128)(2,1)S(1)} %get-tuple-element.57), channel_id=1, source_target_pairs={{0,8},{4,12},{8,0},{12,4},{16,24},{20,28},{24,16},{28,20},{1,9},{5... | collective-permute-start | bytes 884744 | tf_op jit(solution)/shard_map/ppermute | solution.py:84
  25.2 16.2 %collective-permute-start.14 = (bf16[192,768]{1,0:T(8,128)(2,1)S(1)}, bf16[192,768]{1,0:T(8,128)(2,1)S(1)}, u32[]{:S(2)}, u32[]{:S(2)}) collective-permute-start(bf16[192,768]{1,0:T(8,128)(2,1)S(1)} %get-tuple-element.58), channel_id=1, source_target_pairs={{0,16},{4,20},{8,24},{12,28},{16,0},{20,4},{24,8},{28,12},{1,17},{... | collective-permute-start | bytes 884744 | tf_op jit(solution)/shard_map/ppermute | solution.py:84
  26.7 14.7 %collective-permute-start.15 = (bf16[192,768]{1,0:T(8,128)(2,1)S(1)}, bf16[192,768]{1,0:T(8,128)(2,1)S(1)}, u32[]{:S(2)}, u32[]{:S(2)}) collective-permute-start(bf16[192,768]{1,0:T(8,128)(2,1)S(1)} %get-tuple-element.59), channel_id=1, source_target_pairs={{0,24},{4,28},{8,16},{12,20},{16,8},{20,12},{24,0},{28,4},{1,25},{... | collective-permute-start | bytes 884744 | tf_op jit(solution)/shard_map/ppermute | solution.py:84
  36.0 1.5 %collective-permute-start.8 = (bf16[192,512]{1,0:T(8,128)(2,1)S(1)}, bf16[192,512]{1,0:T(8,128)(2,1)S(1)}, u32[]{:S(2)}, u32[]{:S(2)}) collective-permute-start(bf16[192,512]{1,0:T(8,128)(2,1)S(1)} %get-tuple-element.51), channel_id=1, source_target_pairs={{0,4},{4,0},{8,12},{12,8},{16,20},{20,16},{24,28},{28,24},{1,5},{5... | collective-permute-start | bytes 589832 | tf_op jit(solution)/shard_map/ppermute | solution.py:189
  36.0 1.7 %collective-permute-start.9 = (bf16[192,512]{1,0:T(8,128)(2,1)S(1)}, bf16[192,512]{1,0:T(8,128)(2,1)S(1)}, u32[]{:S(2)}, u32[]{:S(2)}) collective-permute-start(bf16[192,512]{1,0:T(8,128)(2,1)S(1)} %get-tuple-element.52), channel_id=1, source_target_pairs={{0,4},{4,0},{8,12},{12,8},{16,20},{20,16},{24,28},{28,24},{1,5},{5... | collective-permute-start | bytes 589832 | tf_op jit(solution)/shard_map/ppermute | solution.py:189
  37.8 12.4 %collective-permute-start.10 = (bf16[192,512]{1,0:T(8,128)(2,1)S(1)}, bf16[192,512]{1,0:T(8,128)(2,1)S(1)}, u32[]{:S(2)}, u32[]{:S(2)}) collective-permute-start(bf16[192,512]{1,0:T(8,128)(2,1)S(1)} %get-tuple-element.54), channel_id=1, source_target_pairs={{0,8},{4,12},{8,0},{12,4},{16,24},{20,28},{24,16},{28,20},{1,9},{5... | collective-permute-start | bytes 589832 | tf_op jit(solution)/shard_map/ppermute | solution.py:84
  38.4 11.8 %collective-permute-start.11 = (bf16[192,512]{1,0:T(8,128)(2,1)S(1)}, bf16[192,512]{1,0:T(8,128)(2,1)S(1)}, u32[]{:S(2)}, u32[]{:S(2)}) collective-permute-start(bf16[192,512]{1,0:T(8,128)(2,1)S(1)} %get-tuple-element.55), channel_id=1, source_target_pairs={{0,16},{4,20},{8,24},{12,28},{16,0},{20,4},{24,8},{28,12},{1,17},{... | collective-permute-start | bytes 589832 | tf_op jit(solution)/shard_map/ppermute | solution.py:84
  39.9 10.3 %collective-permute-start.12 = (bf16[192,512]{1,0:T(8,128)(2,1)S(1)}, bf16[192,512]{1,0:T(8,128)(2,1)S(1)}, u32[]{:S(2)}, u32[]{:S(2)}) collective-permute-start(bf16[192,512]{1,0:T(8,128)(2,1)S(1)} %get-tuple-element.56), channel_id=1, source_target_pairs={{0,24},{4,28},{8,16},{12,20},{16,8},{20,12},{24,0},{28,4},{1,25},{... | collective-permute-start | bytes 589832 | tf_op jit(solution)/shard_map/ppermute | solution.py:84
  44.7 17.0 %collective-permute-start.19 = (bf16[192,512]{1,0:T(8,128)(2,1)S(1)}, bf16[192,512]{1,0:T(8,128)(2,1)S(1)}, u32[]{:S(2)}, u32[]{:S(2)}) collective-permute-start(bf16[192,512]{1,0:T(8,128)(2,1)S(1)} %get-tuple-element.66), channel_id=1, source_target_pairs={{0,2},{1,3},{2,0},{3,1},{4,6},{5,7},{6,4},{7,5},{8,10},{9,11},{10,... | collective-permute-start | bytes 589832 | tf_op jit(solution)/shard_map/ppermute | solution.py:84
  48.6 24.5 %collective-permute-start.20 = (bf16[192,512]{1,0:T(8,128)(2,1)S(1)}, bf16[192,512]{1,0:T(8,128)(2,1)S(1)}, u32[]{:S(2)}, u32[]{:S(2)}) collective-permute-start(bf16[192,512]{1,0:T(8,128)(2,1)S(1)} %get-tuple-element.67), channel_id=1, source_target_pairs={{0,3},{1,2},{2,1},{3,0},{4,7},{5,6},{6,5},{7,4},{8,11},{9,10},{10,... | collective-permute-start | bytes 589832 | tf_op jit(solution)/shard_map/ppermute | solution.py:84
  50.2 22.9 %collective-permute-start.21 = (bf16[192,512]{1,0:T(8,128)(2,1)S(1)}, bf16[192,512]{1,0:T(8,128)(2,1)S(1)}, u32[]{:S(2)}, u32[]{:S(2)}) collective-permute-start(bf16[192,512]{1,0:T(8,128)(2,1)S(1)} %get-tuple-element.68), channel_id=1, source_target_pairs={{0,1},{1,0},{2,3},{3,2},{4,5},{5,4},{6,7},{7,6},{8,9},{9,8},{10,11... | collective-permute-start | bytes 589832 | tf_op jit(solution)/shard_map/ppermute | solution.py:84
  53.3 23.2 %collective-permute-start.16 = (bf16[192,512]{1,0:T(8,128)(2,1)S(1)}, bf16[192,512]{1,0:T(8,128)(2,1)S(1)}, u32[]{:S(2)}, u32[]{:S(2)}) collective-permute-start(bf16[192,512]{1,0:T(8,128)(2,1)S(1)} %get-tuple-element.62), channel_id=1, source_target_pairs={{0,2},{1,3},{2,0},{3,1},{4,6},{5,7},{6,4},{7,5},{8,10},{9,11},{10,... | collective-permute-start | bytes 589832 | tf_op jit(solution)/shard_map/ppermute | solution.py:84
  55.2 26.2 %collective-permute-start.17 = (bf16[192,512]{1,0:T(8,128)(2,1)S(1)}, bf16[192,512]{1,0:T(8,128)(2,1)S(1)}, u32[]{:S(2)}, u32[]{:S(2)}) collective-permute-start(bf16[192,512]{1,0:T(8,128)(2,1)S(1)} %get-tuple-element.63), channel_id=1, source_target_pairs={{0,3},{1,2},{2,1},{3,0},{4,7},{5,6},{6,5},{7,4},{8,11},{9,10},{10,... | collective-permute-start | bytes 589832 | tf_op jit(solution)/shard_map/ppermute | solution.py:84
  61.7 19.7 %collective-permute-start.18 = (bf16[192,512]{1,0:T(8,128)(2,1)S(1)}, bf16[192,512]{1,0:T(8,128)(2,1)S(1)}, u32[]{:S(2)}, u32[]{:S(2)}) collective-permute-start(bf16[192,512]{1,0:T(8,128)(2,1)S(1)} %get-tuple-element.64), channel_id=1, source_target_pairs={{0,1},{1,0},{2,3},{3,2},{4,5},{5,4},{6,7},{7,6},{8,9},{9,8},{10,11... | collective-permute-start | bytes 589832 | tf_op jit(solution)/shard_map/ppermute | solution.py:84

commit v7 on v6

--- a/solution.py
+++ b/solution.py
@@ -355,7 +355,7 @@
 
     kv, sends = None, []
     for at, chunk in enumerate(chunks):
-        after = [sends[-1][0]] if sends else [p[0] for p in packed[1:2]]
+        after = [] if sends else []
         blocks, kv = attend(
             packed[at], slot, live, doc_ids, doc_col, kv, chunk[1], ctx_size, after
         )

time: 82.6 us -> 82.6 us (level)
  no operation moved by 1% of the time
where the time goes in v7:
time: 82.6 us; the launch traced here: 82.3 us
  waiting for transfers between devices  41.8 us (51%)
  starting transfers between devices  26.3 us (32%)
  Pallas kernels  12.7 us (15%)
    ppermute x18, waiting for transfers between devices, swap(): lax.ppermute(blocks[step], axis, [(j, j ^ step * unit) for j in range(siz...  40.4 us
    ppermute x18, starting transfers between devices, swap(): lax.ppermute(blocks[step], axis, [(j, j ^ step * unit) for j in range(siz...  25.1 us
    pallas_call x2, Pallas kernels, attend(): pl.pallas_call(functools.partial(attend_kernel, heads, doc_most, ctx_size...  6.39 us
    pallas_call x2, Pallas kernels, cut(): pl.pallas_call(functools.partial(cut_kernel, chunk, ctx_size, with_kv, le...  2.46 us
    pallas_call x2, Pallas kernels, join(): pl.pallas_call(functools.partial(join_kernel, chunk, ctx_size, steps), ou...  1.81 us
  transfers between devices with their start and end apart: 22, of which 12 were waited for; matrix products, arithmetic and copies ran while one was open for 2% of the time, Pallas kernels for 12%

profile of v7, /device:TPU:18, one launch (start us, length us, event | category | flops | bytes accessed | tf_op | source)
XLA Modules:
  0.0 82.3 jit_solution(12257596006048922495)
XLA Ops:
  0.0 1.3 %shard_map.47 = (bf16[128,768]{1,0:T(8,128)(2,1)S(1)}, bf16[128,768]{1,0:T(8,128)(2,1)S(1)}, bf16[128,768]{1,0:T(8,128)(2,1)S(1)}, bf16[128,768]{1,0:T(8,128)(2,1)S(1)}) custom-call(bf16[128,4096]{1,0:T(8,128)(2,1)} %q_ref.3, bf16[128,1024]{1,0:T(8,128)(2,1)} %refs_0_.1), custom_call_target="tpu_custom_call" | custom-call | bytes 1572864 | tf_op jit(solution)/shard_map/pallas_call | solution.py:70
  1.3 1.6 %collective-permute-start.3 = (bf16[128,768]{1,0:T(8,128)(2,1)S(1)}, bf16[128,768]{1,0:T(8,128)(2,1)S(1)}, u32[]{:S(2)}, u32[]{:S(2)}) collective-permute-start(bf16[128,768]{1,0:T(8,128)(2,1)S(1)} %get-tuple-element.45), channel_id=1, source_target_pairs={{0,1},{1,0},{2,3},{3,2},{4,5},{5,4},{6,7},{7,6},{8,9},{9,8},{10,11... | collective-permute-start | bytes 589832 | tf_op jit(solution)/shard_map/ppermute | solution.py:84
  3.3 1.6 %collective-permute-start.5 = (bf16[128,768]{1,0:T(8,128)(2,1)S(1)}, bf16[128,768]{1,0:T(8,128)(2,1)S(1)}, u32[]{:S(2)}, u32[]{:S(2)}) collective-permute-start(bf16[128,768]{1,0:T(8,128)(2,1)S(1)} %get-tuple-element.47), channel_id=1, source_target_pairs={{0,3},{1,2},{2,1},{3,0},{4,7},{5,6},{6,5},{7,4},{8,11},{9,10},{10,... | collective-permute-start | bytes 589832 | tf_op jit(solution)/shard_map/ppermute | solution.py:84
  4.9 1.1 %shard_map.48 = (bf16[128,512]{1,0:T(8,128)(2,1)S(1)}, bf16[128,512]{1,0:T(8,128)(2,1)S(1)}, bf16[128,512]{1,0:T(8,128)(2,1)S(1)}, bf16[128,512]{1,0:T(8,128)(2,1)S(1)}) custom-call(bf16[128,4096]{1,0:T(8,128)(2,1)} %q_ref.3, bf16[128,768]{1,0:T(8,128)(2,1)S(1)} %get-tuple-element.40.refs_0_), custom_call_target="tpu_custom_call" | custom-call | bytes 1048576 | tf_op jit(solution)/shard_map/pallas_call | solution.py:70
  6.0 2.5 %collective-permute-start = (bf16[128,512]{1,0:T(8,128)(2,1)S(1)}, bf16[128,512]{1,0:T(8,128)(2,1)S(1)}, u32[]{:S(2)}, u32[]{:S(2)}) collective-permute-start(bf16[128,512]{1,0:T(8,128)(2,1)S(1)} %get-tuple-element.42), channel_id=1, source_target_pairs={{0,1},{1,0},{2,3},{3,2},{4,5},{5,4},{6,7},{7,6},{8,9},{9,8},{10,11... | collective-permute-start | bytes 393224 | tf_op jit(solution)/shard_map/ppermute | solution.py:84
  8.6 0.5 broadcast.4
  9.1 0.7 reduce.4
  10.2 9.1 %collective-permute-done.refs_1_.refs_4_ = bf16[128,512]{1,0:T(8,128)(2,1)S(1)} collective-permute-done((bf16[128,512]{1,0:T(8,128)(2,1)S(1)}, bf16[128,512]{1,0:T(8,128)(2,1)S(1)}, u32[]{:S(2)}, u32[]{:S(2)}) %collective-permute-start) | collective-permute-done | bytes 131104 | tf_op jit(solution)/shard_map/ppermute | solution.py:84
  19.3 2.6 %collective-permute-done.5.refs_3_ = bf16[128,768]{1,0:T(8,128)(2,1)S(1)} collective-permute-done((bf16[128,768]{1,0:T(8,128)(2,1)S(1)}, bf16[128,768]{1,0:T(8,128)(2,1)S(1)}, u32[]{:S(2)}, u32[]{:S(2)}) %collective-permute-start.5) | collective-permute-done | bytes 196640 | tf_op jit(solution)/shard_map/ppermute | solution.py:84
  22.5 0.5 collective-permute-start.7
  24.6 0.6 collective-permute-start.13
  25.2 1.5 %collective-permute-start.14 = (bf16[192,768]{1,0:T(8,128)(2,1)S(1)}, bf16[192,768]{1,0:T(8,128)(2,1)S(1)}, u32[]{:S(2)}, u32[]{:S(2)}) collective-permute-start(bf16[192,768]{1,0:T(8,128)(2,1)S(1)} %get-tuple-element.58), channel_id=1, source_target_pairs={{0,16},{4,20},{8,24},{12,28},{16,0},{20,4},{24,8},{28,12},{1,17},{... | collective-permute-start | bytes 884744 | tf_op jit(solution)/shard_map/ppermute | solution.py:84
  26.7 1.4 %collective-permute-start.15 = (bf16[192,768]{1,0:T(8,128)(2,1)S(1)}, bf16[192,768]{1,0:T(8,128)(2,1)S(1)}, u32[]{:S(2)}, u32[]{:S(2)}) collective-permute-start(bf16[192,768]{1,0:T(8,128)(2,1)S(1)} %get-tuple-element.59), channel_id=1, source_target_pairs={{0,24},{4,28},{8,16},{12,20},{16,8},{20,12},{24,0},{28,4},{1,25},{... | collective-permute-start | bytes 884744 | tf_op jit(solution)/shard_map/ppermute | solution.py:84
  28.1 4.3 %collective-permute-done.1.refs_2_ = bf16[128,512]{1,0:T(8,128)(2,1)S(1)} collective-permute-done((bf16[128,512]{1,0:T(8,128)(2,1)S(1)}, bf16[128,512]{1,0:T(8,128)(2,1)S(1)}, u32[]{:S(2)}, u32[]{:S(2)}) %collective-permute-start.1) | collective-permute-done | bytes 131104 | tf_op jit(solution)/shard_map/ppermute | solution.py:84
  32.5 3.1 %collective-permute-done.2.refs_3_ = bf16[128,512]{1,0:T(8,128)(2,1)S(1)} collective-permute-done((bf16[128,512]{1,0:T(8,128)(2,1)S(1)}, bf16[128,512]{1,0:T(8,128)(2,1)S(1)}, u32[]{:S(2)}, u32[]{:S(2)}) %collective-permute-start.2) | collective-permute-done | bytes 131104 | tf_op jit(solution)/shard_map/ppermute | solution.py:84
  36.9 0.6 collective-permute-done.8.refs_0_
  37.8 0.6 collective-permute-start.10
  38.4 1.5 %collective-permute-start.11 = (bf16[192,512]{1,0:T(8,128)(2,1)S(1)}, bf16[192,512]{1,0:T(8,128)(2,1)S(1)}, u32[]{:S(2)}, u32[]{:S(2)}) collective-permute-start(bf16[192,512]{1,0:T(8,128)(2,1)S(1)} %get-tuple-element.55), channel_id=1, source_target_pairs={{0,16},{4,20},{8,24},{12,28},{16,0},{20,4},{24,8},{28,12},{1,17},{... | collective-permute-start | bytes 589832 | tf_op jit(solution)/shard_map/ppermute | solution.py:84
  39.9 1.4 %collective-permute-start.12 = (bf16[192,512]{1,0:T(8,128)(2,1)S(1)}, bf16[192,512]{1,0:T(8,128)(2,1)S(1)}, u32[]{:S(2)}, u32[]{:S(2)}) collective-permute-start(bf16[192,512]{1,0:T(8,128)(2,1)S(1)} %get-tuple-element.56), channel_id=1, source_target_pairs={{0,24},{4,28},{8,16},{12,20},{16,8},{20,12},{24,0},{28,4},{1,25},{... | collective-permute-start | bytes 589832 | tf_op jit(solution)/shard_map/ppermute | solution.py:84
  41.4 3.3 %shard_map.55 = (bf16[192,512]{1,0:T(8,128)(2,1)S(1)}, bf16[192,512]{1,0:T(8,128)(2,1)S(1)}, bf16[192,512]{1,0:T(8,128)(2,1)S(1)}, bf16[192,512]{1,0:T(8,128)(2,1)S(1)}, bf16[768,256]{1,0:T(8,128)(2,1)S(1)}) custom-call(s32[1,768]{1,0:T(1,128)S(1)} %get-tuple-element.37.refs_0_, s32[1,128]{1,0:T(1,128)S(1)} %get-tuple-element.38.refs_1_, ...), custom_call_target="tpu_custom_call" | custom-call | flops 1811939328 | bytes 3145728 | tf_op jit(solution)/shard_map/pallas_call | solution.py:277
  44.7 3.8 %collective-permute-start.19 = (bf16[192,512]{1,0:T(8,128)(2,1)S(1)}, bf16[192,512]{1,0:T(8,128)(2,1)S(1)}, u32[]{:S(2)}, u32[]{:S(2)}) collective-permute-start(bf16[192,512]{1,0:T(8,128)(2,1)S(1)} %get-tuple-element.65), channel_id=1, source_target_pairs={{0,2},{1,3},{2,0},{3,1},{4,6},{5,7},{6,4},{7,5},{8,10},{9,11},{10,... | collective-permute-start | bytes 589832 | tf_op jit(solution)/shard_map/ppermute | solution.py:84
  48.5 1.7 %collective-permute-start.20 = (bf16[192,512]{1,0:T(8,128)(2,1)S(1)}, bf16[192,512]{1,0:T(8,128)(2,1)S(1)}, u32[]{:S(2)}, u32[]{:S(2)}) collective-permute-start(bf16[192,512]{1,0:T(8,128)(2,1)S(1)} %get-tuple-element.66), channel_id=1, source_target_pairs={{0,3},{1,2},{2,1},{3,0},{4,7},{5,6},{6,5},{7,4},{8,11},{9,10},{10,... | collective-permute-start | bytes 589832 | tf_op jit(solution)/shard_map/ppermute | solution.py:84
  50.2 3.0 %shard_map.56 = (bf16[192,512]{1,0:T(8,128)(2,1)S(1)}, bf16[192,512]{1,0:T(8,128)(2,1)S(1)}, bf16[192,512]{1,0:T(8,128)(2,1)S(1)}, bf16[192,512]{1,0:T(8,128)(2,1)S(1)}) custom-call(s32[1,768]{1,0:T(1,128)S(1)} %get-tuple-element.37.refs_0_, s32[1,128]{1,0:T(1,128)S(1)} %get-tuple-element.38.refs_1_, s32[1,768]{1,0:T(1,128)S(1)} %copy-done, ...), custom_call_target="tpu_custom_call" | custom-call | flops 1509949440 | bytes 3145728 | tf_op jit(solution)/shard_map/pallas_call | solution.py:277
  53.3 1.9 %collective-permute-start.16 = (bf16[192,512]{1,0:T(8,128)(2,1)S(1)}, bf16[192,512]{1,0:T(8,128)(2,1)S(1)}, u32[]{:S(2)}, u32[]{:S(2)}) collective-permute-start(bf16[192,512]{1,0:T(8,128)(2,1)S(1)} %get-tuple-element.61), channel_id=1, source_target_pairs={{0,2},{1,3},{2,0},{3,1},{4,6},{5,7},{6,4},{7,5},{8,10},{9,11},{10,... | collective-permute-start | bytes 589832 | tf_op jit(solution)/shard_map/ppermute | solution.py:84
  55.2 1.7 %collective-permute-start.17 = (bf16[192,512]{1,0:T(8,128)(2,1)S(1)}, bf16[192,512]{1,0:T(8,128)(2,1)S(1)}, u32[]{:S(2)}, u32[]{:S(2)}) collective-permute-start(bf16[192,512]{1,0:T(8,128)(2,1)S(1)} %get-tuple-element.62), channel_id=1, source_target_pairs={{0,3},{1,2},{2,1},{3,0},{4,7},{5,6},{6,5},{7,4},{8,11},{9,10},{10,... | collective-permute-start | bytes 589832 | tf_op jit(solution)/shard_map/ppermute | solution.py:84
  56.8 4.9 %collective-permute-done.19.refs_0_ = bf16[192,512]{1,0:T(8,128)(2,1)S(1)} collective-permute-done((bf16[192,512]{1,0:T(8,128)(2,1)S(1)}, bf16[192,512]{1,0:T(8,128)(2,1)S(1)}, u32[]{:S(2)}, u32[]{:S(2)}) %collective-permute-start.19) | collective-permute-done | bytes 196640 | tf_op jit(solution)/shard_map/ppermute | solution.py:84
  61.7 2.5 %collective-permute-start.18 = (bf16[192,512]{1,0:T(8,128)(2,1)S(1)}, bf16[192,512]{1,0:T(8,128)(2,1)S(1)}, u32[]{:S(2)}, u32[]{:S(2)}) collective-permute-start(bf16[192,512]{1,0:T(8,128)(2,1)S(1)} %get-tuple-element.63), channel_id=1, source_target_pairs={{0,1},{1,0},{2,3},{3,2},{4,5},{5,4},{6,7},{7,6},{8,9},{9,8},{10,11... | collective-permute-start | bytes 589832 | tf_op jit(solution)/shard_map/ppermute | solution.py:84
  64.2 8.9 %collective-permute-done.20.refs_1_ = bf16[192,512]{1,0:T(8,128)(2,1)S(1)} collective-permute-done((bf16[192,512]{1,0:T(8,128)(2,1)S(1)}, bf16[192,512]{1,0:T(8,128)(2,1)S(1)}, u32[]{:S(2)}, u32[]{:S(2)}) %collective-permute-start.20) | collective-permute-done | bytes 196640 | tf_op jit(solution)/shard_map/ppermute | solution.py:84
  73.1 0.9 %shard_map.57.refs_4_ = bf16[192,4096]{1,0:T(8,128)(2,1)} custom-call(bf16[192,512]{1,0:T(8,128)(2,1)S(1)} %collective-permute-done.19.refs_0_, bf16[192,512]{1,0:T(8,128)(2,1)S(1)} %collective-permute-done.20.refs_1_, bf16[192,512]{1,0:T(8,128)(2,1)S(1)} %collective-permute-done.21.refs_2_, bf16[192,512]{1,0:T(8,128)(2,1)S(1)} %get-tuple-element.68.refs_3_), custom_call_target="tpu_custom_call" | custom-call | bytes 1572864 | tf_op jit(solution)/shard_map/pallas_call | solution.py:323
  74.0 2.5 %collective-permute-done.16.refs_0_ = bf16[192,512]{1,0:T(8,128)(2,1)S(1)} collective-permute-done((bf16[192,512]{1,0:T(8,128)(2,1)S(1)}, bf16[192,512]{1,0:T(8,128)(2,1)S(1)}, u32[]{:S(2)}, u32[]{:S(2)}) %collective-permute-start.16) | collective-permute-done | bytes 196640 | tf_op jit(solution)/shard_map/ppermute | solution.py:84
  76.5 4.9 %collective-permute-done.17.refs_1_ = bf16[192,512]{1,0:T(8,128)(2,1)S(1)} collective-permute-done((bf16[192,512]{1,0:T(8,128)(2,1)S(1)}, bf16[192,512]{1,0:T(8,128)(2,1)S(1)}, u32[]{:S(2)}, u32[]{:S(2)}) %collective-permute-start.17) | collective-permute-done | bytes 196640 | tf_op jit(solution)/shard_map/ppermute | solution.py:84
  81.4 0.9 %shard_map.58 = bf16[192,4096]{1,0:T(8,128)(2,1)} custom-call(bf16[192,512]{1,0:T(8,128)(2,1)S(1)} %collective-permute-done.16.refs_0_, bf16[192,512]{1,0:T(8,128)(2,1)S(1)} %collective-permute-done.17.refs_1_, bf16[192,512]{1,0:T(8,128)(2,1)S(1)} %collective-permute-done.18.refs_2_, ...), custom_call_target="tpu_custom_call", output_to_operand_aliasing={{}: (4, {})} | custom-call | bytes 1572864 | tf_op jit(solution)/shard_map/pallas_call | solution.py:323
  (34 shorter events, 4.5 us)
Async XLA Ops:
  0.0 8.6 %copy-start = (s32[1,768]{1,0:T(1,128)S(1)}, s32[1,768]{1,0:T(1,128)}, u32[]{:S(2)}) copy-start(s32[1,768]{1,0:T(1,128)} %refs_2_.3) | copy-start | bytes 9220
  0.0 9.1 %copy-start.1 = (s32[4096,1]{0,1:T(1,128)S(1)}, s32[4096,1]{0,1:T(1,128)}, u32[]{:S(2)}) copy-start(s32[4096,1]{0,1:T(1,128)} %param.6) | copy-start | bytes 49156
  1.3 18.0 %collective-permute-start.3 = (bf16[128,768]{1,0:T(8,128)(2,1)S(1)}, bf16[128,768]{1,0:T(8,128)(2,1)S(1)}, u32[]{:S(2)}, u32[]{:S(2)}) collective-permute-start(bf16[128,768]{1,0:T(8,128)(2,1)S(1)} %get-tuple-element.45), channel_id=1, source_target_pairs={{0,1},{1,0},{2,3},{3,2},{4,5},{5,4},{6,7},{7,6},{8,9},{9,8},{10,11... | collective-permute-start | bytes 589832 | tf_op jit(solution)/shard_map/ppermute | solution.py:84
  3.0 16.4 %collective-permute-start.4 = (bf16[128,768]{1,0:T(8,128)(2,1)S(1)}, bf16[128,768]{1,0:T(8,128)(2,1)S(1)}, u32[]{:S(2)}, u32[]{:S(2)}) collective-permute-start(bf16[128,768]{1,0:T(8,128)(2,1)S(1)} %get-tuple-element.46), channel_id=1, source_target_pairs={{0,2},{1,3},{2,0},{3,1},{4,6},{5,7},{6,4},{7,5},{8,10},{9,11},{10,... | collective-permute-start | bytes 589832 | tf_op jit(solution)/shard_map/ppermute | solution.py:84
  3.3 18.6 %collective-permute-start.5 = (bf16[128,768]{1,0:T(8,128)(2,1)S(1)}, bf16[128,768]{1,0:T(8,128)(2,1)S(1)}, u32[]{:S(2)}, u32[]{:S(2)}) collective-permute-start(bf16[128,768]{1,0:T(8,128)(2,1)S(1)} %get-tuple-element.47), channel_id=1, source_target_pairs={{0,3},{1,2},{2,1},{3,0},{4,7},{5,6},{6,5},{7,4},{8,11},{9,10},{10,... | collective-permute-start | bytes 589832 | tf_op jit(solution)/shard_map/ppermute | solution.py:84
  6.0 13.3 %collective-permute-start = (bf16[128,512]{1,0:T(8,128)(2,1)S(1)}, bf16[128,512]{1,0:T(8,128)(2,1)S(1)}, u32[]{:S(2)}, u32[]{:S(2)}) collective-permute-start(bf16[128,512]{1,0:T(8,128)(2,1)S(1)} %get-tuple-element.42), channel_id=1, source_target_pairs={{0,1},{1,0},{2,3},{3,2},{4,5},{5,4},{6,7},{7,6},{8,9},{9,8},{10,11... | collective-permute-start | bytes 393224 | tf_op jit(solution)/shard_map/ppermute | solution.py:84
  22.4 1.6 %collective-permute-start.6 = (bf16[192,768]{1,0:T(8,128)(2,1)S(1)}, bf16[192,768]{1,0:T(8,128)(2,1)S(1)}, u32[]{:S(2)}, u32[]{:S(2)}) collective-permute-start(bf16[192,768]{1,0:T(8,128)(2,1)S(1)} %get-tuple-element.48), channel_id=1, source_target_pairs={{0,4},{4,0},{8,12},{12,8},{16,20},{20,16},{24,28},{28,24},{1,5},{5... | collective-permute-start | bytes 884744 | tf_op jit(solution)/shard_map/ppermute | solution.py:189
  22.5 2.0 %collective-permute-start.7 = (bf16[192,768]{1,0:T(8,128)(2,1)S(1)}, bf16[192,768]{1,0:T(8,128)(2,1)S(1)}, u32[]{:S(2)}, u32[]{:S(2)}) collective-permute-start(bf16[192,768]{1,0:T(8,128)(2,1)S(1)} %get-tuple-element.49), channel_id=1, source_target_pairs={{0,4},{4,0},{8,12},{12,8},{16,20},{20,16},{24,28},{28,24},{1,5},{5... | collective-permute-start | bytes 884744 | tf_op jit(solution)/shard_map/ppermute | solution.py:189
  23.0 9.5 %collective-permute-start.1 = (bf16[128,512]{1,0:T(8,128)(2,1)S(1)}, bf16[128,512]{1,0:T(8,128)(2,1)S(1)}, u32[]{:S(2)}, u32[]{:S(2)}) collective-permute-start(bf16[128,512]{1,0:T(8,128)(2,1)S(1)} %get-tuple-element.43), channel_id=1, source_target_pairs={{0,2},{1,3},{2,0},{3,1},{4,6},{5,7},{6,4},{7,5},{8,10},{9,11},{10,... | collective-permute-start | bytes 393224 | tf_op jit(solution)/shard_map/ppermute | solution.py:84
  23.0 12.6 %collective-permute-start.2 = (bf16[128,512]{1,0:T(8,128)(2,1)S(1)}, bf16[128,512]{1,0:T(8,128)(2,1)S(1)}, u32[]{:S(2)}, u32[]{:S(2)}) collective-permute-start(bf16[128,512]{1,0:T(8,128)(2,1)S(1)} %get-tuple-element.44), channel_id=1, source_target_pairs={{0,3},{1,2},{2,1},{3,0},{4,7},{5,6},{6,5},{7,4},{8,11},{9,10},{10,... | collective-permute-start | bytes 393224 | tf_op jit(solution)/shard_map/ppermute | solution.py:84
  24.6 15.3 %collective-permute-start.13 = (bf16[192,768]{1,0:T(8,128)(2,1)S(1)}, bf16[192,768]{1,0:T(8,128)(2,1)S(1)}, u32[]{:S(2)}, u32[]{:S(2)}) collective-permute-start(bf16[192,768]{1,0:T(8,128)(2,1)S(1)} %get-tuple-element.57), channel_id=1, source_target_pairs={{0,8},{4,12},{8,0},{12,4},{16,24},{20,28},{24,16},{28,20},{1,9},{5... | collective-permute-start | bytes 884744 | tf_op jit(solution)/shard_map/ppermute | solution.py:84
  25.2 16.2 %collective-permute-start.14 = (bf16[192,768]{1,0:T(8,128)(2,1)S(1)}, bf16[192,768]{1,0:T(8,128)(2,1)S(1)}, u32[]{:S(2)}, u32[]{:S(2)}) collective-permute-start(bf16[192,768]{1,0:T(8,128)(2,1)S(1)} %get-tuple-element.58), channel_id=1, source_target_pairs={{0,16},{4,20},{8,24},{12,28},{16,0},{20,4},{24,8},{28,12},{1,17},{... | collective-permute-start | bytes 884744 | tf_op jit(solution)/shard_map/ppermute | solution.py:84
  26.7 14.7 %collective-permute-start.15 = (bf16[192,768]{1,0:T(8,128)(2,1)S(1)}, bf16[192,768]{1,0:T(8,128)(2,1)S(1)}, u32[]{:S(2)}, u32[]{:S(2)}) collective-permute-start(bf16[192,768]{1,0:T(8,128)(2,1)S(1)} %get-tuple-element.59), channel_id=1, source_target_pairs={{0,24},{4,28},{8,16},{12,20},{16,8},{20,12},{24,0},{28,4},{1,25},{... | collective-permute-start | bytes 884744 | tf_op jit(solution)/shard_map/ppermute | solution.py:84
  36.0 1.5 %collective-permute-start.8 = (bf16[192,512]{1,0:T(8,128)(2,1)S(1)}, bf16[192,512]{1,0:T(8,128)(2,1)S(1)}, u32[]{:S(2)}, u32[]{:S(2)}) collective-permute-start(bf16[192,512]{1,0:T(8,128)(2,1)S(1)} %get-tuple-element.51), channel_id=1, source_target_pairs={{0,4},{4,0},{8,12},{12,8},{16,20},{20,16},{24,28},{28,24},{1,5},{5... | collective-permute-start | bytes 589832 | tf_op jit(solution)/shard_map/ppermute | solution.py:189
  36.0 1.7 %collective-permute-start.9 = (bf16[192,512]{1,0:T(8,128)(2,1)S(1)}, bf16[192,512]{1,0:T(8,128)(2,1)S(1)}, u32[]{:S(2)}, u32[]{:S(2)}) collective-permute-start(bf16[192,512]{1,0:T(8,128)(2,1)S(1)} %get-tuple-element.52), channel_id=1, source_target_pairs={{0,4},{4,0},{8,12},{12,8},{16,20},{20,16},{24,28},{28,24},{1,5},{5... | collective-permute-start | bytes 589832 | tf_op jit(solution)/shard_map/ppermute | solution.py:189
  37.8 12.4 %collective-permute-start.10 = (bf16[192,512]{1,0:T(8,128)(2,1)S(1)}, bf16[192,512]{1,0:T(8,128)(2,1)S(1)}, u32[]{:S(2)}, u32[]{:S(2)}) collective-permute-start(bf16[192,512]{1,0:T(8,128)(2,1)S(1)} %get-tuple-element.54), channel_id=1, source_target_pairs={{0,8},{4,12},{8,0},{12,4},{16,24},{20,28},{24,16},{28,20},{1,9},{5... | collective-permute-start | bytes 589832 | tf_op jit(solution)/shard_map/ppermute | solution.py:84
  38.4 11.8 %collective-permute-start.11 = (bf16[192,512]{1,0:T(8,128)(2,1)S(1)}, bf16[192,512]{1,0:T(8,128)(2,1)S(1)}, u32[]{:S(2)}, u32[]{:S(2)}) collective-permute-start(bf16[192,512]{1,0:T(8,128)(2,1)S(1)} %get-tuple-element.55), channel_id=1, source_target_pairs={{0,16},{4,20},{8,24},{12,28},{16,0},{20,4},{24,8},{28,12},{1,17},{... | collective-permute-start | bytes 589832 | tf_op jit(solution)/shard_map/ppermute | solution.py:84
  39.9 10.3 %collective-permute-start.12 = (bf16[192,512]{1,0:T(8,128)(2,1)S(1)}, bf16[192,512]{1,0:T(8,128)(2,1)S(1)}, u32[]{:S(2)}, u32[]{:S(2)}) collective-permute-start(bf16[192,512]{1,0:T(8,128)(2,1)S(1)} %get-tuple-element.56), channel_id=1, source_target_pairs={{0,24},{4,28},{8,16},{12,20},{16,8},{20,12},{24,0},{28,4},{1,25},{... | collective-permute-start | bytes 589832 | tf_op jit(solution)/shard_map/ppermute | solution.py:84
  44.7 17.0 %collective-permute-start.19 = (bf16[192,512]{1,0:T(8,128)(2,1)S(1)}, bf16[192,512]{1,0:T(8,128)(2,1)S(1)}, u32[]{:S(2)}, u32[]{:S(2)}) collective-permute-start(bf16[192,512]{1,0:T(8,128)(2,1)S(1)} %get-tuple-element.65), channel_id=1, source_target_pairs={{0,2},{1,3},{2,0},{3,1},{4,6},{5,7},{6,4},{7,5},{8,10},{9,11},{10,... | collective-permute-start | bytes 589832 | tf_op jit(solution)/shard_map/ppermute | solution.py:84
  48.5 24.5 %collective-permute-start.20 = (bf16[192,512]{1,0:T(8,128)(2,1)S(1)}, bf16[192,512]{1,0:T(8,128)(2,1)S(1)}, u32[]{:S(2)}, u32[]{:S(2)}) collective-permute-start(bf16[192,512]{1,0:T(8,128)(2,1)S(1)} %get-tuple-element.66), channel_id=1, source_target_pairs={{0,3},{1,2},{2,1},{3,0},{4,7},{5,6},{6,5},{7,4},{8,11},{9,10},{10,... | collective-permute-start | bytes 589832 | tf_op jit(solution)/shard_map/ppermute | solution.py:84
  50.2 22.9 %collective-permute-start.21 = (bf16[192,512]{1,0:T(8,128)(2,1)S(1)}, bf16[192,512]{1,0:T(8,128)(2,1)S(1)}, u32[]{:S(2)}, u32[]{:S(2)}) collective-permute-start(bf16[192,512]{1,0:T(8,128)(2,1)S(1)} %get-tuple-element.67), channel_id=1, source_target_pairs={{0,1},{1,0},{2,3},{3,2},{4,5},{5,4},{6,7},{7,6},{8,9},{9,8},{10,11... | collective-permute-start | bytes 589832 | tf_op jit(solution)/shard_map/ppermute | solution.py:84
  53.3 23.2 %collective-permute-start.16 = (bf16[192,512]{1,0:T(8,128)(2,1)S(1)}, bf16[192,512]{1,0:T(8,128)(2,1)S(1)}, u32[]{:S(2)}, u32[]{:S(2)}) collective-permute-start(bf16[192,512]{1,0:T(8,128)(2,1)S(1)} %get-tuple-element.61), channel_id=1, source_target_pairs={{0,2},{1,3},{2,0},{3,1},{4,6},{5,7},{6,4},{7,5},{8,10},{9,11},{10,... | collective-permute-start | bytes 589832 | tf_op jit(solution)/shard_map/ppermute | solution.py:84
  55.2 26.2 %collective-permute-start.17 = (bf16[192,512]{1,0:T(8,128)(2,1)S(1)}, bf16[192,512]{1,0:T(8,128)(2,1)S(1)}, u32[]{:S(2)}, u32[]{:S(2)}) collective-permute-start(bf16[192,512]{1,0:T(8,128)(2,1)S(1)} %get-tuple-element.62), channel_id=1, source_target_pairs={{0,3},{1,2},{2,1},{3,0},{4,7},{5,6},{6,5},{7,4},{8,11},{9,10},{10,... | collective-permute-start | bytes 589832 | tf_op jit(solution)/shard_map/ppermute | solution.py:84
  61.7 19.7 %collective-permute-start.18 = (bf16[192,512]{1,0:T(8,128)(2,1)S(1)}, bf16[192,512]{1,0:T(8,128)(2,1)S(1)}, u32[]{:S(2)}, u32[]{:S(2)}) collective-permute-start(bf16[192,512]{1,0:T(8,128)(2,1)S(1)} %get-tuple-element.63), channel_id=1, source_target_pairs={{0,1},{1,0},{2,3},{3,2},{4,5},{5,4},{6,7},{7,6},{8,9},{9,8},{10,11... | collective-permute-start | bytes 589832 | tf_op jit(solution)/shard_map/ppermute | solution.py:84
